TPU v7x, 32 devices: a whole 2x2x4 slice. The times are simulated.
32 devices in a mesh: dp: 8 (over y, x, core), seq: 4 (over z).
Axes of the slice: x: 2, y: 2, z: 4, core: 2. Of those that a mesh axis runs over, the one named last changes fastest.
Arguments:
- image_tokens: bfloat16 [16, 1024, 1152], P('dp', 'seq'), may hold values from -6 to 6
- cotangent: bfloat16 [16, 1024, 1152], P('dp', 'seq'), may hold values from -6 to 6
- targets: bfloat16 [16, 1024, 768], P('dp', 'seq'), may hold values from -8 to 8
- bucket: int32 [16], P('dp'), may hold values from 0 to 999, as said below
- labels: int32 [16], P('dp'), may hold values from 0 to 999
- time_table: float32 [1000, 1152], replicated, may hold values from -6 to 6
- class_table: float32 [1000, 1152], replicated, may hold values from -6 to 6
- ada_weight: float32 [1152, 6912], P('dp'), may hold values from -0.1875 to 0.1875
- ada_bias: float32 [6912], P('dp'), may hold values from -4 to 4
- qkv_weight: float32 [1152, 3456], P('dp'), may hold values from -0.25 to 0.25
- qkv_bias: float32 [3456], P('dp'), may hold values from -4 to 4
- out_weight: float32 [1152, 1152], P('dp'), may hold values from -2 to 2
- out_bias: float32 [1152], P('dp'), may hold values from -4 to 4
- up_weight: float32 [1152, 4608], P('dp'), may hold values from -0.1875 to 0.1875
- up_bias: float32 [4608], P('dp'), may hold values from -4 to 4
- down_weight: float32 [4608, 1152], P('dp'), may hold values from -0.09375 to 0.09375
- down_bias: float32 [1152], P('dp'), may hold values from -4 to 4
- tap_first: float32 [1152, 2048], P('dp'), may hold values from -0.1875 to 0.1875
- tap_first_bias: float32 [2048], P('dp'), may hold values from -4 to 4
- tap_second: float32 [2048, 2048], P('dp'), may hold values from -0.125 to 0.125
- tap_second_bias: float32 [2048], P('dp'), may hold values from -4 to 4
- tap_third: float32 [2048, 768], P('dp'), may hold values from -0.125 to 0.125
- tap_third_bias: float32 [768], P('dp'), may hold values from -6 to 6
Outputs:
- block_output: bfloat16 [16, 1024, 1152], P('dp', 'seq')
- input_grad: float32 [16, 1024, 1152], P('dp', 'seq')
- align_loss: float32 [], replicated
- time_table_grad: float32 [1000, 1152], replicated
- class_table_grad: float32 [1000, 1152], replicated
- ada_weight_grad: float32 [1152, 6912], P('dp')
- ada_bias_grad: float32 [6912], P('dp')
- qkv_weight_grad: float32 [1152, 3456], P('dp')
- qkv_bias_grad: float32 [3456], P('dp')
- out_weight_grad: float32 [1152, 1152], P('dp')
- out_bias_grad: float32 [1152], P('dp')
- up_weight_grad: float32 [1152, 4608], P('dp')
- up_bias_grad: float32 [4608], P('dp')
- down_weight_grad: float32 [4608, 1152], P('dp')
- down_bias_grad: float32 [1152], P('dp')
- tap_first_grad: float32 [1152, 2048], P('dp')
- tap_first_bias_grad: float32 [2048], P('dp')
- tap_second_grad: float32 [2048, 2048], P('dp')
- tap_second_bias_grad: float32 [2048], P('dp')
- tap_third_grad: float32 [2048, 768], P('dp')
- tap_third_bias_grad: float32 [768], P('dp')
Inputs may be any that keep to these rules, and one draw needn't show every extreme that they name: `bucket`: bell-shaped over the buckets, most images near the middle one; one image at each end of the range.
All inputs are finite; a program needn't handle non-finite values.
Results may differ from a plain program's by a relative error of at most 0.024.
The roundings to bfloat16 on the way count: a program that leaves them out, or rounds other values in their place, can miss the bound.
Values may be sent and summed in bfloat16 or wider, within the bound.
No kernel may reach another device: no remote copies, remote signals or barrier semaphores. Data moves between devices by JAX's collectives and lax.ppermute only.
A program may use at most 448 MiB of HBM per device.

v0:
```python
import math

import jax
import jax.numpy as jnp
from jax import lax
from jax.sharding import PartitionSpec as P

HEADS = 16
HEAD_DIM = 72


EPS_NORM = 1e-06
HIGH = lax.Precision.HIGHEST


def layer_norm(values):
    centre = values - jnp.mean(values, axis=-1, keepdims=True)
    spread = jnp.mean(centre * centre, axis=-1, keepdims=True)
    return centre * lax.rsqrt(spread + EPS_NORM)


def modulate(values, scale, shift):
    return layer_norm(values) * (1.0 + scale) + shift


def gelu_tanh(values):
    return jax.nn.gelu(values, approximate=True)


def cosine(latent, target):
    inner = jnp.sum(latent * target, axis=-1)
    return (
        inner
        * lax.rsqrt(jnp.sum(latent * latent, axis=-1) + EPS_NORM)
        * lax.rsqrt(jnp.sum(target * target, axis=-1) + EPS_NORM)
    )


def linear(values, weight, bias):
    return jnp.einsum(
        "bqi,ij->bqj", values, weight, preferred_element_type=jnp.float32
    ) + bias.astype(jnp.float32)


def weight_grad(values, grad):
    return jnp.einsum("bqi,bqj->ij", values, grad, preferred_element_type=jnp.float32)


def bias_grad(grad):
    return jnp.sum(grad.astype(jnp.float32), axis=(0, 1))


def input_side(grad, weight):
    return jnp.einsum("bqj,ij->bqi", grad, weight, preferred_element_type=jnp.float32)


def shards(
    image_tokens,
    cotangent,
    targets,
    bucket,
    labels,
    time_table,
    class_table,
    ada_weight,
    ada_bias,
    qkv_weight,
    qkv_bias,
    out_weight,
    out_bias,
    up_weight,
    up_bias,
    down_weight,
    down_bias,
    tap_first,
    tap_first_bias,
    tap_second,
    tap_second_bias,
    tap_third,
    tap_third_bias,
):
    images = image_tokens.shape[0]
    rows = image_tokens.shape[1]
    width = image_tokens.shape[2]
    factor = 1.0 / math.sqrt(HEAD_DIM)
    half = jnp.bfloat16
    ada_full, ada_bias_full, qkv_full, qkv_bias_full, out_full, out_bias_full = (
        lax.all_gather(ada_weight.astype(half), "dp", axis=0, tiled=True),
        lax.all_gather(ada_bias.astype(half), "dp", axis=0, tiled=True),
        lax.all_gather(qkv_weight.astype(half), "dp", axis=0, tiled=True),
        lax.all_gather(qkv_bias.astype(half), "dp", axis=0, tiled=True),
        lax.all_gather(out_weight.astype(half), "dp", axis=0, tiled=True),
        lax.all_gather(out_bias.astype(half), "dp", axis=0, tiled=True),
    )
    (
        up_full,
        up_bias_full,
        down_full,
        down_bias_full,
        first_full,
        first_bias_full,
        second_full,
        second_bias_full,
        third_full,
        third_bias_full,
    ) = (
        lax.all_gather(up_weight.astype(half), "dp", axis=0, tiled=True),
        lax.all_gather(up_bias.astype(half), "dp", axis=0, tiled=True),
        lax.all_gather(down_weight.astype(half), "dp", axis=0, tiled=True),
        lax.all_gather(down_bias.astype(half), "dp", axis=0, tiled=True),
        lax.all_gather(tap_first.astype(half), "dp", axis=0, tiled=True),
        lax.all_gather(tap_first_bias.astype(half), "dp", axis=0, tiled=True),
        lax.all_gather(tap_second.astype(half), "dp", axis=0, tiled=True),
        lax.all_gather(tap_second_bias.astype(half), "dp", axis=0, tiled=True),
        lax.all_gather(tap_third.astype(half), "dp", axis=0, tiled=True),
        lax.all_gather(tap_third_bias.astype(half), "dp", axis=0, tiled=True),
    )
    time_hot = (
        bucket[:, None] == jnp.arange(time_table.shape[0], dtype=jnp.int32)[None, :]
    ).astype(jnp.float32)
    class_hot = (
        labels[:, None] == jnp.arange(class_table.shape[0], dtype=jnp.int32)[None, :]
    ).astype(jnp.float32)
    condition = jnp.dot(time_hot, time_table, precision=HIGH) + jnp.dot(
        class_hot, class_table, precision=HIGH
    )
    cond_act, cond_back = jax.vjp(jax.nn.silu, condition)
    cond_low = cond_act.astype(half)
    modulation = jnp.dot(
        cond_low, ada_full, preferred_element_type=jnp.float32
    ) + ada_bias_full.astype(jnp.float32)
    shift_one, scale_one, gate_one, shift_two, scale_two, gate_two = jnp.split(
        modulation[:, None, :], 6, axis=-1
    )
    tokens32 = image_tokens.astype(jnp.float32)
    norm_one, norm_one_back = jax.vjp(modulate, tokens32, scale_one, shift_one)
    hidden_one = norm_one.astype(half)
    qkv_rows = linear(hidden_one, qkv_full, qkv_bias_full).astype(half)
    query_rows, key_rows, value_rows = jnp.split(qkv_rows, 3, axis=-1)
    key_all, value_all = (
        lax.all_gather(key_rows, "seq", axis=1, tiled=True),
        lax.all_gather(value_rows, "seq", axis=1, tiled=True),
    )
    length = key_all.shape[1]
    query_heads = query_rows.reshape(images, rows, HEADS, HEAD_DIM)
    key_heads = key_all.reshape(images, length, HEADS, HEAD_DIM)
    value_heads = value_all.reshape(images, length, HEADS, HEAD_DIM)
    scores = (
        jnp.einsum("bqhd,bkhd->bhqk", query_heads, key_heads, preferred_element_type=jnp.float32)
        * factor
    )
    highest = jnp.max(scores, axis=-1, keepdims=True)
    expo = jnp.exp(scores - highest)
    summed = jnp.sum(expo, axis=-1, keepdims=True)
    log_total = highest + jnp.log(summed)
    probs = expo / summed
    context = jnp.einsum(
        "bhqk,bkhd->bqhd", probs.astype(half), value_heads, preferred_element_type=jnp.float32
    )
    context_low = context.reshape(images, rows, width).astype(half)
    attended = linear(context_low, out_full, out_bias_full)
    mixed = tokens32 + gate_one * attended
    norm_two, norm_two_back = jax.vjp(modulate, mixed, scale_two, shift_two)
    hidden_two = norm_two.astype(half)
    upper = linear(hidden_two, up_full, up_bias_full)
    act, gelu_back = jax.vjp(gelu_tanh, upper)
    act_low = act.astype(half)
    feed = linear(act_low, down_full, down_bias_full)
    output32 = mixed + gate_two * feed
    output_low = output32.astype(half)
    first_pre = linear(output_low, first_full, first_bias_full)
    first_act, first_back = jax.vjp(jax.nn.silu, first_pre)
    first_low = first_act.astype(half)
    second_pre = linear(first_low, second_full, second_bias_full)
    second_act, second_back = jax.vjp(jax.nn.silu, second_pre)
    second_low = second_act.astype(half)
    latent = linear(second_low, third_full, third_bias_full)
    target32 = targets.astype(jnp.float32)
    cos_rows, cos_back = jax.vjp(lambda values: cosine(values, target32), latent)
    latent_grad = cos_back(jnp.full(cos_rows.shape, -0.5, jnp.float32))[0].astype(half)
    third_wg = weight_grad(second_low, latent_grad)
    third_bg = bias_grad(latent_grad)
    second_pre_grad = second_back(input_side(latent_grad, third_full))[0].astype(half)
    second_wg = weight_grad(first_low, second_pre_grad)
    second_bg = bias_grad(second_pre_grad)
    first_pre_grad = first_back(input_side(second_pre_grad, second_full))[0].astype(half)
    first_wg = weight_grad(output_low, first_pre_grad)
    first_bg = bias_grad(first_pre_grad)
    output_grad = cotangent.astype(jnp.float32) + input_side(first_pre_grad, first_full)
    feed_grad = (output_grad * gate_two).astype(half)
    gate_two_grad = jnp.sum(output_grad * feed, axis=1, keepdims=True)
    down_wg = weight_grad(act_low, feed_grad)
    down_bg = bias_grad(feed_grad)
    upper_grad = gelu_back(input_side(feed_grad, down_full))[0].astype(half)
    up_wg = weight_grad(hidden_two, upper_grad)
    up_bg = bias_grad(upper_grad)
    mixed_norm_grad, scale_two_grad, shift_two_grad = norm_two_back(input_side(upper_grad, up_full))
    mixed_grad = output_grad + mixed_norm_grad
    attended_grad = (mixed_grad * gate_one).astype(half)
    gate_one_grad = jnp.sum(mixed_grad * attended, axis=1, keepdims=True)
    out_wg = weight_grad(context_low, attended_grad)
    out_bg = bias_grad(attended_grad)
    context_grad = (
        input_side(attended_grad, out_full).astype(half).reshape(images, rows, HEADS, HEAD_DIM)
    )
    again = (
        jnp.einsum("bqhd,bkhd->bhqk", query_heads, key_heads, preferred_element_type=jnp.float32)
        * factor
    )
    probs_again = jnp.exp(again - log_total)
    prob_grad = jnp.einsum(
        "bqhd,bkhd->bhqk", context_grad, value_heads, preferred_element_type=jnp.float32
    )
    value_part = jnp.einsum(
        "bhqk,bqhd->bkhd",
        probs_again.astype(half),
        context_grad,
        preferred_element_type=jnp.float32,
    )
    score_grad = (
        probs_again * (prob_grad - jnp.sum(probs_again * prob_grad, axis=-1, keepdims=True))
    ).astype(half)
    query_grad = (
        jnp.einsum("bhqk,bkhd->bqhd", score_grad, key_heads, preferred_element_type=jnp.float32)
        * factor
    )
    key_part = (
        jnp.einsum("bhqk,bqhd->bkhd", score_grad, query_heads, preferred_element_type=jnp.float32)
        * factor
    )
    key_grad, value_grad = (
        lax.psum_scatter(
            key_part.reshape(images, length, width).astype(jnp.bfloat16),
            "seq",
            scatter_dimension=1,
            tiled=True,
        ).astype(jnp.float32),
        lax.psum_scatter(
            value_part.reshape(images, length, width).astype(jnp.bfloat16),
            "seq",
            scatter_dimension=1,
            tiled=True,
        ).astype(jnp.float32),
    )
    qkv_grad = jnp.concatenate(
        [query_grad.reshape(images, rows, width), key_grad, value_grad], axis=-1
    ).astype(half)
    qkv_wg = weight_grad(hidden_one, qkv_grad)
    qkv_bg = bias_grad(qkv_grad)
    token_norm_grad, scale_one_grad, shift_one_grad = norm_one_back(input_side(qkv_grad, qkv_full))
    input_grad = mixed_grad + token_norm_grad
    modulation_grad = jnp.concatenate(
        [
            shift_one_grad,
            scale_one_grad,
            gate_one_grad,
            shift_two_grad,
            scale_two_grad,
            gate_two_grad,
        ],
        axis=-1,
    )[:, 0, :]
    cond_wide = cond_low.astype(jnp.float32)
    cond_grad = cond_back(
        jnp.einsum("bj,ij->bi", modulation_grad, ada_full.astype(jnp.float32), precision=HIGH)
    )[0]
    loss_part = jnp.sum(cos_rows).reshape(1)
    cond_all, time_all, class_all, loss_all = (
        lax.all_gather(cond_grad.astype(jnp.bfloat16), ("dp", "seq"), axis=0, tiled=True).astype(
            cond_grad.dtype
        ),
        lax.all_gather(time_hot.astype(jnp.bfloat16), ("dp", "seq"), axis=0, tiled=True).astype(
            time_hot.dtype
        ),
        lax.all_gather(class_hot.astype(jnp.bfloat16), ("dp", "seq"), axis=0, tiled=True).astype(
            class_hot.dtype
        ),
        lax.all_gather(loss_part.astype(jnp.bfloat16), ("dp", "seq"), axis=0, tiled=True).astype(
            loss_part.dtype
        ),
    )
    time_grad = jnp.einsum("bt,bd->td", time_all, cond_all, precision=HIGH)
    class_grad = jnp.einsum("bt,bd->td", class_all, cond_all, precision=HIGH)
    total_rows = images * rows * lax.axis_size("dp") * lax.axis_size("seq")
    align_loss = -0.5 * jnp.sum(loss_all) / total_rows
    ada_wg = jnp.einsum("bi,bj->ij", cond_wide, modulation_grad, precision=HIGH)
    ada_bg = jnp.sum(modulation_grad, axis=0)
    ada_parts = (
        lax.psum_scatter(ada_wg.astype(jnp.bfloat16), "dp", scatter_dimension=0, tiled=True).astype(
            jnp.float32
        ),
        lax.psum_scatter(ada_bg.astype(jnp.bfloat16), "dp", scatter_dimension=0, tiled=True).astype(
            jnp.float32
        ),
    )
    ada_own, ada_bias_own = (
        lax.psum(ada_parts[0].astype(jnp.bfloat16), "seq").astype(jnp.float32),
        lax.psum(ada_parts[1].astype(jnp.bfloat16), "seq").astype(jnp.float32),
    )
    pieces = (
        lax.psum_scatter(qkv_wg.astype(jnp.bfloat16), "dp", scatter_dimension=0, tiled=True).astype(
            jnp.float32
        ),
        lax.psum_scatter(qkv_bg.astype(jnp.bfloat16), "dp", scatter_dimension=0, tiled=True).astype(
            jnp.float32
        ),
        lax.psum_scatter(out_wg.astype(jnp.bfloat16), "dp", scatter_dimension=0, tiled=True).astype(
            jnp.float32
        ),
        lax.psum_scatter(out_bg.astype(jnp.bfloat16), "dp", scatter_dimension=0, tiled=True).astype(
            jnp.float32
        ),
        lax.psum_scatter(up_wg.astype(jnp.bfloat16), "dp", scatter_dimension=0, tiled=True).astype(
            jnp.float32
        ),
        lax.psum_scatter(up_bg.astype(jnp.bfloat16), "dp", scatter_dimension=0, tiled=True).astype(
            jnp.float32
        ),
        lax.psum_scatter(
            down_wg.astype(jnp.bfloat16), "dp", scatter_dimension=0, tiled=True
        ).astype(jnp.float32),
        lax.psum_scatter(
            down_bg.astype(jnp.bfloat16), "dp", scatter_dimension=0, tiled=True
        ).astype(jnp.float32),
        lax.psum_scatter(
            first_wg.astype(jnp.bfloat16), "dp", scatter_dimension=0, tiled=True
        ).astype(jnp.float32),
        lax.psum_scatter(
            first_bg.astype(jnp.bfloat16), "dp", scatter_dimension=0, tiled=True
        ).astype(jnp.float32),
        lax.psum_scatter(
            second_wg.astype(jnp.bfloat16), "dp", scatter_dimension=0, tiled=True
        ).astype(jnp.float32),
        lax.psum_scatter(
            second_bg.astype(jnp.bfloat16), "dp", scatter_dimension=0, tiled=True
        ).astype(jnp.float32),
        lax.psum_scatter(
            third_wg.astype(jnp.bfloat16), "dp", scatter_dimension=0, tiled=True
        ).astype(jnp.float32),
        lax.psum_scatter(
            third_bg.astype(jnp.bfloat16), "dp", scatter_dimension=0, tiled=True
        ).astype(jnp.float32),
    )
    owned = (
        lax.psum(pieces[0].astype(jnp.bfloat16), "seq").astype(jnp.float32),
        lax.psum(pieces[1].astype(jnp.bfloat16), "seq").astype(jnp.float32),
        lax.psum(pieces[2].astype(jnp.bfloat16), "seq").astype(jnp.float32),
        lax.psum(pieces[3].astype(jnp.bfloat16), "seq").astype(jnp.float32),
        lax.psum(pieces[4].astype(jnp.bfloat16), "seq").astype(jnp.float32),
        lax.psum(pieces[5].astype(jnp.bfloat16), "seq").astype(jnp.float32),
        lax.psum(pieces[6].astype(jnp.bfloat16), "seq").astype(jnp.float32),
        lax.psum(pieces[7].astype(jnp.bfloat16), "seq").astype(jnp.float32),
        lax.psum(pieces[8].astype(jnp.bfloat16), "seq").astype(jnp.float32),
        lax.psum(pieces[9].astype(jnp.bfloat16), "seq").astype(jnp.float32),
        lax.psum(pieces[10].astype(jnp.bfloat16), "seq").astype(jnp.float32),
        lax.psum(pieces[11].astype(jnp.bfloat16), "seq").astype(jnp.float32),
        lax.psum(pieces[12].astype(jnp.bfloat16), "seq").astype(jnp.float32),
        lax.psum(pieces[13].astype(jnp.bfloat16), "seq").astype(jnp.float32),
    )
    return (
        output_low,
        input_grad,
        align_loss,
        time_grad,
        class_grad,
        ada_own,
        ada_bias_own,
        owned[0],
        owned[1],
        owned[2],
        owned[3],
        owned[4],
        owned[5],
        owned[6],
        owned[7],
        owned[8],
        owned[9],
        owned[10],
        owned[11],
        owned[12],
        owned[13],
    )


def solution(mesh):
    placed = (
        P("dp", "seq", None),
        P("dp", "seq", None),
        P("dp", "seq", None),
        P("dp"),
        P("dp"),
        P(),
        P(),
        P("dp", None),
        P("dp"),
        P("dp", None),
        P("dp"),
        P("dp", None),
        P("dp"),
        P("dp", None),
        P("dp"),
        P("dp", None),
        P("dp"),
        P("dp", None),
        P("dp"),
        P("dp", None),
        P("dp"),
        P("dp", None),
        P("dp"),
    )
    return jax.shard_map(
        shards,
        mesh=mesh,
        in_specs=placed,
        out_specs=(
            P("dp", "seq", None),
            P("dp", "seq", None),
            P(),
            P(),
            P(),
            P("dp", None),
            P("dp"),
            P("dp", None),
            P("dp"),
            P("dp", None),
            P("dp"),
            P("dp", None),
            P("dp"),
            P("dp", None),
            P("dp"),
            P("dp", None),
            P("dp"),
            P("dp", None),
            P("dp"),
            P("dp", None),
            P("dp"),
        ),
        check_vma=False,
    )
```

profile of v0, /device:TPU:1, one launch (start us, length us, event | category | flops | bytes accessed | tf_op | source)
XLA Modules:
  0.0 1856.7 jit_solution(8672066293554293570)
XLA Ops:
  17.6 24.2 %all-reduce.16 = (bf16[3456]{0:T(1024)(128)(2,1)S(1)}, bf16[6912]{0:T(1024)(128)(2,1)S(1)}, bf16[1152]{0:T(1024)(128)(2,1)}, bf16[1152]{0:T(1024)(128)(2,1)S(1)}...) all-reduce(bf16[3456]{0:T(1024)(128)(2,1)S(1)} %dynamic-update-slice.1, ...), channel_id=1, replica_groups=mesh['dp'=8,'seq'=4] {'dp'}, use_global_device_ids=true, to_apply=%add.1 | all-reduce | flops 18048 | bytes 72192
  48.8 51.8 %all-gather.16.cloned.1.call-done = bf16[1152,6912]{1,0:T(8,128)(2,1)} async-done(((bf16[144,6912]{1,0:T(8,128)(2,1)}), bf16[1152,6912]{1,0:T(8,128)(2,1)}) %all-gather.16.cloned.1.call-update) | async-done | bytes 15925264 | tf_op jit(solution)/shard_map/all_gather | solution.py:88
  108.9 46.8 %all-gather.18.cloned.1.call-done = bf16[1152,3456]{1,0:T(8,128)(2,1)} async-done(((bf16[144,3456]{1,0:T(8,128)(2,1)}), bf16[1152,3456]{1,0:T(8,128)(2,1)}) %all-gather.18.cloned.1.call-update) | async-done | bytes 7962640 | tf_op jit(solution)/shard_map/all_gather | solution.py:90
  200.3 55.2 %all-gather.22.cloned.1.call-done = bf16[2,1024,1152]{2,1,0:T(8,128)(2,1)} async-done(((bf16[2,256,1152]{2,1,0:T(8,128)(2,1)}), bf16[2,1024,1152]{2,1,0:T(8,128)(2,1)}) %all-gather.22.cloned.1.call-update) | async-done | bytes 4718608 | tf_op jit(solution)/shard_map/all_gather | solution.py:141
  293.5 51.9 %all-gather.20.cloned.1.call-done = bf16[2,1024,1152]{2,1,0:T(8,128)(2,1)} async-done(((bf16[2,256,1152]{2,1,0:T(8,128)(2,1)}), bf16[2,1024,1152]{2,1,0:T(8,128)(2,1)}) %all-gather.20.cloned.1.call-update) | async-done | bytes 4718608 | tf_op jit(solution)/shard_map/all_gather | solution.py:142
  382.7 60.3 %all-gather.26.cloned.1.call-done = bf16[1152,4608]{1,0:T(8,128)(2,1)} async-done(((bf16[144,4608]{1,0:T(8,128)(2,1)}), bf16[1152,4608]{1,0:T(8,128)(2,1)}) %all-gather.26.cloned.1.call-update) | async-done | bytes 10616848 | tf_op jit(solution)/shard_map/all_gather | solution.py:107
  455.9 53.4 %all-gather.28.cloned.1.call-done = bf16[4608,1152]{1,0:T(8,128)(2,1)} async-done(((bf16[576,1152]{1,0:T(8,128)(2,1)}), bf16[4608,1152]{1,0:T(8,128)(2,1)}) %all-gather.28.cloned.1.call-update) | async-done | bytes 10616848 | tf_op jit(solution)/shard_map/all_gather | solution.py:109
  523.5 27.2 %all-gather.30.cloned.1.call-done = bf16[1152,2048]{1,0:T(8,128)(2,1)} async-done(((bf16[144,2048]{1,0:T(8,128)(2,1)}), bf16[1152,2048]{1,0:T(8,128)(2,1)}) %all-gather.30.cloned.1.call-update) | async-done | bytes 4718608 | tf_op jit(solution)/shard_map/all_gather | solution.py:111
  558.3 49.3 %all-gather.32.cloned.1.call-done = bf16[2048,2048]{1,0:T(8,128)(2,1)} async-done(((bf16[256,2048]{1,0:T(8,128)(2,1)}), bf16[2048,2048]{1,0:T(8,128)(2,1)}) %all-gather.32.cloned.1.call-update) | async-done | bytes 8388624 | tf_op jit(solution)/shard_map/all_gather | solution.py:113
  732.7 26.1 %multiply_reduce_fusion = (f32[2,16,256]{2,1,0:T(8,128)}, f32[2,16,256,1024]{3,2,1,0:T(8,128)}) fusion(f32[2,16,256,1024]{3,2,1,0:T(8,128)} %get-tuple-element.86, f32[2,16,256]{2,1,0:T(8,128)} %log_add_fusion, bf16[2,256,16,72]{1,3,2,0:T(8,128)(2,1)S(1)} %bitcast.198, bf16[2,1024,16,72]{1,3,2,0:T(8,128)(2,1)} %bitcast.194), kind=kOutput, calls=%fused_computation.1 | convolution fusion | flops 1241505792 | bytes 73072640 | tf_op jit(solution)/shard_map/bqhd,bkhd->bhqk/dot_general | solution.py:211
  758.8 28.2 %multiply_convert_fusion = bf16[2,16,256,1024]{3,2,1,0:T(8,128)(2,1)} fusion(f32[2,16,256,1024]{3,2,1,0:T(8,128)} %get-tuple-element.95, f32[2,16,256,1024]{3,2,1,0:T(8,128)} %get-tuple-element.86, f32[2,16,256]{2,1,0:T(8,128)} %get-tuple-element.94, f32[2,16,256]{2,1,0:T(8,128)} %log_add_fusion), kind=kLoop, calls=%fused_computation | loop fusion | flops 41943040 | bytes 83951616 | tf_op jit(solution)/shard_map/convert_element_type | solution.py:222
  871.6 34.1 %reduce-scatter.11.cloned.1.call-done = bf16[2,256,1152]{2,1,0:T(8,128)(2,1)} async-done(((bf16[2,1024,1152]{2,1,0:T(8,128)(2,1)}), bf16[2,256,1152]{2,1,0:T(8,128)(2,1)}) %reduce-scatter.11.cloned.1.call-update) | async-done | bytes 1179664 | tf_op jit(solution)/shard_map/reduce_scatter | solution.py:232
  954.0 50.5 %reduce-scatter.29.cloned.1.call-done = bf16[256,768]{1,0:T(8,128)(2,1)} async-done(((bf16[2048,768]{1,0:T(8,128)(2,1)}), bf16[256,768]{1,0:T(8,128)(2,1)}) %reduce-scatter.29.cloned.1.call-update) | async-done | bytes 393232 | tf_op jit(solution)/shard_map/reduce_scatter | solution.py:337
  1004.5 57.2 %reduce-scatter.25.cloned.1.call-done = bf16[144,2048]{1,0:T(8,128)(2,1)} async-done(((bf16[1152,2048]{1,0:T(8,128)(2,1)}), bf16[144,2048]{1,0:T(8,128)(2,1)}) %reduce-scatter.25.cloned.1.call-update) | async-done | bytes 589840 | tf_op jit(solution)/shard_map/reduce_scatter | solution.py:325
  1061.7 75.0 %reduce-scatter.27.cloned.1.call-done = bf16[256,2048]{1,0:T(8,128)(2,1)} async-done(((bf16[2048,2048]{1,0:T(8,128)(2,1)}), bf16[256,2048]{1,0:T(8,128)(2,1)}) %reduce-scatter.27.cloned.1.call-update) | async-done | bytes 1048592 | tf_op jit(solution)/shard_map/reduce_scatter | solution.py:331
  1136.7 85.6 %reduce-scatter.23.cloned.1.call-done = bf16[576,1152]{1,0:T(8,128)(2,1)} async-done(((bf16[4608,1152]{1,0:T(8,128)(2,1)}), bf16[576,1152]{1,0:T(8,128)(2,1)}) %reduce-scatter.23.cloned.1.call-update) | async-done | bytes 1327120 | tf_op jit(solution)/shard_map/reduce_scatter | solution.py:319
  1222.3 85.6 %reduce-scatter.21.cloned.1.call-done = bf16[144,4608]{1,0:T(8,128)(2,1)} async-done(((bf16[1152,4608]{1,0:T(8,128)(2,1)}), bf16[144,4608]{1,0:T(8,128)(2,1)}) %reduce-scatter.21.cloned.1.call-update) | async-done | bytes 1327120 | tf_op jit(solution)/shard_map/reduce_scatter | solution.py:313
  1307.8 73.6 %reduce-scatter.17.cloned.1.call-done = bf16[144,3456]{1,0:T(8,128)(2,1)} async-done(((bf16[1152,3456]{1,0:T(8,128)(2,1)}), bf16[144,3456]{1,0:T(8,128)(2,1)}) %reduce-scatter.17.cloned.1.call-update) | async-done | bytes 995344 | tf_op jit(solution)/shard_map/reduce_scatter | solution.py:301
  1381.4 116.8 %reduce-scatter.15.cloned.1.call-done = bf16[144,6912]{1,0:T(8,128)(2,1)} async-done(((bf16[1152,6912]{1,0:T(8,128)(2,1)}), bf16[144,6912]{1,0:T(8,128)(2,1)}) %reduce-scatter.15.cloned.1.call-update) | async-done | bytes 1990672 | tf_op jit(solution)/shard_map/reduce_scatter | solution.py:289
  1503.3 73.6 %all-gather.4 = bf16[32,2,1000]{2,1,0:T(2,128)(2,1)} all-gather(bf16[1,2,1000]{2,1,0:T(2,128)(2,1)S(1)} %fusion.110), channel_id=1, replica_groups=mesh['dp'=8,'seq'=4] {'dp','seq'}, dimensions={0}, use_global_device_ids=true | all-gather | bytes 132000 | tf_op jit(solution)/shard_map/all_gather | solution.py:275
  1579.3 72.0 %all-gather.2 = bf16[32,2,1000]{2,1,0:T(2,128)(2,1)} all-gather(bf16[1,2,1000]{2,1,0:T(2,128)(2,1)S(1)} %fusion.109), channel_id=1, replica_groups=mesh['dp'=8,'seq'=4] {'dp','seq'}, dimensions={0}, use_global_device_ids=true | all-gather | bytes 132000 | tf_op jit(solution)/shard_map/all_gather | solution.py:272
  1655.3 47.6 %all-reduce.6 = bf16[32]{0:T(256)(128)(2,1)} all-reduce(bf16[32]{0:T(256)(128)(2,1)} %dynamic-update-slice.6), channel_id=1, replica_groups=mesh['dp'=8,'seq'=4] {'dp','seq'}, use_global_device_ids=true, to_apply=%add.6 | all-reduce | flops 32 | bytes 128
  1707.5 23.4 %all-reduce.15 = (bf16[6912]{0:T(1024)(128)(2,1)S(1)}, bf16[3456]{0:T(1024)(128)(2,1)S(1)}, bf16[1152]{0:T(1024)(128)(2,1)S(1)}, bf16[4608]{0:T(1024)(128)(2,1)S...) all-reduce(bf16[6912]{0:T(1024)(128)(2,1)} %reduce_sum.319, ...), channel_id=5, replica_groups=mesh['dp'=8,'seq'=4] {'dp'}, use_global_device_ids=true, to_apply=%region_27.28.clone | all-reduce | flops 22144 | bytes 88576
  1764.9 62.6 %all-gather.3 = bf16[32,2,1152]{2,1,0:T(2,128)(2,1)S(1)} all-gather(bf16[1,2,1152]{2,1,0:T(2,128)(2,1)S(1)} %fusion.103), channel_id=1, replica_groups=mesh['dp'=8,'seq'=4] {'dp','seq'}, dimensions={0}, use_global_device_ids=true | all-gather | bytes 152064 | tf_op jit(solution)/shard_map/all_gather | solution.py:269
  (363 shorter events, 500.0 us)
Async XLA Ops:
  7.2 93.4 %all-gather.16.cloned.1.call-start = ((), (), s32[]{:S(2)}) async-start(), calls=%async_computation.10 | async-start | bytes 17915904 | tf_op jit(solution)/shard_map/all_gather | solution.py:88
  11.1 144.6 %all-gather.18.cloned.1.call-start = ((), (), s32[]{:S(2)}) async-start(), calls=%async_computation.11 | async-start | bytes 8957952 | tf_op jit(solution)/shard_map/all_gather | solution.py:90
  12.2 243.3 %all-gather.22.cloned.1.call-start = ((), (), s32[]{:S(2)}) async-start(), calls=%async_computation.13 | async-start | bytes 5898240 | tf_op jit(solution)/shard_map/all_gather | solution.py:141
  166.3 179.2 %all-gather.20.cloned.1.call-start = ((), (), s32[]{:S(2)}) async-start(), calls=%async_computation.12 | async-start | bytes 5898240 | tf_op jit(solution)/shard_map/all_gather | solution.py:142
  166.9 210.0 %all-gather.24.cloned.1.call-start = ((), (), s32[]{:S(2)}) async-start(), calls=%async_computation.14 | async-start | bytes 2985984 | tf_op jit(solution)/shard_map/all_gather | solution.py:92
  167.7 275.3 %all-gather.26.cloned.1.call-start = ((), (), s32[]{:S(2)}) async-start(), calls=%async_computation.15 | async-start | bytes 11943936 | tf_op jit(solution)/shard_map/all_gather | solution.py:107
  170.7 338.6 %all-gather.28.cloned.1.call-start = ((), (), s32[]{:S(2)}) async-start(), calls=%async_computation.16 | async-start | bytes 11943936 | tf_op jit(solution)/shard_map/all_gather | solution.py:109
  174.1 376.6 %all-gather.30.cloned.1.call-start = ((), (), s32[]{:S(2)}) async-start(), calls=%async_computation.17 | async-start | bytes 5308416 | tf_op jit(solution)/shard_map/all_gather | solution.py:111
  175.1 432.5 %all-gather.32.cloned.1.call-start = ((), (), s32[]{:S(2)}) async-start(), calls=%async_computation.18 | async-start | bytes 9437184 | tf_op jit(solution)/shard_map/all_gather | solution.py:113
  178.1 464.1 %all-gather.34.cloned.1.call-start = ((), (), s32[]{:S(2)}) async-start(), calls=%async_computation.19 | async-start | bytes 3538944 | tf_op jit(solution)/shard_map/all_gather | solution.py:115
  179.0 692.6 %reduce-scatter.13.cloned.1.call-start = ((), (), s32[]{:S(2)}) async-start(), calls=%async_computation.21 | async-start | bytes 5898240 | tf_op jit(solution)/shard_map/reduce_scatter | solution.py:238
  382.7 318.8 %copy-start.48 = (f32[2,256]{1,0:T(2,128)}, f32[2,256]{1,0:T(2,128)S(1)}, u32[]{:S(2)}) copy-start(f32[2,256]{1,0:T(2,128)S(1)} %fusion.116) | copy-start | bytes 6148
  732.7 173.0 %reduce-scatter.11.cloned.1.call-start = ((), (), s32[]{:S(2)}) async-start(), calls=%async_computation.20 | async-start | bytes 5898240 | tf_op jit(solution)/shard_map/reduce_scatter | solution.py:232
  804.8 149.2 %reduce-scatter.19.cloned.1.call-start = ((), (), s32[]{:S(2)}) async-start(), calls=%async_computation.24 | async-start | bytes 2985984 | tf_op jit(solution)/shard_map/reduce_scatter | solution.py:307
  810.6 193.9 %reduce-scatter.29.cloned.1.call-start = ((), (), s32[]{:S(2)}) async-start(), calls=%async_computation.29 | async-start | bytes 3538944 | tf_op jit(solution)/shard_map/reduce_scatter | solution.py:337
  816.8 244.8 %reduce-scatter.25.cloned.1.call-start = ((), (), s32[]{:S(2)}) async-start(), calls=%async_computation.27 | async-start | bytes 5308416 | tf_op jit(solution)/shard_map/reduce_scatter | solution.py:325
  823.6 313.1 %reduce-scatter.27.cloned.1.call-start = ((), (), s32[]{:S(2)}) async-start(), calls=%async_computation.28 | async-start | bytes 9437184 | tf_op jit(solution)/shard_map/reduce_scatter | solution.py:331
  835.3 387.0 %reduce-scatter.23.cloned.1.call-start = ((), (), s32[]{:S(2)}) async-start(), calls=%async_computation.26 | async-start | bytes 11943936 | tf_op jit(solution)/shard_map/reduce_scatter | solution.py:319
  849.2 458.7 %reduce-scatter.21.cloned.1.call-start = ((), (), s32[]{:S(2)}) async-start(), calls=%async_computation.25 | async-start | bytes 11943936 | tf_op jit(solution)/shard_map/reduce_scatter | solution.py:313
  860.6 520.8 %reduce-scatter.17.cloned.1.call-start = ((), (), s32[]{:S(2)}) async-start(), calls=%async_computation.23 | async-start | bytes 8957952 | tf_op jit(solution)/shard_map/reduce_scatter | solution.py:301
  915.1 583.2 %reduce-scatter.15.cloned.1.call-start = ((), (), s32[]{:S(2)}) async-start(), calls=%async_computation.22 | async-start | bytes 17915904 | tf_op jit(solution)/shard_map/reduce_scatter | solution.py:289
  948.7 884.9 %all-reduce.21.cloned.1.call-start = ((), (), s32[]{:S(2)}) async-start(), calls=%async_computation.30 | async-start | bytes 16007168 | tf_op jit(solution)/shard_map/psum | solution.py:297
  1498.3 208.1 %copy-start.22 = (bf16[2,256,1152]{2,1,0:T(8,128)(2,1)S(1)}, bf16[2,256,1152]{2,1,0:T(8,128)(2,1)}, u32[]{:S(2)}) copy-start(bf16[2,256,1152]{2,1,0:T(8,128)(2,1)} %reduce-scatter.11.cloned.1.call-done) | copy-start | bytes 3538948
  1498.3 209.3 %copy-start.52 = (bf16[1152]{0:T(1024)(128)(2,1)S(1)}, bf16[1152]{0:T(1024)(128)(2,1)}, u32[]{:S(2)}) copy-start(bf16[1152]{0:T(1024)(128)(2,1)} %get-tuple-element.64) | copy-start | bytes 6916
  (82 other events, 1984.4 us)
Sparse Core Ops, SparseCore 0:
  11.2 89.3 all-gather.15
  103.0 52.5 all-gather.17
  166.4 89.0 all-gather.21
  257.5 87.8 all-gather.19
  347.7 29.0 all-gather.23
  379.1 63.8 all-gather.25
  445.4 63.8 all-gather.27
  511.7 38.9 all-gather.29
  553.2 54.3 all-gather.31
  609.9 32.3 all-gather.33
  732.8 84.8 reduce-scatter.12
  819.9 85.7 reduce-scatter.10
  909.7 44.2 reduce-scatter.18
  958.2 46.2 reduce-scatter.28
  1007.8 53.8 reduce-scatter.24
  1065.4 71.2 reduce-scatter.26
  1140.0 82.1 reduce-scatter.22
  1225.6 82.1 reduce-scatter.20
  1311.4 70.0 reduce-scatter.16
  1385.3 112.8 reduce-scatter.14
  1501.7 291.4 all-reduce.20
where the time goes:
time: 1870 us; the launch traced here: 1860 us
  waiting for transfers between devices  1010 us (54%)
  matrix products  336 us (18%)
  blocking collectives  333 us (18%)
  other arithmetic  102 us (5%)
  local copies, waits for them, and re-layouts  47.1 us (3%)
  between operations  24.8 us (1%)
    reduce_scatter x1, waiting for transfers between devices, shards(): lax.psum_scatter(ada_wg.astype(jnp.bfloat16), 'dp', scatter_dimension=0,...  117 us
    unnamed x3, blocking collectives  95.2 us
    reduce_scatter x1, waiting for transfers between devices, shards(): lax.psum_scatter(up_wg.astype(jnp.bfloat16), 'dp', scatter_dimension=0, t...  85.6 us
    reduce_scatter x1, waiting for transfers between devices, shards(): lax.psum_scatter(down_wg.astype(jnp.bfloat16), 'dp', scatter_dimension=0,...  85.6 us
    reduce_scatter x1, waiting for transfers between devices, shards(): lax.psum_scatter(second_wg.astype(jnp.bfloat16), 'dp', scatter_dimension=...  75 us
    all_gather x1, blocking collectives, shards(): lax.all_gather(class_hot.astype(jnp.bfloat16), ('dp', 'seq'), axis=0, til...  73.6 us
    reduce_scatter x1, waiting for transfers between devices, shards(): lax.psum_scatter(qkv_wg.astype(jnp.bfloat16), 'dp', scatter_dimension=0,...  73.6 us
    all_gather x1, blocking collectives, shards(): lax.all_gather(time_hot.astype(jnp.bfloat16), ('dp', 'seq'), axis=0, tile...  72 us
  transfers between devices with their start and end apart: 21, of which 19 were waited for; matrix products, arithmetic and copies ran while one was open for 19% of the time, Pallas kernels for 0%

commit v1 on v0

v1 whole, which is shorter than its diff:
```python
import functools
import math

import jax
import jax.numpy as jnp
from jax import lax
from jax.experimental import pallas as pl
from jax.experimental.pallas import tpu as pltpu
from jax.sharding import PartitionSpec as P

HEADS = 16
HEAD_DIM = 72
EPS_NORM = 1e-06
HIGH = lax.Precision.HIGHEST
HALF = jnp.bfloat16
WIDE = jnp.float32
VMEM_BYTES = 56 * 1024 * 1024
GELU_A = math.sqrt(2.0 / math.pi)
GELU_B = 0.044715
SCALE = 1
MARK = (8, 128)
DONE = {}
TAKES = {
    "qkv": 13,
    "attention": 30,
    "out": 8,
    "feed": 27,
    "tap": 16,
    "latent": 9,
    "cosine": 9,
    "tap_back": 16,
    "third_grad": 5,
    "second_grad": 8,
    "first_grad": 6,
    "feed_back": 28,
    "down_grad": 12,
    "up_grad": 12,
    "mix_back": 14,
    "out_grad": 5,
    "attention_back": 31,
    "qkv_back": 12,
    "qkv_grad": 10,
    "input_grad": 5,
    "split_qkv": 3,
    "split_rest": 3,
    "pack_near": 4,
    "pack_far": 4,
    "condition": 2,
}


def cost(microseconds):
    return pl.CostEstimate(
        flops=int(microseconds * SCALE * 1.15e9),
        bytes_accessed=int(microseconds * SCALE * 3.6e6),
        transcendentals=0,
    )


def dot(left, right):
    return jnp.dot(left, right, preferred_element_type=WIDE)


def dot_nt(left, right):
    return lax.dot_general(left, right, (((1,), (1,)), ((), ())), preferred_element_type=WIDE)


def normed(values):
    centre = values - jnp.mean(values, axis=-1, keepdims=True)
    spread = jnp.mean(centre * centre, axis=-1, keepdims=True)
    inverse = lax.rsqrt(spread + EPS_NORM)
    return centre * inverse, inverse


def normed_back(norm, inverse, grad):
    return (
        grad
        - jnp.mean(grad, axis=-1, keepdims=True)
        - norm * jnp.mean(grad * norm, axis=-1, keepdims=True)
    ) * inverse


def sigmoid(values):
    return 1.0 / (1.0 + jnp.exp(-values))


def silu_back(pre, grad):
    gate = sigmoid(pre)
    return grad * (gate * (1.0 + pre * (1.0 - gate)))


def gelu(values):
    inner = jnp.tanh(GELU_A * (values + GELU_B * (values * values * values)))
    return 0.5 * values * (1.0 + inner)


def gelu_back(values, grad):
    square = values * values
    inner = jnp.tanh(GELU_A * (values + GELU_B * (square * values)))
    slope = 0.5 * (1.0 + inner) + 0.5 * values * (1.0 - inner * inner) * (
        GELU_A * (1.0 + 3.0 * GELU_B * square)
    )
    return grad * slope


def total(values):
    return jnp.sum(values, axis=0, keepdims=True)


def spans(size, most):
    count = -(-size // most)
    while size % count or (size // count) % 128:
        count += 1
        if count > size // 128:
            return [(0, size)]
    return [(k * (size // count), size // count) for k in range(count)]


def joined(ref, index=slice(None)):
    return jnp.concatenate([ref[h] for h in range(ref.shape[0])], axis=-1)


class Weight:
    def __init__(self, me, step, arrays, how, store, sems):
        self.me, self.step, self.arrays, self.how = me, step, arrays, how
        self.store, self.sems = store, sems

    def copies(self):
        groups, by_me, height, _ = self.how
        count = 0
        for places, pieces in groups:
            for r, (number, base) in enumerate(places):
                start = pl.multiple_of((self.me ^ r) * height, height) if by_me else r * height
                for row, rows, column, columns, to_row, to_column in pieces:
                    yield pltpu.make_async_copy(
                        self.arrays[number].at[pl.ds(base + row, rows), pl.ds(column, columns)],
                        self.store.at[pl.ds(start + to_row, rows), pl.ds(to_column, columns)],
                        self.sems.at[count],
                    )
                    count += 1

    def start(self):
        @pl.when(self.step == 0)
        def _():
            for copy in self.copies():
                copy.start()

    def ready(self):
        @pl.when(self.step == 0)
        def _():
            for copy in self.copies():
                copy.wait()

        return self.store


def token_kernel(body, counts, hows, me_ref, *refs):
    n_tok, n_const, n_blocks, n_after, n_out, n_sum = counts
    refs = list(refs)
    take = lambda n: [refs.pop(0) for _ in range(n)]
    toks, consts = take(n_tok), take(n_const)
    blocks = [take(n) for n in n_blocks]
    take(n_after)
    outs, sums, (mark,) = take(n_out), take(n_sum), take(1)
    step = pl.program_id(0)

    @pl.when(step == 0)
    def _():
        mark[...] = jnp.zeros_like(mark)

    weights = [
        Weight(me_ref[0], step, group, hows[k], refs[2 * k], refs[2 * k + 1])
        for k, group in enumerate(blocks)
    ]
    for weight in weights:
        weight.start()
    if sums:

        @pl.when(step == 0)
        def _():
            for ref in sums:
                ref[...] = jnp.zeros_like(ref)

    body(toks, consts, weights, outs, sums)


def token_call(name, body, me, toks, consts, weights, outs, sums, rows, tile, after=()):
    steps = rows // tile

    def spec(shape, dim, swapped=False):
        block = tuple(tile if k == dim else s for k, s in enumerate(shape))

        def place(i, me_ref):
            at = lax.rem(i + steps // 2, steps) if swapped else i
            return tuple(at if k == dim else 0 for k in range(len(shape)))

        return pl.BlockSpec(block, place)

    def whole(shape):
        return pl.BlockSpec(shape, lambda i, me_ref: (0,) * len(shape))

    in_specs = [spec(a.shape, a.ndim - 2, swapped) for a, swapped in toks]
    in_specs += [whole(c.shape) for c in consts]
    blocks = [array for group, _ in weights for array in group]
    in_specs += [pl.BlockSpec(memory_space=pl.ANY)] * (len(blocks) + len(after))
    out_specs = [spec(shape, dim) for shape, _, dim in outs] + [whole(shape) for shape in sums]
    out_shape = [jax.ShapeDtypeStruct(shape, dtype) for shape, dtype, _ in outs]
    out_shape += [jax.ShapeDtypeStruct(shape, WIDE) for shape in sums]
    out_specs.append(whole(MARK))
    out_shape.append(jax.ShapeDtypeStruct(MARK, WIDE))
    scratch = []
    for _, (groups, _, height, columns) in weights:
        scratch += [
            pltpu.VMEM((height * len(groups[0][0]), columns), HALF),
            pltpu.SemaphoreType.DMA((sum(len(a) * len(b) for a, b in groups),)),
        ]
    counts = (len(toks), len(consts), [len(g) for g, _ in weights], len(after), len(outs), len(sums))
    *found, DONE[name] = pl.pallas_call(
        functools.partial(token_kernel, body, counts, [how for _, how in weights]),
        grid_spec=pltpu.PrefetchScalarGridSpec(
            num_scalar_prefetch=1,
            grid=(steps,),
            in_specs=in_specs,
            out_specs=out_specs,
            scratch_shapes=scratch,
        ),
        out_shape=out_shape,
        compiler_params=pltpu.CompilerParams(
            dimension_semantics=("arbitrary",), vmem_limit_bytes=VMEM_BYTES
        ),
        cost_estimate=cost(TAKES[name]),
        name=name,
    )(me, *[a for a, _ in toks], *consts, *blocks, *after)
    return found


def qkv_body(toks, consts, weights, outs, sums):
    (x,), (shift, scale, bias), (weight,) = toks, consts, weights
    hidden_t, query, key, value = outs
    norm, _ = normed(x[...].astype(WIDE))
    hidden = norm * (1.0 + scale[...]) + shift[...]
    low = hidden.astype(HALF)
    hidden_t[...] = hidden.T.astype(HALF)
    store = weight.ready()
    width = store.shape[1] // 3
    for k, out in enumerate((query, key, value)):
        part = dot(low, store[:, k * width : (k + 1) * width])
        part = (part + bias[:, k * width : (k + 1) * width]).astype(HALF)
        for h in range(out.shape[0]):
            out[h] = part[:, h * HEAD_DIM : (h + 1) * HEAD_DIM]


def attention_kernel(query, key, value, *refs):
    context, lse, mark = refs[-3:]
    mark[...] = jnp.zeros_like(mark)
    factor = 1.0 / math.sqrt(HEAD_DIM)
    keys, values = key[0], value[0]
    rows = query.shape[1]
    tile = min(rows, 256)
    for start in range(0, rows, tile):
        at = slice(start, start + tile)
        scores = dot_nt(keys, query[0, at, :]) * factor
        highest = jnp.max(scores, axis=0, keepdims=True)
        expo = jnp.exp(scores - highest)
        summed = jnp.sum(expo, axis=0, keepdims=True)
        probs = (expo / summed).astype(HALF)
        lse[0, :, at] = highest + jnp.log(summed)
        found = lax.dot_general(
            values, probs, (((0,), (0,)), ((), ())), preferred_element_type=WIDE
        )
        context[0, at, :] = found.T.astype(HALF)


def attention_call(query, key, value, after=()):
    heads, rows, _ = query.shape
    block = pl.BlockSpec((1, rows, HEAD_DIM), lambda h: (h, 0, 0))
    line = pl.BlockSpec((1, 1, rows), lambda h: (h, 0, 0))
    *found, DONE["attention"] = pl.pallas_call(
        attention_kernel,
        grid=(heads,),
        in_specs=[block] * 3 + [pl.BlockSpec(memory_space=pl.ANY)] * len(after),
        out_specs=[block, line, pl.BlockSpec(MARK, lambda h: (0, 0))],
        out_shape=[
            jax.ShapeDtypeStruct(query.shape, HALF),
            jax.ShapeDtypeStruct((heads, 1, rows), WIDE),
            jax.ShapeDtypeStruct(MARK, WIDE),
        ],
        compiler_params=pltpu.CompilerParams(
            dimension_semantics=("arbitrary",), vmem_limit_bytes=VMEM_BYTES
        ),
        cost_estimate=cost(TAKES["attention"]),
        name="attention",
    )(query, key, value, *after)
    return found


def attention_back_kernel(query, key, value, grad, lse, *refs):
    dquery, dkey, dvalue, mark, sum_key, sum_value = refs[-6:]
    mark[...] = jnp.zeros_like(mark)
    factor = 1.0 / math.sqrt(HEAD_DIM)
    keys, values = key[0], value[0]
    rows = query.shape[1]
    tile = min(rows, 256)
    for start in range(0, rows, tile):
        at = slice(start, start + tile)
        queries, grads = query[0, at, :], grad[0, at, :]
        probs = jnp.exp(dot_nt(keys, queries) * factor - lse[0, :, at])
        dprobs = dot_nt(values, grads)
        held = jnp.sum(probs * dprobs, axis=0, keepdims=True)
        dscores = (probs * (dprobs - held)).astype(HALF)
        value_part = dot(probs.astype(HALF), grads)
        key_part = dot(dscores, queries)
        if start == 0:
            sum_value[...] = value_part
            sum_key[...] = key_part
        else:
            sum_value[...] += value_part
            sum_key[...] += key_part
        found = lax.dot_general(
            keys, dscores, (((0,), (0,)), ((), ())), preferred_element_type=WIDE
        )
        dquery[0, at, :] = (found * factor).T.astype(HALF)
    dkey[0] = (sum_key[...] * factor).astype(HALF)
    dvalue[0] = sum_value[...].astype(HALF)


def attention_back_call(query, key, value, grad, lse, after=()):
    heads, rows, _ = query.shape
    block = pl.BlockSpec((1, rows, HEAD_DIM), lambda h: (h, 0, 0))
    line = pl.BlockSpec((1, 1, rows), lambda h: (h, 0, 0))
    *found, DONE["attention_back"] = pl.pallas_call(
        attention_back_kernel,
        grid=(heads,),
        in_specs=[block] * 4 + [line] + [pl.BlockSpec(memory_space=pl.ANY)] * len(after),
        out_specs=[block] * 3 + [pl.BlockSpec(MARK, lambda h: (0, 0))],
        out_shape=[jax.ShapeDtypeStruct(query.shape, HALF)] * 3
        + [jax.ShapeDtypeStruct(MARK, WIDE)],
        scratch_shapes=[pltpu.VMEM((rows, HEAD_DIM), WIDE)] * 2,
        compiler_params=pltpu.CompilerParams(
            dimension_semantics=("arbitrary",), vmem_limit_bytes=VMEM_BYTES
        ),
        cost_estimate=cost(TAKES["attention_back"]),
        name="attention_back",
    )(query, key, value, grad, lse, *after)
    return found


def out_body(toks, consts, weights, outs, sums):
    (context,), (weight,) = toks, weights
    part, low, context_t = outs
    heads = joined(context)
    context_t[...] = heads.astype(WIDE).T.astype(HALF)
    found = dot(heads, weight.ready()[...])
    part[...] = found
    low[...] = found.astype(HALF)


def feed_body(toks, consts, weights, outs, sums):
    x, part, other = toks
    gate_one, shift, scale, out_bias, up_bias = consts
    up, down = weights
    mixed, hidden_t, upper, act_t, feed, feed_low = outs
    attended = part[...] + other[...].astype(WIDE) + out_bias[...]
    mix = x[...].astype(WIDE) + gate_one[...] * attended
    mixed[...] = mix
    norm, _ = normed(mix)
    hidden = norm * (1.0 + scale[...]) + shift[...]
    low = hidden.astype(HALF)
    hidden_t[...] = hidden.T.astype(HALF)
    up_store = up.ready()
    acc = None
    for k, (start, size) in enumerate(spans(up_store.shape[1], 768)):
        at = slice(start, start + size)
        pre = dot(low, up_store[:, at]) + up_bias[:, at]
        upper[:, at] = pre
        act = gelu(pre)
        act_t[at, :] = act.T.astype(HALF)
        if k == 0:
            down_store = down.ready()
        term = dot(act.astype(HALF), down_store[at, :])
        acc = term if acc is None else acc + term
    feed[...] = acc
    feed_low[...] = acc.astype(HALF)


def tap_body(toks, consts, weights, outs, sums):
    mixed, part, other = toks
    gate_two, down_bias, first_bias = consts
    first, second = weights
    block_out, block_t, first_pre, first_t, own, sent = outs
    feed = part[...] + other[...].astype(WIDE) + down_bias[...]
    output = mixed[...] + gate_two[...] * feed
    low = output.astype(HALF)
    block_out[...] = low
    block_t[...] = output.T.astype(HALF)
    pre = dot(low, first.ready()[...]) + first_bias[...]
    first_pre[...] = pre
    act = pre * sigmoid(pre)
    first_t[...] = act.T.astype(HALF)
    act_low = act.astype(HALF)
    store = second.ready()
    half = store.shape[1] // 2
    own[...] = dot(act_low, store[:, :half])
    sent[...] = dot(act_low, store[:, half:]).astype(HALF)


def latent_body(toks, consts, weights, outs, sums):
    (part, other), (bias,), (third,) = toks, consts, weights
    second_pre, second_t, own, low = outs
    pre = part[...] + other[...].astype(WIDE) + bias[...]
    second_pre[...] = pre
    act = pre * sigmoid(pre)
    second_t[...] = act.T.astype(HALF)
    found = dot(act.astype(HALF), third.ready()[...])
    own[...] = found
    low[...] = found.astype(HALF)


def cosine_body(toks, consts, weights, outs, sums):
    part, other, targets, second_pre = toks
    (bias,), (third,) = consts, weights
    dlatent, dsecond = outs
    cos_sum, third_bias_sum, second_bias_sum = sums
    latent = part[...] + other[...].astype(WIDE) + bias[...]
    target = targets[...].astype(WIDE)
    inner = jnp.sum(latent * target, axis=-1, keepdims=True)
    length = jnp.sum(latent * latent, axis=-1, keepdims=True) + EPS_NORM
    inverse = lax.rsqrt(length)
    inverse_target = lax.rsqrt(jnp.sum(target * target, axis=-1, keepdims=True) + EPS_NORM)
    cos = inner * inverse * inverse_target
    cos_sum[...] += jnp.broadcast_to(total(cos), cos_sum.shape)
    low = (-0.5 * (target * (inverse * inverse_target) - latent * (cos / length))).astype(HALF)
    dlatent[...] = low
    third_bias_sum[...] += total(low.astype(WIDE))
    pre_grad = silu_back(second_pre[...], dot_nt(low, third.ready()[...])).astype(HALF)
    dsecond[...] = pre_grad
    second_bias_sum[...] += total(pre_grad.astype(WIDE))


def tap_back_body(toks, consts, weights, outs, sums):
    own, other, first_pre = toks
    second, first = weights
    dfirst, part, low = outs
    (bias_sum,) = sums
    grads = jnp.concatenate([own[...], other[...]], axis=-1)
    pre_grad = silu_back(first_pre[...], dot_nt(grads, second.ready()[...])).astype(HALF)
    dfirst[...] = pre_grad
    bias_sum[...] += total(pre_grad.astype(WIDE))
    found = dot_nt(pre_grad, first.ready()[...])
    part[...] = found
    low[...] = found.astype(HALF)


def feed_back_body(toks, consts, weights, outs, sums):
    cotangent, part, other, feed_part, feed_other, upper = toks
    gate_two, down_bias = consts
    down, up = weights
    doutput, dfeed, dupper, hidden, hidden_low = outs
    gate_sum, down_bias_sum, up_bias_sum = sums
    grad = cotangent[...].astype(WIDE) + part[...] + other[...].astype(WIDE)
    doutput[...] = grad
    feed = feed_part[...] + feed_other[...].astype(WIDE) + down_bias[...]
    gate_sum[...] += total(grad * feed)
    low = (grad * gate_two[...]).astype(HALF)
    dfeed[...] = low
    down_bias_sum[...] += total(low.astype(WIDE))
    down_store = down.ready()
    acc = None
    for k, (start, size) in enumerate(spans(down_store.shape[0], 768)):
        at = slice(start, start + size)
        pre_grad = gelu_back(upper[:, at], dot_nt(low, down_store[at, :])).astype(HALF)
        dupper[:, at] = pre_grad
        up_bias_sum[:, at] += total(pre_grad.astype(WIDE))
        if k == 0:
            up_store = up.ready()
        term = dot_nt(pre_grad, up_store[:, at])
        acc = term if acc is None else acc + term
    hidden[...] = acc
    hidden_low[...] = acc.astype(HALF)


def mix_back_body(toks, consts, weights, outs, sums):
    mixed, doutput, part, other, out_part, out_other = toks
    scale, gate_one, out_bias = consts
    (weight,) = weights
    dmixed, dattended, dcontext = outs
    shift_sum, scale_sum, gate_sum, bias_sum = sums
    grad = part[...] + other[...].astype(WIDE)
    norm, inverse = normed(mixed[...])
    shift_sum[...] += total(grad)
    scale_sum[...] += total(grad * norm)
    mix_grad = doutput[...] + normed_back(norm, inverse, grad * (1.0 + scale[...]))
    dmixed[...] = mix_grad
    attended = out_part[...] + out_other[...].astype(WIDE) + out_bias[...]
    gate_sum[...] += total(mix_grad * attended)
    low = (mix_grad * gate_one[...]).astype(HALF)
    dattended[...] = low
    bias_sum[...] += total(low.astype(WIDE))
    found = dot_nt(low, weight.ready()[...]).astype(HALF)
    for h in range(dcontext.shape[0]):
        dcontext[h] = found[:, h * HEAD_DIM : (h + 1) * HEAD_DIM]


def qkv_back_body(toks, consts, weights, outs, sums):
    (weight,) = weights
    grads, part, low = outs
    (bias_sum,) = sums
    row = jnp.concatenate([joined(ref) for ref in toks], axis=-1)
    grads[...] = row
    bias_sum[...] += total(row.astype(WIDE))
    found = dot_nt(row, weight.ready()[...])
    part[...] = found
    low[...] = found.astype(HALF)


def input_body(toks, consts, weights, outs, sums):
    x, dmixed, part, other = toks
    (scale,) = consts
    (found,) = outs
    shift_sum, scale_sum = sums
    grad = part[...] + other[...].astype(WIDE)
    norm, inverse = normed(x[...].astype(WIDE))
    shift_sum[...] += total(grad)
    scale_sum[...] += total(grad * norm)
    result = dmixed[...] + normed_back(norm, inverse, grad * (1.0 + scale[...]))
    found[...] = result.astype(HALF)


def weight_grad_kernel(plan, size, sides, me_ref, left, *refs):
    count = 2 * len(plan)
    rights, (*outs, mark, hold) = refs[:sides], refs[-2 - count :]
    mark[...] = jnp.zeros_like(mark)

    def emit(found):
        hold[...] = found.astype(hold.dtype)
        for (ranks, row, rows), near, far in zip(plan, outs[::2], outs[1::2]):
            for k, r in enumerate(ranks):
                start = pl.multiple_of((me_ref[0] ^ r) * size + row, math.gcd(size, row or size))
                out = near if k < len(ranks) // 2 else far
                at = k % (len(ranks) // 2) * rows
                out[at : at + rows, :] = hold[pl.ds(start, rows), :].astype(HALF)

    if sides == 1:
        emit(dot(left[...], rights[0][...]))
        return
    is_own = pl.program_id(0) < pl.num_programs(0) // 2

    @pl.when(is_own)
    def _():
        emit(dot(left[...], rights[0][...]))

    @pl.when(jnp.logical_not(is_own))
    def _():
        half = left.shape[1] // 2
        emit(
            dot(left[:, :half], rights[1][half:, :]) + dot(left[:, half:], rights[1][:half, :])
        )


def weight_grad_call(name, me, left, rights, plan, tile, after=()):
    features, rows = left.shape
    columns = rights[0].shape[1]
    sides = len(rights)
    size = features // len(plan[0][0])
    tile = min(tile, columns)
    steps = pl.cdiv(columns, tile)
    hold = HALF if all(row % 16 == 0 and part % 16 == 0 for _, row, part in plan) else WIDE
    assert sides == 1 or columns % tile == 0
    outs = [(part * len(ranks) // 2, sides * columns) for ranks, _, part in plan for _ in range(2)]
    *found, DONE[name] = pl.pallas_call(
        functools.partial(weight_grad_kernel, plan, size, sides),
        grid_spec=pltpu.PrefetchScalarGridSpec(
            num_scalar_prefetch=1,
            grid=(sides * steps,),
            in_specs=[
                pl.BlockSpec((features, rows), lambda n, me_ref: (0, 0)),
                pl.BlockSpec((rows, tile), lambda n, me_ref: (0, jnp.minimum(n, steps - 1))),
                pl.BlockSpec((rows, tile), lambda n, me_ref: (0, jnp.maximum(n - steps, 0))),
            ][: 1 + sides]
            + [pl.BlockSpec(memory_space=pl.ANY)] * len(after),
            out_specs=[pl.BlockSpec((o[0], tile), lambda n, me_ref: (0, n)) for o in outs]
            + [pl.BlockSpec(MARK, lambda n, me_ref: (0, 0))],
            scratch_shapes=[pltpu.VMEM((features, tile), hold)],
        ),
        out_shape=[jax.ShapeDtypeStruct(o, HALF) for o in outs]
        + [jax.ShapeDtypeStruct(MARK, WIDE)],
        compiler_params=pltpu.CompilerParams(
            dimension_semantics=("arbitrary",), vmem_limit_bytes=VMEM_BYTES
        ),
        cost_estimate=cost(TAKES[name]),
        name=name,
    )(me, left, *rights, *after)
    return found


def split_kernel(plan, core_ref, *refs):
    ins, outs = refs[: len(plan)], list(refs[len(plan) :])
    for ref, (kind, groups, chips) in zip(ins, plan):
        if kind == "cast":
            outs.pop(0)[...] = ref[...].astype(HALF)
            continue
        size = ref.shape[1] // (groups * chips * 2)
        pick = lambda odd: jnp.concatenate(
            [ref[:, (2 * k + odd) * size : (2 * k + odd + 1) * size] for k in range(groups * chips)],
            axis=1,
        )
        even, odd = pick(0), pick(1)
        is_even = core_ref[0] == 0
        own = jnp.where(is_even, even, odd).astype(HALF)
        other = jnp.where(is_even, odd, even).astype(HALF)
        if kind == "split":
            outs.pop(0)[...] = own
            outs.pop(0)[...] = other
        else:
            out = outs.pop(0)
            out[:, : own.shape[1]] = own
            out[:, own.shape[1] :] = other


def split_call(name, core, weights, plan):
    outs = []
    for weight, (kind, _, _) in zip(weights, plan):
        size, columns = weight.shape
        if kind == "split":
            outs += [jax.ShapeDtypeStruct((size, columns // 2), HALF)] * 2
        else:
            outs.append(jax.ShapeDtypeStruct((size, columns), HALF))
    return pl.pallas_call(
        functools.partial(split_kernel, plan),
        in_specs=[pl.BlockSpec(memory_space=pltpu.SMEM)]
        + [pl.BlockSpec(memory_space=pltpu.VMEM)] * len(weights),
        out_specs=[pl.BlockSpec(memory_space=pltpu.VMEM)] * len(outs),
        out_shape=outs,
        compiler_params=pltpu.CompilerParams(vmem_limit_bytes=VMEM_BYTES),
        cost_estimate=cost(TAKES[name]),
        name=name,
    )(core, *weights)


def pack_kernel(width, split_count, chips, core_ref, *refs):
    *ins, out = refs
    at = 0
    for k in range(split_count):
        own, other = ins[2 * k], ins[2 * k + 1]
        rows = own.shape[0]
        is_even = core_ref[0] == 0
        for column in range(0, own.shape[1], width):
            mine, came = own[:, column : column + width], other[:, column : column + width]
            out[at : at + rows, :] = jnp.where(is_even, mine, came)
            out[at + rows : at + 2 * rows, :] = jnp.where(is_even, came, mine)
            at += 2 * rows
    for ref in ins[2 * split_count :]:
        rows, columns = ref.shape
        if chips and ref is ins[-1]:
            size = columns // (2 * chips)
            even, odd = (
                jnp.concatenate(
                    [ref[:, (2 * k + o) * size : (2 * k + o + 1) * size] for k in range(chips)],
                    axis=1,
                )
                for o in (0, 1)
            )
            is_even = core_ref[0] == 0
            whole = [jnp.where(is_even, even, odd), jnp.where(is_even, odd, even)]
            found = [v[:, c : c + width] for v in whole for c in range(0, columns // 2, width)]
        else:
            found = [ref[:, c : c + width] for c in range(0, columns, width)]
        for value in found:
            out[at : at + rows, :] = value.astype(HALF)
            at += rows


def pack_call(name, core, width, split, plain, chips=0):
    ins = [a for pair in split for a in pair] + list(plain)
    size = sum(a.size for a in ins) // width
    return pl.pallas_call(
        functools.partial(pack_kernel, width, len(split), chips),
        in_specs=[pl.BlockSpec(memory_space=pltpu.SMEM)]
        + [pl.BlockSpec(memory_space=pltpu.VMEM)] * len(ins),
        out_specs=pl.BlockSpec(memory_space=pltpu.VMEM),
        out_shape=jax.ShapeDtypeStruct((size, width), HALF),
        compiler_params=pltpu.CompilerParams(vmem_limit_bytes=VMEM_BYTES),
        cost_estimate=cost(TAKES[name]),
        name=name,
    )(core, *ins)


def condition_kernel(buckets, labels, times, classes, out, one, two, sems):
    count = out.shape[0]

    def copies(i):
        yield pltpu.make_async_copy(
            times.at[pl.ds(buckets[i], 1), :], one.at[pl.ds(i, 1), :], sems.at[0, i]
        )
        yield pltpu.make_async_copy(
            classes.at[pl.ds(labels[i], 1), :], two.at[pl.ds(i, 1), :], sems.at[1, i]
        )

    for i in range(count):
        for copy in copies(i):
            copy.start()
    for i in range(count):
        for copy in copies(i):
            copy.wait()
    out[...] = one[...] + two[...]


def condition_call(buckets, labels, times, classes):
    shape = (buckets.shape[0], times.shape[1])
    return pl.pallas_call(
        condition_kernel,
        in_specs=[pl.BlockSpec(memory_space=pltpu.SMEM)] * 2
        + [pl.BlockSpec(memory_space=pl.ANY)] * 2,
        out_specs=pl.BlockSpec(memory_space=pltpu.VMEM),
        out_shape=jax.ShapeDtypeStruct(shape, WIDE),
        scratch_shapes=[
            pltpu.VMEM(shape, WIDE),
            pltpu.VMEM(shape, WIDE),
            pltpu.SemaphoreType.DMA((2, shape[0])),
        ],
        cost_estimate=cost(TAKES["condition"]),
        name="condition",
    )(buckets, labels, times, classes)


def join_kernel(groups, chips, core_ref, own, other, out):
    size = own.shape[1] // (groups * chips)
    is_even = core_ref[0] == 0
    even = jnp.where(is_even, own[...], other[...]).astype(WIDE)
    odd = jnp.where(is_even, other[...], own[...]).astype(WIDE)
    parts = []
    for k in range(groups * chips):
        parts += [v[:, k * size : (k + 1) * size] for v in (even, odd)]
    out[...] = jnp.concatenate(parts, axis=1)


def join_call(name, core, own, other, groups, chips):
    rows, columns = own.shape
    return pl.pallas_call(
        functools.partial(join_kernel, groups, chips),
        in_specs=[pl.BlockSpec(memory_space=pltpu.SMEM)]
        + [pl.BlockSpec(memory_space=pltpu.VMEM)] * 2,
        out_specs=pl.BlockSpec(memory_space=pltpu.VMEM),
        out_shape=jax.ShapeDtypeStruct((rows, 2 * columns), WIDE),
        compiler_params=pltpu.CompilerParams(vmem_limit_bytes=VMEM_BYTES),
        cost_estimate=cost(4),
        name=name,
    )(core, own, other)


def last_kernel(value, *refs):
    refs[-1][...] = value[...]


def last_call(value, after):
    return pl.pallas_call(
        last_kernel,
        in_specs=[pl.BlockSpec(memory_space=pltpu.VMEM)]
        + [pl.BlockSpec(memory_space=pl.ANY)] * len(after),
        out_specs=pl.BlockSpec(memory_space=pltpu.VMEM),
        out_shape=jax.ShapeDtypeStruct(value.shape, value.dtype),
        cost_estimate=cost(1),
        name="last",
    )(value, *after)


def shards(
    n_dp,
    n_seq,
    image_tokens,
    cotangent,
    targets,
    bucket,
    labels,
    time_table,
    class_table,
    ada_weight,
    ada_bias,
    qkv_weight,
    qkv_bias,
    out_weight,
    out_bias,
    up_weight,
    up_bias,
    down_weight,
    down_bias,
    tap_first,
    tap_first_bias,
    tap_second,
    tap_second_bias,
    tap_third,
    tap_third_bias,
):
    images, part_rows, width = image_tokens.shape
    chips = n_dp // 2
    bits = chips.bit_length() - 1
    assert 1 << bits == chips and 2 * images == n_seq and n_seq & (n_seq - 1) == 0
    rows = 2 * images * part_rows
    place = lax.axis_index("dp")
    plane = lax.axis_index("seq")
    core, chip = place % 2, place // 2
    first_core = core == 0
    me = chip.astype(jnp.int32).reshape(1)

    def flip_core(array):
        return lax.ppermute(array, "dp", [(i, i ^ 1) for i in range(n_dp)])

    def flip_chip(array, bit):
        return lax.ppermute(array, "dp", [(i, i ^ (2 << bit)) for i in range(n_dp)])

    def flip_plane(array, bit):
        return lax.ppermute(array, "seq", [(i, i ^ (1 << bit)) for i in range(n_seq)])

    spent = []

    def later(array, *done):
        if not done:
            return array
        marks = []
        for item in done:
            item = DONE[item] if isinstance(item, str) else item
            marks.append(item)
        array, *marks = lax.optimization_barrier((array, *marks))
        spent.extend(marks)
        return array

    def pull(have, level, first):
        for r in range(chips):
            if r.bit_count() == level:
                bit = next(
                    b for b in ((first + k) % bits for k in range(bits)) if r >> b & 1
                )
                have[r] = flip_chip(have[r ^ 1 << bit], bit)

    def ranks(first):
        order = [(first + k) % bits for k in range(bits)]
        return sorted(range(chips), key=lambda r: [r >> b & 1 for b in order])

    def scatter_begin(arrays, plan, *done):
        found = []
        for k, (order, _, _) in enumerate(plan):
            first = next(f for f in range(bits) if ranks(f) == order)
            came = flip_chip(arrays[2 * k + 1], first)
            found.append(([arrays[2 * k], later(came, *done)], first))
        sent = []
        for parts, first in found:
            for step in range(1, bits):
                half = parts[0].shape[0] // 2
                far = sum(p[half:].astype(WIDE) for p in parts).astype(HALF)
                came = flip_chip(far, (first + step) % bits)
                parts = [p[:half] for p in parts] + [came]
            sent.append(parts)
        return sent, [parts[1] for parts, _ in found]

    def scatter_end(sent, *done):
        found = [
            sum(p.astype(WIDE) for p in (*parts[:-1], later(parts[-1], *done))).astype(HALF)
            for parts in sent
        ]
        return found[0] if len(found) == 1 else jnp.concatenate(found)

    def halves(size):
        if size % 32:
            return [(ranks(0), 0, size)]
        return [(ranks(0), 0, size // 2), (ranks(1 % bits), size // 2, size // 2)]

    def sum_line(array, *windows):
        extra = n_seq // 4
        for bit in range(extra.bit_length() - 1):
            array = (array.astype(WIDE) + flip_plane(array, bit).astype(WIDE)).astype(HALF)

        def move(what, pairs):
            pairs = [(a * extra + k, b * extra + k) for a, b in pairs for k in range(extra)]
            return lax.ppermute(what, "seq", pairs)

        at = plane // extra
        half = array.shape[0] // 2
        came = later(move(array, [(0, 1), (3, 2)]), *windows)
        array = (array.astype(WIDE) + came.astype(WIDE)).astype(HALF)
        low, high = array[:half], array[half:]
        came = move(jnp.where(at == 1, high, low), [(1, 2), (2, 1)])
        kept = (jnp.where(at == 1, low, high).astype(WIDE) + came.astype(WIDE)).astype(HALF)
        came = move(kept, [(1, 2), (2, 1)])
        array = jnp.where(
            at == 1, jnp.concatenate([kept, came]), jnp.concatenate([came, kept])
        )
        came = move(array, [(1, 0), (2, 3)])
        return jnp.where((at == 1) | (at == 2), array, came)

    def sum_planes(array, seen=None):
        steps = range(n_seq.bit_length() - 1)
        for bit in steps:
            half = array.shape[0] // 2
            low, high = array[:half], array[half:]
            upper = (plane >> bit & 1) == 1
            came = flip_plane(jnp.where(upper, low, high), bit)
            if seen is not None:
                seen.append(came)
            array = (jnp.where(upper, high, low).astype(WIDE) + came.astype(WIDE)).astype(HALF)
        for bit in reversed(steps):
            came = flip_plane(array, bit)
            if seen is not None:
                seen.append(came)
            upper = (plane >> bit & 1) == 1
            array = jnp.where(
                upper, jnp.concatenate([came, array]), jnp.concatenate([array, came])
            )
        return array

    def routes(turn):
        pairs = []
        for at in range(n_dp):
            for z in range(n_seq):
                k = z ^ turn
                goal = (at - at % 2 + k // images, (at % 2) * images + k % images)
                pairs.append((at * n_seq + z, goal[0] * n_seq + goal[1]))
        return pairs

    def to_chip(array, depth, *after):
        half = array.shape[1] // 2
        found = []
        for turn in range(n_seq):
            k = plane ^ turn
            piece = lax.dynamic_slice(
                array, (k % images, (k // images) * half, 0), (1, half, array.shape[2])
            )[0]
            piece = later(piece, *([found[-depth]] if len(found) >= depth else []), *after)
            found.append(lax.ppermute(piece, ("dp", "seq"), routes(turn)))
        return found

    def from_chip(array, depth, windows=((),) * 4):
        half = array.shape[0] // n_seq
        found = []
        for turn in range(n_seq):
            back = [(b, a) for a, b in routes(turn)]
            piece = array[turn * half : (turn + 1) * half]
            piece = later(piece, *([found[-depth]] if len(found) >= depth else []))
            came = lax.ppermute(piece, ("dp", "seq"), back)
            found.append(later(came, *windows[turn % len(windows)]))
        pieces = list(found)
        stacked = jnp.stack(found)
        for bit in range(n_seq.bit_length() - 1):
            pairs = stacked.reshape(-1, 2, 1 << bit, *stacked.shape[1:])
            swapped = jnp.where((plane >> bit & 1) == 1, pairs[:, ::-1], pairs)
            stacked = swapped.reshape(stacked.shape)
        parts = stacked.reshape(2, images, half, array.shape[1])
        return parts.transpose(1, 0, 2, 3).reshape(images, 2 * half, array.shape[1]), pieces

    def by_core(array, groups):
        lead = array.shape[:-1]
        cut = array.reshape(*lead, groups, chips, 2, -1)
        even = cut[..., 0, :].reshape(*lead, -1)
        odd = cut[..., 1, :].reshape(*lead, -1)
        return jnp.where(first_core, even, odd), jnp.where(first_core, odd, even)

    def from_cores(own, other, groups):
        lead = own.shape[:-1]
        even = jnp.where(first_core, own, other).reshape(*lead, groups, chips, 1, -1)
        odd = jnp.where(first_core, other, own).reshape(*lead, groups, chips, 1, -1)
        return jnp.concatenate([even, odd], axis=-2).reshape(*lead, -1)

    def in_order(own, other):
        return jnp.where(
            first_core, jnp.concatenate([own, other]), jnp.concatenate([other, own])
        )

    def spread(array, columns):
        return jnp.concatenate(
            [array[:, k : k + columns] for k in range(0, array.shape[1], columns)]
        )

    def weight_of(groups, columns, height):
        if all(v % 16 == 0 for _, pieces in groups for p in pieces for v in (p[0], p[1], p[4], height)):
            arrays, found = [], []
            for places, pieces in groups:
                numbers = []
                for array, base in places:
                    known = [k for k, seen in enumerate(arrays) if seen is array]
                    numbers.append((known[0] if known else len(arrays), base))
                    if not known:
                        arrays.append(array)
                found.append((numbers, pieces))
            return arrays, (found, True, height, columns)
        blocks = []
        for r in range(chips):
            block = jnp.zeros((height, columns), HALF)
            for places, pieces in groups:
                array, base = places[r]
                for row, rows, column, wide, to_row, to_column in pieces:
                    part = array[base + row : base + row + rows, column : column + wide]
                    block = lax.dynamic_update_slice(block, part, (to_row, to_column))
            blocks.append(block)
        stacked = jnp.take(jnp.stack(blocks), jnp.arange(chips) ^ chip, axis=0)
        stacked = stacked.reshape(-1, columns)
        size = stacked.shape[0]
        return [stacked], ([([(0, 0)], [(0, size, 0, columns, 0, 0)])], False, size, columns)

    def stacked_weight(places, at, width, columns, height):
        pieces = [
            (at + k * height, height, 0, width, 0, k * width) for k in range(columns // width)
        ]
        return weight_of([(places, pieces)], columns, height)

    biases = (
        ada_bias,
        qkv_bias,
        out_bias,
        up_bias,
        down_bias,
        tap_first_bias,
        tap_second_bias,
        tap_third_bias,
    )
    core_at = core.astype(jnp.int32).reshape(1)
    qkv_own, qkv_other = split_call("split_qkv", core_at, [qkv_weight], [("split", 3, chips)])
    qkv_have = {0: in_order(qkv_own, flip_core(qkv_other))}
    pull(qkv_have, 1, 0)
    qkv_near = [qkv_have[1 << b] for b in range(bits)]
    def pull_rest(have, first):
        for level in range(2, bits + 1):
            pull(have, level, first)
        return [have[r] for r in range(chips) if r.bit_count() > 1]

    def pull_parts(have, split):
        places, came = [[None] * chips for _ in range(2)], []
        for k in range(2):
            part = {r: have[r][:split] if k == 0 else have[r][split:] for r in have}
            came.append(pull_rest(part, 1 - k))
            for r in range(chips):
                places[k][r] = (have[r], k * split) if r in have else (part[r], 0)
        return places, came

    qkv_height, qkv_columns = qkv_have[0].shape
    (low_places, high_places), (low_last, high_last) = pull_parts(qkv_have, qkv_height // 2)
    qkv_weights = weight_of(
        [
            (places, [(0, qkv_height // 2, 0, qkv_columns, at, 0)])
            for places, at in ((low_places, 0), (high_places, qkv_height // 2))
        ],
        qkv_columns,
        qkv_height,
    )
    qkv_rest = low_last + high_last
    tokens_pieces = to_chip(image_tokens, 2, qkv_have[0])
    tokens_own = jnp.concatenate(tokens_pieces, axis=0)
    packed = jnp.concatenate(
        [b.astype(HALF).astype(WIDE) for b in biases]
        + [bucket.astype(WIDE), labels.astype(WIDE)]
    )
    everyone = jnp.pad(packed, (0, -packed.shape[0] % 128)).reshape(1, -1)
    everyone = jnp.concatenate([everyone, flip_core(everyone)])
    for bit in range(bits):
        everyone = jnp.concatenate([everyone, flip_chip(everyone, bit)])
    everyone = jnp.concatenate(
        [
            lax.dynamic_slice(everyone, (place ^ d, 0), (1, everyone.shape[1]))
            for d in range(n_dp)
        ]
    )
    full, at = [], 0
    for bias in biases:
        full.append(everyone[:, at : at + bias.shape[0]].reshape(1, -1))
        at += bias.shape[0]
    bucket_all = everyone[:, at : at + images].reshape(-1).astype(jnp.int32)
    labels_all = everyone[:, at + images : at + 2 * images].reshape(-1).astype(jnp.int32)
    ada_bias_full, qkv_bias_full, out_bias_full, up_bias_full = full[:4]
    down_bias_full, first_bias_full, second_bias_full, third_bias_full = full[4:]
    qkv_bias_own = by_core(qkv_bias_full, 3)[0]
    up_bias_own = by_core(up_bias_full, 1)[0]
    first_bias_own = by_core(first_bias_full, 1)[0]
    second_bias_own = by_core(second_bias_full, 1)[0]

    condition = condition_call(bucket_all, labels_all, time_table, class_table)
    shard = ada_weight.shape[0]
    condition_own = lax.dynamic_slice(
        condition, (0, place * shard), (condition.shape[0], shard)
    )
    cond_act, cond_back = jax.vjp(jax.nn.silu, condition_own)
    cond_low = cond_act.astype(HALF)
    cond_plane = lax.dynamic_index_in_dim(
        cond_low.reshape(chips, n_seq, shard), plane, axis=1, keepdims=False
    )
    ada_low = ada_weight.astype(HALF)
    modulation = jnp.dot(cond_plane, ada_low, preferred_element_type=WIDE)
    modulation = later(modulation, *qkv_rest)
    modulation = modulation + flip_core(modulation)
    ranked = [
        lax.dynamic_slice(modulation, (chip ^ r, 0), (1, modulation.shape[1]))
        for r in range(chips)
    ]
    for bit in reversed(range(bits)):
        half = 1 << bit
        came = flip_chip(jnp.concatenate(ranked[half : 2 * half]), bit)
        ranked = [ranked[r] + came[r : r + 1] for r in range(half)]
    modulation = ranked[0] + ada_bias_full
    shift_one, scale_one, gate_one, shift_two, scale_two, gate_two = jnp.split(
        modulation, 6, axis=-1
    )

    up_weight = later(up_weight, qkv_have[0])
    up_own, up_other, first_own, first_other = split_call(
        "split_rest",
        core_at,
        [up_weight, tap_first],
        [("split", 1, chips), ("split", 1, chips)],
    )
    same_core = [[2 * k + c for k in range(chips)] for c in range(2)]


    up_came, first_came = flip_core(up_other), flip_core(first_other)
    wide, narrow = width, math.gcd(tap_second.shape[1], tap_third.shape[1])
    near = pack_call(
        "pack_near", core_at, wide, [(up_own, up_came)], [down_weight, out_weight]
    )
    far = pack_call(
        "pack_far",
        core_at,
        narrow,
        [(first_own, first_came)],
        [tap_third, later(tap_second, qkv_have[1])],
        chips,
    )
    near_have = {0: later(near, modulation)}
    pull(near_have, 1, 0)
    near_own = [near_have[1 << b] for b in range(bits)]

    tile = 256 if rows % 512 == 0 else rows // 2
    heads = HEADS // 2
    tokens = jnp.concatenate([tokens_own, flip_core(tokens_own)])
    head_shape = (heads, rows, HEAD_DIM)
    inner = heads * HEAD_DIM
    hidden_ff = up_weight.shape[1] // 2
    tap_width = tap_first.shape[1] // 2
    tap_out = tap_third.shape[1]

    def flat(columns, dtype):
        return ((rows, columns), dtype, 0)

    def turned(columns):
        return ((columns, rows), HALF, 1)

    call = functools.partial(token_call, rows=rows, tile=tile)
    hidden_one_t, query, key, value = call(
        "qkv",
        qkv_body,
        me,
        [(tokens, False)],
        [shift_one, scale_one, qkv_bias_own],
        [qkv_weights],
        [turned(width)] + [(head_shape, HALF, 1)] * 3,
        [],
    )
    context, lse = attention_call(query, key, value)
    for r in [r for r in near_have if r]:
        near_have[r] = later(near_have[r], "attention")
    far_have = {0: far}
    height, high = 2 * up_own.shape[0], tap_second.shape[0]
    columns, tap_columns = up_own.shape[1], first_own.shape[1]
    cut = height * columns // wide
    (up_places, mixed_places), (up_last, _) = pull_parts(near_have, cut)
    up_weights = stacked_weight(up_places, 0, wide, columns, height)
    down_weights = stacked_weight(mixed_places, 0, wide, wide, down_weight.shape[0])
    out_weights = stacked_weight(
        mixed_places, down_weight.shape[0], wide, wide, out_weight.shape[0]
    )
    for bit in range(bits):
        far_have[1 << bit] = flip_chip(later(far, *near_own), bit)
    cut = height * tap_columns // narrow + high * tap_third.shape[1] // narrow
    (first_places, second_places), _ = pull_parts(far_have, cut)
    first_weights = stacked_weight(first_places, 0, narrow, tap_columns, height)
    third_weights = stacked_weight(
        first_places, height * tap_columns // narrow, narrow, tap_third.shape[1], high
    )
    second_weights = stacked_weight(second_places, 0, narrow, tap_second.shape[1], high)

    beside_pieces = to_chip(
        later(jnp.concatenate([cotangent, targets], axis=2), "qkv"), 1
    )
    beside = jnp.concatenate(beside_pieces)
    out_part, out_low, context_t = call(
        "out",
        out_body,
        me,
        [(context, False)],
        [],
        [out_weights],
        [flat(width, WIDE), flat(width, HALF), turned(inner)],
        [],
        after=[*up_last, far, beside_pieces[1]],
    )
    out_came = flip_core(out_low)
    mixed, hidden_two_t, upper, act_t, feed_part, feed_low = call(
        "feed",
        feed_body,
        me,
        [(tokens, False), (out_part, False), (out_came, True)],
        [gate_one, shift_two, scale_two, out_bias_full, up_bias_own],
        [up_weights, down_weights],
        [
            flat(width, WIDE),
            turned(width),
            flat(hidden_ff, WIDE),
            turned(hidden_ff),
            flat(width, WIDE),
            flat(width, HALF),
        ],
        [],
        after=[beside, *[far_have[1 << b] for b in range(bits)]],
    )
    feed_came = flip_core(feed_low)
    beside_all = jnp.concatenate([beside, flip_core(beside)])
    cotangent_all, targets_all = beside_all[:, :width], beside_all[:, width:]
    block_out, block_t, first_pre, first_t, second_part, second_low = call(
        "tap",
        tap_body,
        me,
        [(mixed, False), (feed_part, False), (feed_came, True)],
        [gate_two, down_bias_full, first_bias_own],
        [first_weights, second_weights],
        [
            flat(width, HALF),
            turned(width),
            flat(tap_width, WIDE),
            turned(tap_width),
            flat(tap_width, WIDE),
            flat(tap_width, HALF),
        ],
        [],
    )
    second_came = flip_core(second_low)
    second_pre, second_t, latent_part, latent_low = call(
        "latent",
        latent_body,
        me,
        [(second_part, False), (second_came, True)],
        [second_bias_own],
        [third_weights],
        [flat(tap_width, WIDE), turned(tap_width), flat(tap_out, WIDE), flat(tap_out, HALF)],
        [],
    )
    latent_came = flip_core(latent_low)

    dlatent, dsecond, cos_sum, third_bg, second_bg = call(
        "cosine",
        cosine_body,
        me,
        [(latent_part, False), (latent_came, True), (targets_all, False), (second_pre, False)],
        [third_bias_full],
        [third_weights],
        [flat(tap_out, HALF), flat(tap_width, HALF)],
        [(1, 128), (1, tap_out), (1, tap_width)],
    )
    dsecond_came = flip_core(dsecond)
    third_plan = [(ranks(1 % bits), 0, tap_third.shape[0])]
    third_wg = weight_grad_call("third_grad", me, second_t, [dlatent], third_plan, 384)
    second_plan = [(ranks(0), 0, tap_second.shape[0])]
    second_wg = weight_grad_call(
        "second_grad", me, first_t, [dsecond, dsecond_came], second_plan, 512, after=third_wg[:1]
    )
    dfirst, tap_part, tap_low, first_bg = call(
        "tap_back",
        tap_back_body,
        me,
        [(dsecond, False), (dsecond_came, True), (first_pre, False)],
        [],
        [second_weights, first_weights],
        [flat(tap_width, HALF), flat(width, WIDE), flat(width, HALF)],
        [(1, tap_width)],
        after=[second_wg[0]],
    )
    tap_came = flip_core(tap_low)
    block_output, block_pieces = from_chip(
        block_out[: rows // 2], 2, (("cosine",), ("cosine",), ("tap_back",), ("tap_back",))
    )
    third_sent, third_far = scatter_begin(third_wg, third_plan, "tap_back")
    first_plan = [(ranks(1 % bits), 0, height)]
    first_wg = weight_grad_call(
        "first_grad", me, block_t, [dfirst], first_plan, 512, after=third_far + block_pieces[:2]
    )
    doutput, dfeed, dupper, hidden_part, hidden_low, gate_two_grad, down_bg, up_bg = call(
        "feed_back",
        feed_back_body,
        me,
        [
            (cotangent_all, False),
            (tap_part, False),
            (tap_came, True),
            (feed_part, False),
            (feed_came, True),
            (upper, False),
        ],
        [gate_two, down_bias_full],
        [down_weights, up_weights],
        [
            flat(width, WIDE),
            flat(width, HALF),
            flat(hidden_ff, HALF),
            flat(width, WIDE),
            flat(width, HALF),
        ],
        [(1, width), (1, width), (1, hidden_ff)],
        after=[first_wg[0], *block_pieces],
    )

    second_sent, second_far = scatter_begin(second_wg, second_plan, "feed_back")
    first_sent, first_far = scatter_begin(first_wg, first_plan, "feed_back")
    third_part = scatter_end(third_sent, "feed_back")
    hidden_came = flip_core(hidden_low)
    down_plan = halves(down_weight.shape[0])
    down_wg = weight_grad_call(
        "down_grad", me, act_t, [dfeed], down_plan, 384, after=first_far
    )
    up_plan = halves(height)
    up_wg = weight_grad_call(
        "up_grad", me, hidden_two_t, [dupper], up_plan, 384, after=[down_wg[0], *second_far]
    )
    first_sum = scatter_end(first_sent, "up_grad")
    second_sum = scatter_end(second_sent, "up_grad")
    third_part = lax.psum(third_part, "seq")
    first_sum = lax.psum(later(first_sum, third_part), "seq")
    (
        dmixed,
        dattended,
        dcontext,
        shift_two_grad,
        scale_two_grad,
        gate_one_grad,
        out_bg,
    ) = call(
        "mix_back",
        mix_back_body,
        me,
        [
            (mixed, False),
            (doutput, False),
            (hidden_part, False),
            (hidden_came, True),
            (out_part, False),
            (out_came, True),
        ],
        [scale_two, gate_one, out_bias_full],
        [out_weights],
        [flat(width, WIDE), flat(width, HALF), (head_shape, HALF, 1)],
        [(1, width)] * 4,
        after=[up_wg[0], third_part],
    )
    down_sent, down_far = scatter_begin(down_wg, down_plan, "mix_back")
    out_plan = [(ranks(0), 0, out_weight.shape[0])]
    out_wg = weight_grad_call(
        "out_grad", me, context_t, [dattended], out_plan, 384
    )
    dquery, dkey, dvalue = attention_back_call(
        query, key, value, dcontext, lse, after=[out_wg[0], *[parts[-1] for parts in down_sent]]
    )
    second_sum = lax.psum(later(second_sum, first_sum, "out_grad"), "seq")
    up_sent, up_far = scatter_begin(up_wg, up_plan, "attention_back")
    dqkv, one_part, one_low, qkv_bg = call(
        "qkv_back",
        qkv_back_body,
        me,
        [(dquery, False), (dkey, False), (dvalue, False)],
        [],
        [qkv_weights],
        [flat(3 * inner, HALF), flat(width, WIDE), flat(width, HALF)],
        [(1, 3 * inner)],
        after=[first_sum, *up_far],
    )
    one_came = flip_core(one_low[rows // 2 :])
    qkv_plan = halves(qkv_have[0].shape[0])
    out_sent, out_far = scatter_begin(out_wg, out_plan, "qkv_back")
    qkv_wg = weight_grad_call(
        "qkv_grad", me, hidden_one_t, [dqkv], qkv_plan, 384
    )
    up_part = scatter_end(up_sent, "qkv_grad")
    out_part = scatter_end(out_sent, "qkv_grad")
    down_part = scatter_end(down_sent, "attention_back")
    down_part = lax.psum(later(down_part, second_sum), "seq")
    up_part, out_part = lax.psum((later(up_part, down_part), out_part), "seq")
    input_low, shift_one_grad, scale_one_grad = token_call(
        "input_grad",
        input_body,
        me,
        [(tokens, False), (dmixed, False), (one_part, False), (one_came, False)],
        [scale_one],
        [],
        [((rows // 2, width), HALF, 0)],
        [(1, width)] * 2,
        rows=rows // 2,
        tile=tile,
        after=[qkv_wg[0], second_sum, *out_far],
    )
    input_grad = from_chip(input_low, 2)[0].astype(WIDE)

    qkv_sent, qkv_far = scatter_begin(qkv_wg, qkv_plan, "input_grad")
    qkv_scattered = scatter_end(qkv_sent)
    qkv_hops = []
    qkv_part = sum_planes(qkv_scattered, qkv_hops)
    one_grads = jnp.concatenate([shift_one_grad, scale_one_grad], axis=1)
    one_grads = later(one_grads + flip_core(one_grads), *qkv_far)
    modulation_grad = jnp.concatenate(
        [one_grads, gate_one_grad, shift_two_grad, scale_two_grad, gate_two_grad], axis=1
    )
    for bit in range(bits):
        modulation_grad = jnp.concatenate([modulation_grad, flip_chip(modulation_grad, bit)])
    for bit in range(n_seq.bit_length() - 1):
        modulation_grad = jnp.concatenate([modulation_grad, flip_plane(modulation_grad, bit)])
    nth = jnp.arange(chips * n_seq)
    picked = ((nth % chips) ^ chip) * n_seq + ((nth // chips) ^ plane)
    pick = (picked[:, None] == jnp.arange(chips * n_seq)[None, :]).astype(WIDE)
    modulation_all = later(jnp.dot(pick.T, modulation_grad, precision=HIGH), qkv_hops[-1])
    ada_wg = jnp.einsum(
        "bi,bj->ij", cond_low.astype(WIDE), modulation_all, precision=HIGH
    )
    ada_size = ada_bias.shape[0]
    ada_bg = lax.dynamic_slice(jnp.sum(modulation_all, axis=0), (place * ada_size,), (ada_size,))
    cond_grad = cond_back(
        jnp.einsum("bj,ij->bi", modulation_all, ada_low.astype(WIDE), precision=HIGH)
    )[0]
    cond_grad = lax.all_gather(cond_grad, "dp", axis=1, tiled=True)
    time_hot = (
        bucket_all[:, None] == jnp.arange(time_table.shape[0], dtype=jnp.int32)[None, :]
    ).astype(WIDE)
    class_hot = (
        labels_all[:, None] == jnp.arange(class_table.shape[0], dtype=jnp.int32)[None, :]
    ).astype(WIDE)
    time_grad = jnp.einsum("bt,bd->td", time_hot, cond_grad, precision=HIGH)
    class_grad = jnp.einsum("bt,bd->td", class_hot, cond_grad, precision=HIGH)

    sums = [qkv_bg, up_bg, first_bg, second_bg, out_bg, down_bg, third_bg, cos_sum]
    line = later(jnp.concatenate(sums, axis=1), *qkv_far)
    for bit in range(bits):
        line = line + flip_chip(line, bit)
    for bit in range(n_seq.bit_length() - 1):
        line = line + flip_plane(line, bit)
    split_at = sum(s.shape[1] for s in sums[:4])
    came = flip_core(line[:, :split_at])
    bias_grads, at = [], 0
    for k, (item, groups) in enumerate(zip(sums[:4], (3, 1, 1, 1))):
        size = item.shape[1]
        bias_grads.append(
            from_cores(line[:, at : at + size], came[:, at : at + size], groups)
        )
        at += size
    for item in sums[4:7]:
        bias_grads.append(line[:, at : at + item.shape[1]])
        at += item.shape[1]
    align_loss = -0.5 * line[:, at : at + 1] / (rows * chips * n_seq)

    def own_part(grad):
        size = grad.shape[1] // n_dp
        return lax.dynamic_slice(grad, (0, place * size), (1, size))[0]

    qkv_bo, up_bo, first_bo, second_bo, out_bo, down_bo, third_bo = map(own_part, bias_grads)

    def whole_columns(grad, groups):
        size = grad.shape[0] // 2
        own = lax.dynamic_slice(grad, (core * size, 0), (size, grad.shape[1]))
        other = lax.dynamic_slice(grad, ((1 - core) * size, 0), (size, grad.shape[1]))
        return join_call("join", core_at, own, flip_core(other), groups, chips)

    block_output = later(block_output, "input_grad")
    third_part, second_sum, first_sum, down_part, up_part, out_part = (
        later(a, "input_grad", qkv_scattered)
        for a in (third_part, second_sum, first_sum, down_part, up_part, out_part)
    )
    third_own = third_part.astype(WIDE)
    second_own = join_call(
        "join", core_at, second_sum[:, :tap_width], second_sum[:, tap_width:], 1, chips
    )
    first_own = whole_columns(first_sum, 1)
    down_own = down_part.astype(WIDE)
    up_own = whole_columns(up_part, 1)
    out_own = out_part.astype(WIDE)
    qkv_own = whole_columns(qkv_part, 3)
    align_loss = last_call(align_loss, spent)[0, 0]
    return (
        block_output,
        input_grad,
        align_loss,
        time_grad,
        class_grad,
        ada_wg,
        ada_bg,
        qkv_own,
        qkv_bo,
        out_own,
        out_bo,
        up_own,
        up_bo,
        down_own,
        down_bo,
        first_own,
        first_bo,
        second_own,
        second_bo,
        third_own,
        third_bo,
    )


def solution(mesh):
    tokens, rows, line = P("dp", "seq", None), P("dp", None), P("dp")
    return jax.shard_map(
        functools.partial(shards, mesh.shape["dp"], mesh.shape["seq"]),
        mesh=mesh,
        in_specs=(tokens, tokens, tokens, line, line, P(), P()) + (rows, line) * 8,
        out_specs=(tokens, tokens, P(), P(), P()) + (rows, line) * 8,
        check_vma=False,
    )
```

time: 1870 us -> 893 us (0.48)
  waiting for transfers between devices: 1010 us -> 271 us
  blocking collectives: 333 us -> 14.7 us
  matrix products: 336 us -> 18.5 us
  Pallas kernels: 0 us -> 312 us
  starting transfers between devices: 2.01 us -> 119 us
  other arithmetic: 102 us -> 58.6 us
  local copies, waits for them, and re-layouts: 47.1 us -> 70 us
    reduce_scatter x10 -> x0, waiting for transfers between devices: 584 us -> none  [the longest x1 117 us: shards(): lax.psum_scatter(ada_wg.astype(jnp.bfloat16), 'dp', scatter_dimension=0,...]
    all_gather x10 -> x0, waiting for transfers between devices: 427 us -> none  [the longest x1 60.3 us: shards(): lax.all_gather(up_weight.astype(half), 'dp', axis=0, tiled=True)]
    dot_general x34 -> x6, matrix products: 336 us -> 18.5 us  [the longest x1 4.43 us: shards(): time_grad = jnp.einsum('bt,bd->td', time_hot, cond_grad, precision=HIGH)]
    pallas_call x0 -> x30, Pallas kernels: none -> 312 us  [the longest x11 163 us: token_call(): pl.pallas_call(functools.partial(token_kernel, body, counts, [how for _,...]
    ppermute x0 -> x84, waiting for transfers between devices: none -> 263 us  [the longest x40 119 us: flip_chip(): return lax.ppermute(array, 'dp', [(i, i ^ 2 << bit) for i in range(n_dp)])]
    all_gather x5 -> x1, blocking collectives: 225 us -> 14.7 us  [shards(): cond_grad = lax.all_gather(cond_grad, 'dp', axis=1, tiled=True)]
    ppermute x0 -> x84, starting transfers between devices: none -> 118 us  [the longest x20 34.2 us: flip_core(): return lax.ppermute(array, 'dp', [(i, i ^ 1) for i in range(n_dp)])]
    unnamed x3 -> x0, blocking collectives: 95.2 us -> none
  transfers between devices with their start and end apart: 21 -> 89, of which waited for: 19 -> 33; matrix products, arithmetic and copies ran while one was open for 19% -> 15% of each run, Pallas kernels for 0% -> 28%
where the time goes in v1:
time: 893 us; the launch traced here: 880 us
  Pallas kernels  312 us (35%)
  waiting for transfers between devices  271 us (30%)
  starting transfers between devices  119 us (13%)
  local copies, waits for them, and re-layouts  70 us (8%)
  other arithmetic  58.6 us (7%)
  matrix products  18.5 us (2%)
  between operations  16.2 us (2%)
  blocking collectives  14.7 us (2%)
    pallas_call x11, Pallas kernels, token_call(): pl.pallas_call(functools.partial(token_kernel, body, counts, [how for _,...  163 us
    ppermute x40, waiting for transfers between devices, flip_chip(): return lax.ppermute(array, 'dp', [(i, i ^ 2 << bit) for i in range(n_dp)])  119 us
    ppermute x8, waiting for transfers between devices, flip_plane(): return lax.ppermute(array, 'seq', [(i, i ^ 1 << bit) for i in range(n_seq)])  94.4 us
    pallas_call x7, Pallas kernels, weight_grad_call(): pl.pallas_call(functools.partial(weight_grad_kernel, plan, size, sides),...  59.9 us
    ppermute x20, starting transfers between devices, flip_core(): return lax.ppermute(array, 'dp', [(i, i ^ 1) for i in range(n_dp)])  34.2 us
    ppermute x8, waiting for transfers between devices, to_chip(): found.append(lax.ppermute(piece, ('dp', 'seq'), routes(turn)))  33.2 us
    ppermute x8, starting transfers between devices, to_chip(): found.append(lax.ppermute(piece, ('dp', 'seq'), routes(turn)))  32.9 us
    ppermute x40, starting transfers between devices, flip_chip(): return lax.ppermute(array, 'dp', [(i, i ^ 2 << bit) for i in range(n_dp)])  32.8 us
  transfers between devices with their start and end apart: 89, of which 33 were waited for; matrix products, arithmetic and copies ran while one was open for 15% of the time, Pallas kernels for 28%

profile of v1, /device:TPU:1, one launch (start us, length us, event | category | flops | bytes accessed | tf_op | source)
XLA Modules:
  0.0 880.1 jit_solution(15233578285676375325)
XLA Ops:
  85.8 13.4 %qkv.1 = (bf16[1152,1024]{1,0:T(8,128)(2,1)}, bf16[8,1024,72]{2,1,0:T(8,128)(2,1)}, bf16[8,1024,72]{2,1,0:T(8,128)(2,1)}, bf16[8,1024,72]{2,1,0:T(8,128)(2,1)}, f32[8,128]{1,0:T(8,128)}) custom-call(s32[1]{0:T(128)} %bitcast.me_ref, bf16[1024,1152]{1,0:T(8,128)(2,1)} %constant_dynamic-update-slice_fusion.refs_0_, f32[1,1152]{1,0:T(1,128)} %get-tuple-element.529.refs_1_, ...), custom_call_target="tpu_custom_call" | custom-call | flops 14949999616 | bytes 46800000 | tf_op jit(solution)/shard_map/qkv/pallas_call | solution.py:218
  99.2 29.7 %attention.1 = (bf16[8,1024,72]{2,1,0:T(8,128)(2,1)}, f32[8,1,1024]{2,1,0:T(1,128)}, f32[8,128]{1,0:T(8,128)}) custom-call(bf16[8,1024,72]{2,1,0:T(8,128)(2,1)} %get-tuple-element.248.query, bf16[8,1024,72]{2,1,0:T(8,128)(2,1)} %get-tuple-element.249.key, bf16[8,1024,72]{2,1,0:T(8,128)(2,1)} %get-tuple-element.250.value), custom_call_target="tpu_custom_call" | custom-call | flops 34500001792 | bytes 108000000 | tf_op jit(solution)/shard_map/attention/pallas_call | solution.py:278
  128.9 18.4 %collective-permute-done.18.refs_3_.refs_10_.refs_14_.refs_11_.refs_16_ = bf16[1296,1152]{1,0:T(8,128)(2,1)S(1)} collective-permute-done((bf16[1296,1152]{1,0:T(8,128)(2,1)}, bf16[1296,1152]{1,0:T(8,128)(2,1)S(1)}, u32[]{:S(2)}, u32[]{:S(2)}) %collective-permute-start.18) | collective-permute-done | bytes 2986016 | tf_op jit(solution)/shard_map/ppermute | solution.py:809
  159.0 10.5 %collective-permute-done.22.refs_18_ = bf16[128,1920]{1,0:T(8,128)(2,1)S(1)} collective-permute-done((bf16[128,1920]{1,0:T(8,128)(2,1)S(1)}, bf16[128,1920]{1,0:T(8,128)(2,1)S(1)}, u32[]{:S(2)}, u32[]{:S(2)}) %collective-permute-start.22) | collective-permute-done | bytes 491552 | tf_op jit(solution)/shard_map/ppermute | solution.py:928
  225.9 14.8 %collective-permute-done.28.refs_18_.refs_8_.refs_12_.refs_5_.refs_7_.refs_9_ = bf16[3968,256]{1,0:T(8,128)(2,1)S(1)} collective-permute-done((bf16[3968,256]{1,0:T(8,128)(2,1)}, bf16[3968,256]{1,0:T(8,128)(2,1)S(1)}, u32[]{:S(2)}, u32[]{:S(2)}) %collective-permute-start.28) | collective-permute-done | bytes 2031648 | tf_op jit(solution)/shard_map/ppermute | solution.py:809
  242.0 26.9 %feed.1 = (f32[1024,1152]{1,0:T(8,128)}, bf16[1152,1024]{1,0:T(8,128)(2,1)}, f32[1024,2304]{1,0:T(8,128)}, bf16[2304,1024]{1,0:T(8,128)(2,1)}, f32[1024,1152]{1,...) custom-call(s32[1]{0:T(128)} %bitcast.me_ref, bf16[1024,1152]{1,0:T(8,128)(2,1)} %constant_dynamic-update-slice_fusion.refs_0_, ...), custom_call_target="tpu_custom_call" | custom-call | flops 31050000384 | bytes 97200000 | tf_op jit(solution)/shard_map/feed/pallas_call | solution.py:218
  276.6 20.1 %collective-permute-done.30.refs_9_.refs_6_.refs_8_.refs_10_ = bf16[1920,256]{1,0:T(8,128)(2,1)} collective-permute-done((bf16[1920,256]{1,0:T(8,128)(2,1)S(1)}, bf16[1920,256]{1,0:T(8,128)(2,1)}, u32[]{:S(2)}, u32[]{:S(2)}) %collective-permute-start.30) | collective-permute-done | bytes 983072 | tf_op jit(solution)/shard_map/ppermute | solution.py:809
  297.6 17.1 %tap.1 = (bf16[1024,1152]{1,0:T(8,128)(2,1)}, bf16[1152,1024]{1,0:T(8,128)(2,1)}, f32[1024,1024]{1,0:T(8,128)}, bf16[1024,1024]{1,0:T(8,128)(2,1)}, f32[1024,102...) custom-call(s32[1]{0:T(128)} %bitcast.me_ref, f32[1024,1152]{1,0:T(8,128)} %get-tuple-element.270.refs_0_, ...), custom_call_target="tpu_custom_call" | custom-call | flops 18400000000 | bytes 57600000 | tf_op jit(solution)/shard_map/tap/pallas_call | solution.py:218
  382.5 16.6 %tap_back.1 = (bf16[1024,1024]{1,0:T(8,128)(2,1)}, f32[1024,1152]{1,0:T(8,128)}, bf16[1024,1152]{1,0:T(8,128)(2,1)}, f32[1,1024]{1,0:T(1,128)}, f32[8,128]{1,0:T(8,128)}) custom-call(s32[1]{0:T(128)} %bitcast.me_ref, bf16[1024,1024]{1,0:T(8,128)(2,1)} %get-tuple-element.283.refs_0_, bf16[1024,1024]{1,0:T(8,128)(2,1)} %collective-permute-done.38.refs_1_, ...), custom_call_target="tpu_custom_call" | custom-call | flops 18400000000 | bytes 57600000 | tf_op jit(solution)/shard_map/tap_back/pallas_call | solution.py:218
  414.6 28.7 %feed_back.1 = (f32[1024,1152]{1,0:T(8,128)}, bf16[1024,1152]{1,0:T(8,128)(2,1)}, bf16[1024,2304]{1,0:T(8,128)(2,1)}, f32[1024,1152]{1,0:T(8,128)}, bf16[1024,11...) custom-call(s32[1]{0:T(128)} %bitcast.me_ref, ...), custom_call_target="tpu_custom_call" | custom-call | flops 32199999488 | bytes 100800000 | tf_op jit(solution)/shard_map/feed_back/pallas_call | solution.py:218
  443.3 15.3 %collective-permute-done.44.refs_2_ = bf16[512,2048]{1,0:T(8,128)(2,1)} collective-permute-done((bf16[512,2048]{1,0:T(8,128)(2,1)}, bf16[512,2048]{1,0:T(8,128)(2,1)}, u32[]{:S(2)}, u32[]{:S(2)}) %collective-permute-start.44) | collective-permute-done | bytes 2097184 | tf_op jit(solution)/shard_map/ppermute | solution.py:809
  468.1 12.1 %down_grad.1 = (bf16[576,1152]{1,0:T(8,128)(2,1)}, bf16[576,1152]{1,0:T(8,128)(2,1)}, bf16[576,1152]{1,0:T(8,128)(2,1)}, bf16[576,1152]{1,0:T(8,128)(2,1)}, f32[8,128]{1,0:T(8,128)}) custom-call(s32[1]{0:T(128)} %bitcast.me_ref, bf16[2304,1024]{1,0:T(8,128)(2,1)} %get-tuple-element.307.left, bf16[1024,1152]{1,0:T(8,128)(2,1)} %get-tuple-element.308.refs_0_, ...), custom_call_target="tpu_custom_call" | custom-call | flops 13799999488 | bytes 43200000 | tf_op jit(solution)/shard_map/down_grad/pallas_call | solution.py:570
  481.2 11.9 %up_grad.1 = (bf16[288,2304]{1,0:T(8,128)(2,1)}, bf16[288,2304]{1,0:T(8,128)(2,1)}, bf16[288,2304]{1,0:T(8,128)(2,1)}, bf16[288,2304]{1,0:T(8,128)(2,1)}, f32[8,128]{1,0:T(8,128)}) custom-call(s32[1]{0:T(128)} %bitcast.me_ref, bf16[1152,1024]{1,0:T(8,128)(2,1)} %get-tuple-element.305.left, bf16[1024,2304]{1,0:T(8,128)(2,1)} %get-tuple-element.306.refs_0_, ...), custom_call_target="tpu_custom_call" | custom-call | flops 13799999488 | bytes 43200000 | tf_op jit(solution)/shard_map/up_grad/pallas_call | solution.py:570
  497.4 14.7 %mix_back.1 = (f32[1024,1152]{1,0:T(8,128)}, bf16[1024,1152]{1,0:T(8,128)(2,1)}, bf16[8,1024,72]{2,1,0:T(8,128)(2,1)}, f32[1,1152]{1,0:T(1,128)}, f32[1,1152]{1,...) custom-call(s32[1]{0:T(128)} %bitcast.me_ref, f32[1024,1152]{1,0:T(8,128)} %get-tuple-element.270.refs_0_, ...), custom_call_target="tpu_custom_call" | custom-call | flops 16099999744 | bytes 50400000 | tf_op jit(solution)/shard_map/mix_back/pallas_call | solution.py:218
  539.1 14.8 %collective-permute-done.49.refs_2_ = bf16[288,1152]{1,0:T(8,128)(2,1)} collective-permute-done((bf16[288,1152]{1,0:T(8,128)(2,1)}, bf16[288,1152]{1,0:T(8,128)(2,1)}, u32[]{:S(2)}, u32[]{:S(2)}) %collective-permute-start.49) | collective-permute-done | bytes 663584 | tf_op jit(solution)/shard_map/ppermute | solution.py:809
  558.6 31.1 %attention_back.1 = (bf16[8,1024,72]{2,1,0:T(8,128)(2,1)}, bf16[8,1024,72]{2,1,0:T(8,128)(2,1)}, bf16[8,1024,72]{2,1,0:T(8,128)(2,1)}, f32[8,128]{1,0:T(8,128)}) custom-call(bf16[8,1024,72]{2,1,0:T(8,128)(2,1)} %get-tuple-element.248.query, bf16[8,1024,72]{2,1,0:T(8,128)(2,1)} %get-tuple-element.249.key, bf16[8,1024,72]{2,1,0:T(8,128)(2,1)} %get-tuple-element.250.value, ...), custom_call_target="tpu_custom_call" | custom-call | flops 35649998848 | bytes 111600000 | tf_op jit(solution)/shard_map/attention_back/pallas_call | solution.py:331
  596.3 12.6 %qkv_back.1 = (bf16[1024,1728]{1,0:T(8,128)(2,1)}, f32[1024,1152]{1,0:T(8,128)}, bf16[1024,1152]{1,0:T(8,128)(2,1)}, f32[1,1728]{1,0:T(1,128)}, f32[8,128]{1,0:T(8,128)}) custom-call(s32[1]{0:T(128)} %bitcast.me_ref, bf16[8,1024,72]{2,1,0:T(8,128)(2,1)} %get-tuple-element.329.refs_0_, bf16[8,1024,72]{2,1,0:T(8,128)(2,1)} %get-tuple-element.330.refs_1_, ...), custom_call_target="tpu_custom_call" | custom-call | flops 13799999488 | bytes 43200000 | tf_op jit(solution)/shard_map/qkv_back/pallas_call | solution.py:218
  617.2 10.4 %qkv_grad.1 = (bf16[288,1728]{1,0:T(8,128)(2,1)}, bf16[288,1728]{1,0:T(8,128)(2,1)}, bf16[288,1728]{1,0:T(8,128)(2,1)}, bf16[288,1728]{1,0:T(8,128)(2,1)}, f32[8,128]{1,0:T(8,128)}) custom-call(s32[1]{0:T(128)} %bitcast.me_ref, bf16[1152,1024]{1,0:T(8,128)(2,1)} %get-tuple-element.342.left, bf16[1024,1728]{1,0:T(8,128)(2,1)} %get-tuple-element.343.refs_0_), custom_call_target="tpu_custom_call" | custom-call | flops 11500000256 | bytes 36000000 | tf_op jit(solution)/shard_map/qkv_grad/pallas_call | solution.py:570
  665.0 12.3 %collective-permute-done.63 = f32[1,9280]{1,0:T(1,128)S(1)} collective-permute-done((f32[1,9280]{1,0:T(1,128)S(1)}, f32[1,9280]{1,0:T(1,128)S(1)}, u32[]{:S(2)}, u32[]{:S(2)}) %collective-permute-start.63) | collective-permute-done | bytes 37152 | tf_op jit(solution)/shard_map/ppermute | solution.py:809
  724.1 13.2 %collective-permute-done.73 = f32[8,6912]{1,0:T(8,128)} collective-permute-done((f32[8,6912]{1,0:T(8,128)S(1)}, f32[8,6912]{1,0:T(8,128)}, u32[]{:S(2)}, u32[]{:S(2)}) %collective-permute-start.73) | collective-permute-done | bytes 221216 | tf_op jit(solution)/shard_map/ppermute | solution.py:812
  757.9 27.7 %collective-permute-done.77 = bf16[72,1728]{1,0:T(8,128)(2,1)S(1)} collective-permute-done((bf16[72,1728]{1,0:T(8,128)(2,1)S(1)}, bf16[72,1728]{1,0:T(8,128)(2,1)S(1)}, u32[]{:S(2)}, u32[]{:S(2)}) %collective-permute-start.77) | collective-permute-done | bytes 248864 | tf_op jit(solution)/shard_map/ppermute | solution.py:812
  786.0 21.3 %collective-permute-done.78 = bf16[72,1728]{1,0:T(8,128)(2,1)S(1)} collective-permute-done((bf16[72,1728]{1,0:T(8,128)(2,1)S(1)}, bf16[72,1728]{1,0:T(8,128)(2,1)S(1)}, u32[]{:S(2)}, u32[]{:S(2)}) %collective-permute-start.78) | collective-permute-done | bytes 248864 | tf_op jit(solution)/shard_map/ppermute | solution.py:812
  811.4 19.1 %collective-permute-done.79.refs_54_ = bf16[144,1728]{1,0:T(8,128)(2,1)S(1)} collective-permute-done((bf16[144,1728]{1,0:T(8,128)(2,1)S(1)}, bf16[144,1728]{1,0:T(8,128)(2,1)S(1)}, u32[]{:S(2)}, u32[]{:S(2)}) %collective-permute-start.79) | collective-permute-done | bytes 497696 | tf_op jit(solution)/shard_map/ppermute | solution.py:812
  832.9 14.7 %all-gather = f32[8,144,16]{1,2,0:T(8,128)S(1)} all-gather(f32[1,144,16]{1,2,0:T(8,128)S(1)} %fusion.16), channel_id=1, replica_groups=mesh['dp'=8,'seq'=4] {'dp'}, dimensions={0}, use_global_device_ids=true | all-gather | bytes 82944 | tf_op jit(solution)/shard_map/all_gather | solution.py:1419
  (541 shorter events, 436.4 us)
Async XLA Ops:
  7.2 489.2 %all-reduce.8.cloned.1.call-start = ((), (), s32[]{:S(2)}) async-start(), calls=%async_computation | async-start | bytes 786432 | tf_op jit(solution)/shard_map/psum | solution.py:1319
  82.7 64.7 %collective-permute-start.18 = (bf16[1296,1152]{1,0:T(8,128)(2,1)}, bf16[1296,1152]{1,0:T(8,128)(2,1)S(1)}, u32[]{:S(2)}, u32[]{:S(2)}) collective-permute-start(bf16[1296,1152]{1,0:T(8,128)(2,1)} %pack_near.1.refs_1_.refs_8_.refs_12_.refs_9_), channel_id=1, source_target_pairs={{0,16},{4,20},{8,24},{12,28},{16,0},{20,4},{24,8},{28,12},{1,17},{... | collective-permute-start | bytes 8957960 | tf_op jit(solution)/shard_map/ppermute | solution.py:809
  83.0 65.7 %collective-permute-start.17 = (bf16[1296,1152]{1,0:T(8,128)(2,1)}, bf16[1296,1152]{1,0:T(8,128)(2,1)S(1)}, u32[]{:S(2)}, u32[]{:S(2)}) collective-permute-start(bf16[1296,1152]{1,0:T(8,128)(2,1)} %pack_near.1.refs_1_.refs_8_.refs_12_.refs_9_), channel_id=1, source_target_pairs={{0,8},{4,12},{8,0},{12,4},{16,24},{20,28},{24,16},{28,20},{1,9},{5... | collective-permute-start | bytes 8957960 | tf_op jit(solution)/shard_map/ppermute | solution.py:809
  190.9 50.3 %collective-permute-start.24 = (bf16[1024,1152]{1,0:T(8,128)(2,1)}, bf16[1024,1152]{1,0:T(8,128)(2,1)}, u32[]{:S(2)}, u32[]{:S(2)}) collective-permute-start(bf16[1024,1152]{1,0:T(8,128)(2,1)} %get-tuple-element.266), channel_id=1, source_target_pairs={{0,4},{4,0},{8,12},{12,8},{16,20},{20,16},{24,28},{28,24},{1,5},{5... | collective-permute-start | bytes 7077896 | tf_op jit(solution)/shard_map/ppermute | solution.py:806
  194.6 46.1 %collective-permute-start.28 = (bf16[3968,256]{1,0:T(8,128)(2,1)}, bf16[3968,256]{1,0:T(8,128)(2,1)S(1)}, u32[]{:S(2)}, u32[]{:S(2)}) collective-permute-start(bf16[3968,256]{1,0:T(8,128)(2,1)} %pack_far.1.refs_6_.refs_10_.refs_3_.refs_5_.refs_7_), channel_id=1, source_target_pairs={{0,16},{4,20},{8,24},{12,28},{16,0},{20,4},{24,8},{28,12},{1,17},{... | collective-permute-start | bytes 6094856 | tf_op jit(solution)/shard_map/ppermute | solution.py:809
  195.4 45.8 %collective-permute-start.27 = (bf16[3968,256]{1,0:T(8,128)(2,1)}, bf16[3968,256]{1,0:T(8,128)(2,1)}, u32[]{:S(2)}, u32[]{:S(2)}) collective-permute-start(bf16[3968,256]{1,0:T(8,128)(2,1)} %pack_far.1.refs_6_.refs_10_.refs_3_.refs_5_.refs_7_), channel_id=1, source_target_pairs={{0,8},{4,12},{8,0},{12,4},{16,24},{20,28},{24,16},{28,20},{1,9},{5... | collective-permute-start | bytes 6094856 | tf_op jit(solution)/shard_map/ppermute | solution.py:809
  364.3 38.9 %collective-permute-start.37 = (bf16[128,1152]{1,0:T(8,128)(2,1)S(1)}, bf16[128,1152]{1,0:T(8,128)(2,1)S(1)}, u32[]{:S(2)}, u32[]{:S(2)}) collective-permute-start(bf16[128,1152]{1,0:T(8,128)(2,1)S(1)} %get-tuple-element.282), channel_id=1, source_target_pairs={{4,0},{5,1},{0,2},{1,3},{6,4},{7,5},{2,6},{3,7},{12,8},{13,9},{8,1... | collective-permute-start | bytes 884744 | tf_op jit(solution)/shard_map/ppermute | solution.py:938
  364.3 38.9 %collective-permute-start.39 = (bf16[128,1152]{1,0:T(8,128)(2,1)S(1)}, bf16[128,1152]{1,0:T(8,128)(2,1)S(1)}, u32[]{:S(2)}, u32[]{:S(2)}) collective-permute-start(bf16[128,1152]{1,0:T(8,128)(2,1)S(1)} %get-tuple-element.292), channel_id=1, source_target_pairs={{5,0},{4,1},{1,2},{0,3},{7,4},{6,5},{3,6},{2,7},{13,8},{12,9},{9,1... | collective-permute-start | bytes 884744 | tf_op jit(solution)/shard_map/ppermute | solution.py:938
  403.3 40.0 %collective-permute-start.45 = (bf16[256,768]{1,0:T(8,128)(2,1)S(1)}, bf16[256,768]{1,0:T(8,128)(2,1)S(1)}, u32[]{:S(2)}, u32[]{:S(2)}) collective-permute-start(bf16[256,768]{1,0:T(8,128)(2,1)S(1)} %add_convert_fusion.18), channel_id=1, source_target_pairs={{0,8},{4,12},{8,0},{12,4},{16,24},{20,28},{24,16},{28,20},{1,9},{5... | collective-permute-start | bytes 1179656 | tf_op jit(solution)/shard_map/ppermute | solution.py:809
  411.5 48.0 %collective-permute-start.43 = (bf16[576,1024]{1,0:T(8,128)(2,1)}, bf16[576,1024]{1,0:T(8,128)(2,1)}, u32[]{:S(2)}, u32[]{:S(2)}) collective-permute-start(bf16[576,1024]{1,0:T(8,128)(2,1)} %get-tuple-element.309), channel_id=1, source_target_pairs={{0,16},{4,20},{8,24},{12,28},{16,0},{20,4},{24,8},{28,12},{1,17},{... | collective-permute-start | bytes 3538952 | tf_op jit(solution)/shard_map/ppermute | solution.py:809
  412.1 46.5 %collective-permute-start.44 = (bf16[512,2048]{1,0:T(8,128)(2,1)}, bf16[512,2048]{1,0:T(8,128)(2,1)}, u32[]{:S(2)}, u32[]{:S(2)}) collective-permute-start(bf16[512,2048]{1,0:T(8,128)(2,1)} %get-tuple-element.313), channel_id=1, source_target_pairs={{0,8},{4,12},{8,0},{12,4},{16,24},{20,28},{24,16},{28,20},{1,9},{5... | collective-permute-start | bytes 6291464 | tf_op jit(solution)/shard_map/ppermute | solution.py:809
  459.5 77.8 %all-reduce.10.cloned.1.call-start = ((), (), s32[]{:S(2)}) async-start(), calls=%async_computation.1 | async-start | bytes 1179648 | tf_op jit(solution)/shard_map/psum | solution.py:1320
  493.1 98.4 %collective-permute-start.51 = (bf16[288,2304]{1,0:T(8,128)(2,1)}, bf16[288,2304]{1,0:T(8,128)(2,1)S(1)}, u32[]{:S(2)}, u32[]{:S(2)}) collective-permute-start(bf16[288,2304]{1,0:T(8,128)(2,1)} %get-tuple-element.335), channel_id=1, source_target_pairs={{0,8},{4,12},{8,0},{12,4},{16,24},{20,28},{24,16},{28,20},{1,9},{5... | collective-permute-start | bytes 3981320 | tf_op jit(solution)/shard_map/ppermute | solution.py:809
  496.5 136.5 %all-reduce.12.cloned.1.call-start = ((), (), s32[]{:S(2)}) async-start(), calls=%async_computation.2 | async-start | bytes 2097152 | tf_op jit(solution)/shard_map/psum | solution.py:1355
  496.5 93.2 %collective-permute-start.52 = (bf16[288,2304]{1,0:T(8,128)(2,1)}, bf16[288,2304]{1,0:T(8,128)(2,1)}, u32[]{:S(2)}, u32[]{:S(2)}) collective-permute-start(bf16[288,2304]{1,0:T(8,128)(2,1)} %get-tuple-element.338), channel_id=1, source_target_pairs={{0,16},{4,20},{8,24},{12,28},{16,0},{20,4},{24,8},{28,12},{1,17},{... | collective-permute-start | bytes 3981320 | tf_op jit(solution)/shard_map/ppermute | solution.py:809
  537.4 214.3 %all-reduce.14.cloned.1.call-start = ((), (), s32[]{:S(2)}) async-start(), calls=%async_computation.3 | async-start | bytes 2654208 | tf_op jit(solution)/shard_map/psum | solution.py:1377
  537.8 72.8 %collective-permute-start.55 = (bf16[288,1152]{1,0:T(8,128)(2,1)}, bf16[288,1152]{1,0:T(8,128)(2,1)S(1)}, u32[]{:S(2)}, u32[]{:S(2)}) collective-permute-start(bf16[288,1152]{1,0:T(8,128)(2,1)} %get-tuple-element.348), channel_id=1, source_target_pairs={{0,8},{4,12},{8,0},{12,4},{16,24},{20,28},{24,16},{28,20},{1,9},{5... | collective-permute-start | bytes 1990664 | tf_op jit(solution)/shard_map/ppermute | solution.py:809
  595.4 39.6 %collective-permute-start.66 = (bf16[144,2304]{1,0:T(8,128)(2,1)}, bf16[144,2304]{1,0:T(8,128)(2,1)}, u32[]{:S(2)}, u32[]{:S(2)}) collective-permute-start(bf16[144,2304]{1,0:T(8,128)(2,1)} %add_convert_fusion.7), channel_id=1, source_target_pairs={{0,16},{4,20},{8,24},{12,28},{16,0},{20,4},{24,8},{28,12},{1,17},{... | collective-permute-start | bytes 1990664 | tf_op jit(solution)/shard_map/ppermute | solution.py:809
  633.0 225.1 %all-reduce.16.cloned.1.call-start = ((), (), s32[]{:S(2)}) async-start(), calls=%async_computation.4 | async-start | bytes 3317760 | tf_op jit(solution)/shard_map/psum | solution.py:1378
  657.2 62.8 %collective-permute-start.56 = (bf16[128,1152]{1,0:T(8,128)(2,1)}, bf16[128,1152]{1,0:T(8,128)(2,1)S(1)}, u32[]{:S(2)}, u32[]{:S(2)}) collective-permute-start(bf16[128,1152]{1,0:T(8,128)(2,1)} %get-tuple-element.480), channel_id=1, source_target_pairs={{0,0},{1,1},{4,2},{5,3},{2,4},{3,5},{6,6},{7,7},{8,8},{9,9},{12,10... | collective-permute-start | bytes 884744 | tf_op jit(solution)/shard_map/ppermute | solution.py:938
  660.0 60.0 %collective-permute-start.57 = (bf16[128,1152]{1,0:T(8,128)(2,1)}, bf16[128,1152]{1,0:T(8,128)(2,1)S(1)}, u32[]{:S(2)}, u32[]{:S(2)}) collective-permute-start(bf16[128,1152]{1,0:T(8,128)(2,1)} %get-tuple-element.483), channel_id=1, source_target_pairs={{1,0},{0,1},{5,2},{4,3},{3,4},{2,5},{7,6},{6,7},{9,8},{8,9},{13,10... | collective-permute-start | bytes 884744 | tf_op jit(solution)/shard_map/ppermute | solution.py:938
  662.5 77.9 %collective-permute-start.75 = (bf16[144,1728]{1,0:T(8,128)(2,1)}, bf16[144,1728]{1,0:T(8,128)(2,1)S(1)}, u32[]{:S(2)}, u32[]{:S(2)}) collective-permute-start(bf16[144,1728]{1,0:T(8,128)(2,1)} %add_convert_fusion.14), channel_id=1, source_target_pairs={{0,16},{4,20},{8,24},{12,28},{16,0},{20,4},{24,8},{28,12},{1,17},{... | collective-permute-start | bytes 1493000 | tf_op jit(solution)/shard_map/ppermute | solution.py:809
  682.8 58.4 %collective-permute-start.74 = (bf16[144,1728]{1,0:T(8,128)(2,1)}, bf16[144,1728]{1,0:T(8,128)(2,1)}, u32[]{:S(2)}, u32[]{:S(2)}) collective-permute-start(bf16[144,1728]{1,0:T(8,128)(2,1)} %add_convert_fusion.16), channel_id=1, source_target_pairs={{0,8},{4,12},{8,0},{12,4},{16,24},{20,28},{24,16},{28,20},{1,9},{5... | collective-permute-start | bytes 1493000 | tf_op jit(solution)/shard_map/ppermute | solution.py:809
  745.9 63.2 %collective-permute-start.83 = (bf16[144,1024]{1,0:T(8,128)(2,1)S(1)}, bf16[144,1024]{1,0:T(8,128)(2,1)}, u32[]{:S(2)}, u32[]{:S(2)}) collective-permute-start(bf16[144,1024]{1,0:T(8,128)(2,1)S(1)} %get-tuple-element.492), channel_id=1, source_target_pairs={{0,4},{4,0},{8,12},{12,8},{16,20},{20,16},{24,28},{28,24},{1,5},{5... | collective-permute-start | bytes 884744 | tf_op jit(solution)/shard_map/ppermute | solution.py:806
  (152 other events, 2244.5 us)
Sparse Core Ops, SparseCore 0:
  459.6 35.0 all-reduce.7
  497.2 40.0 all-reduce.9
  539.8 52.1 all-reduce.11
  633.1 66.3 all-reduce.13
  754.8 93.4 all-reduce.15

commit v2 on v1

--- a/solution.py
+++ b/solution.py
@@ -836,11 +836,11 @@
         order = [(first + k) % bits for k in range(bits)]
         return sorted(range(chips), key=lambda r: [r >> b & 1 for b in order])
 
-    def scatter_begin(arrays, plan, *done):
+    def scatter_begin(arrays, plan, *done, under_way=()):
         found = []
         for k, (order, _, _) in enumerate(plan):
             first = next(f for f in range(bits) if ranks(f) == order)
-            came = flip_chip(arrays[2 * k + 1], first)
+            came = under_way[k] if under_way else flip_chip(arrays[2 * k + 1], first)
             found.append(([arrays[2 * k], later(came, *done)], first))
         sent = []
         for parts, first in found:
@@ -887,7 +887,7 @@
         came = move(array, [(1, 0), (2, 3)])
         return jnp.where((at == 1) | (at == 2), array, came)
 
-    def sum_planes(array, seen=None):
+    def sum_planes(array, seen=None, half_way=None):
         steps = range(n_seq.bit_length() - 1)
         for bit in steps:
             half = array.shape[0] // 2
@@ -898,6 +898,8 @@
                 seen.append(came)
             array = (jnp.where(upper, high, low).astype(WIDE) + came.astype(WIDE)).astype(HALF)
         for bit in reversed(steps):
+            if half_way is not None and bit == 0:
+                array = later(array, half_way)
             came = flip_plane(array, bit)
             if seen is not None:
                 seen.append(came)
@@ -1041,12 +1043,8 @@
         qkv_height,
     )
     qkv_rest = low_last + high_last
-    tokens_pieces = to_chip(image_tokens, 2, qkv_have[0])
-    tokens_own = jnp.concatenate(tokens_pieces, axis=0)
-    packed = jnp.concatenate(
-        [b.astype(HALF).astype(WIDE) for b in biases]
-        + [bucket.astype(WIDE), labels.astype(WIDE)]
-    )
+    packed = jnp.concatenate(biases).astype(HALF).astype(WIDE)
+    packed = jnp.concatenate([packed, jnp.concatenate([bucket, labels]).astype(WIDE)])
     everyone = jnp.pad(packed, (0, -packed.shape[0] % 128)).reshape(1, -1)
     everyone = jnp.concatenate([everyone, flip_core(everyone)])
     for bit in range(bits):
@@ -1070,7 +1068,19 @@
     first_bias_own = by_core(first_bias_full, 1)[0]
     second_bias_own = by_core(second_bias_full, 1)[0]
 
-    condition = condition_call(bucket_all, labels_all, time_table, class_table)
+    up_weight = later(up_weight, qkv_have[0])
+    up_own, up_other, first_own, first_other = split_call(
+        "split_rest",
+        core_at,
+        [up_weight, tap_first],
+        [("split", 1, chips), ("split", 1, chips)],
+    )
+    up_came, first_came = flip_core(up_other), flip_core(first_other)
+    wide, narrow = width, math.gcd(tap_second.shape[1], tap_third.shape[1])
+    near = pack_call(
+        "pack_near", core_at, wide, [(up_own, up_came)], [down_weight, out_weight]
+    )
+    condition = condition_call(later(bucket_all, near, *qkv_near), labels_all, time_table, class_table)
     shard = ada_weight.shape[0]
     condition_own = lax.dynamic_slice(
         condition, (0, place * shard), (condition.shape[0], shard)
@@ -1097,21 +1107,9 @@
         modulation, 6, axis=-1
     )
 
-    up_weight = later(up_weight, qkv_have[0])
-    up_own, up_other, first_own, first_other = split_call(
-        "split_rest",
-        core_at,
-        [up_weight, tap_first],
-        [("split", 1, chips), ("split", 1, chips)],
-    )
     same_core = [[2 * k + c for k in range(chips)] for c in range(2)]
 
 
-    up_came, first_came = flip_core(up_other), flip_core(first_other)
-    wide, narrow = width, math.gcd(tap_second.shape[1], tap_third.shape[1])
-    near = pack_call(
-        "pack_near", core_at, wide, [(up_own, up_came)], [down_weight, out_weight]
-    )
     far = pack_call(
         "pack_far",
         core_at,
@@ -1120,7 +1118,9 @@
         [tap_third, later(tap_second, qkv_have[1])],
         chips,
     )
-    near_have = {0: later(near, modulation)}
+    tokens_pieces = to_chip(image_tokens, 1)
+    tokens_own = jnp.concatenate(tokens_pieces, axis=0)
+    near_have = {0: later(near, modulation, *qkv_rest)}
     pull(near_have, 1, 0)
     near_own = [near_have[1 << b] for b in range(bits)]
 
@@ -1140,6 +1140,7 @@
         return ((columns, rows), HALF, 1)
 
     call = functools.partial(token_call, rows=rows, tile=tile)
+    twice = functools.partial(token_call, rows=rows, tile=2 * tile)
     hidden_one_t, query, key, value = call(
         "qkv",
         qkv_body,
@@ -1302,21 +1303,19 @@
         after=[first_wg[0], *block_pieces],
     )
 
-    second_sent, second_far = scatter_begin(second_wg, second_plan, "feed_back")
     first_sent, first_far = scatter_begin(first_wg, first_plan, "feed_back")
-    third_part = scatter_end(third_sent, "feed_back")
+    third_part = lax.psum(scatter_end(third_sent, "first_grad"), "seq")
     hidden_came = flip_core(hidden_low)
     down_plan = halves(down_weight.shape[0])
     down_wg = weight_grad_call(
-        "down_grad", me, act_t, [dfeed], down_plan, 384, after=first_far
-    )
+        "down_grad", me, act_t, [dfeed], down_plan, 256, after=[*first_far, third_part]
+    )
+    second_sent, second_far = scatter_begin(second_wg, second_plan, "down_grad")
     up_plan = halves(height)
     up_wg = weight_grad_call(
-        "up_grad", me, hidden_two_t, [dupper], up_plan, 384, after=[down_wg[0], *second_far]
-    )
-    first_sum = scatter_end(first_sent, "up_grad")
-    second_sum = scatter_end(second_sent, "up_grad")
-    third_part = lax.psum(third_part, "seq")
+        "up_grad", me, hidden_two_t, [dupper], up_plan, 768, after=[down_wg[0], *second_far]
+    )
+    first_sum = scatter_end(first_sent, "down_grad")
     first_sum = lax.psum(later(first_sum, third_part), "seq")
     (
         dmixed,
@@ -1342,7 +1341,7 @@
         [out_weights],
         [flat(width, WIDE), flat(width, HALF), (head_shape, HALF, 1)],
         [(1, width)] * 4,
-        after=[up_wg[0], third_part],
+        after=[up_wg[0]],
     )
     down_sent, down_far = scatter_begin(down_wg, down_plan, "mix_back")
     out_plan = [(ranks(0), 0, out_weight.shape[0])]
@@ -1350,10 +1349,16 @@
         "out_grad", me, context_t, [dattended], out_plan, 384
     )
     dquery, dkey, dvalue = attention_back_call(
-        query, key, value, dcontext, lse, after=[out_wg[0], *[parts[-1] for parts in down_sent]]
-    )
-    second_sum = lax.psum(later(second_sum, first_sum, "out_grad"), "seq")
-    up_sent, up_far = scatter_begin(up_wg, up_plan, "attention_back")
+        query, key, value, dcontext, lse, after=[out_wg[0], first_sum, *[parts[-1] for parts in down_sent]]
+    )
+    second_sum = scatter_end(second_sent, "mix_back")
+    second_sum = lax.psum(later(second_sum, first_sum), "seq")
+    up_under_way = [
+        flip_chip(later(up_wg[2 * k + 1], *down_far), k) for k in range(len(up_plan))
+    ]
+    up_sent, up_far = scatter_begin(
+        up_wg, up_plan, "attention_back", under_way=up_under_way
+    )
     dqkv, one_part, one_low, qkv_bg = call(
         "qkv_back",
         qkv_back_body,
@@ -1363,19 +1368,19 @@
         [qkv_weights],
         [flat(3 * inner, HALF), flat(width, WIDE), flat(width, HALF)],
         [(1, 3 * inner)],
-        after=[first_sum, *up_far],
+        after=[second_sum, *up_far],
     )
     one_came = flip_core(one_low[rows // 2 :])
     qkv_plan = halves(qkv_have[0].shape[0])
     out_sent, out_far = scatter_begin(out_wg, out_plan, "qkv_back")
     qkv_wg = weight_grad_call(
-        "qkv_grad", me, hidden_one_t, [dqkv], qkv_plan, 384
+        "qkv_grad", me, hidden_one_t, [dqkv], qkv_plan, 256
     )
     up_part = scatter_end(up_sent, "qkv_grad")
     out_part = scatter_end(out_sent, "qkv_grad")
     down_part = scatter_end(down_sent, "attention_back")
     down_part = lax.psum(later(down_part, second_sum), "seq")
-    up_part, out_part = lax.psum((later(up_part, down_part), out_part), "seq")
+    up_part = lax.psum(later(up_part, down_part), "seq")
     input_low, shift_one_grad, scale_one_grad = token_call(
         "input_grad",
         input_body,
@@ -1387,14 +1392,14 @@
         [(1, width)] * 2,
         rows=rows // 2,
         tile=tile,
-        after=[qkv_wg[0], second_sum, *out_far],
+        after=[qkv_wg[0], down_part, *out_far],
     )
     input_grad = from_chip(input_low, 2)[0].astype(WIDE)
 
     qkv_sent, qkv_far = scatter_begin(qkv_wg, qkv_plan, "input_grad")
     qkv_scattered = scatter_end(qkv_sent)
-    qkv_hops = []
-    qkv_part = sum_planes(qkv_scattered, qkv_hops)
+    qkv_part, out_part = lax.psum((later(qkv_scattered, up_part), out_part), "seq")
+    qkv_hops = [qkv_scattered, qkv_scattered]
     one_grads = jnp.concatenate([shift_one_grad, scale_one_grad], axis=1)
     one_grads = later(one_grads + flip_core(one_grads), *qkv_far)
     modulation_grad = jnp.concatenate(
@@ -1402,6 +1407,7 @@
     )
     for bit in range(bits):
         modulation_grad = jnp.concatenate([modulation_grad, flip_chip(modulation_grad, bit)])
+    modulation_grad = later(modulation_grad, up_part)
     for bit in range(n_seq.bit_length() - 1):
         modulation_grad = jnp.concatenate([modulation_grad, flip_plane(modulation_grad, bit)])
     nth = jnp.arange(chips * n_seq)
@@ -1427,11 +1433,12 @@
     class_grad = jnp.einsum("bt,bd->td", class_hot, cond_grad, precision=HIGH)
 
     sums = [qkv_bg, up_bg, first_bg, second_bg, out_bg, down_bg, third_bg, cos_sum]
-    line = later(jnp.concatenate(sums, axis=1), *qkv_far)
+    line = later(jnp.concatenate(sums, axis=1), qkv_scattered)
     for bit in range(bits):
         line = line + flip_chip(line, bit)
     for bit in range(n_seq.bit_length() - 1):
         line = line + flip_plane(line, bit)
+    line = later(line, qkv_hops[0])
     split_at = sum(s.shape[1] for s in sums[:4])
     came = flip_core(line[:, :split_at])
     bias_grads, at = [], 0

time: 893 us -> 828 us (0.927)
  waiting for transfers between devices: 271 us -> 235 us
  other arithmetic: 58.6 us -> 45.8 us
    ppermute x8 -> x4, waiting for transfers between devices: 94.4 us -> 23.8 us  [flip_plane(): return lax.ppermute(array, 'seq', [(i, i ^ 1 << bit) for i in range(n_seq)])]
    psum x3 -> x4, waiting for transfers between devices: 0.01 us -> 28.9 us  [the longest x1 17.3 us: shards(): lax.psum((later(qkv_scattered, up_part), out_part), 'seq')]
    ppermute x8 -> x4, starting transfers between devices: 0.88 us -> 16.9 us  [flip_plane(): return lax.ppermute(array, 'seq', [(i, i ^ 1 << bit) for i in range(n_seq)])]
    psum x1, waiting for transfers between devices: 0.01 us -> 15.8 us  [shards(): down_part = lax.psum(later(down_part, second_sum), 'seq')]
    ppermute x20, starting transfers between devices: 34.2 us -> 22.1 us  [flip_core(): return lax.ppermute(array, 'dp', [(i, i ^ 1) for i in range(n_dp)])]
    unnamed x190 -> x188, local copies, waits for them, and re-layouts: 16.9 us -> 19.8 us
  transfers between devices with their start and end apart: 89 -> 86, of which waited for: 33 -> 33; matrix products, arithmetic and copies ran while one was open for 15% -> 14% of each run, Pallas kernels for 28% -> 30%
where the time goes in v2:
time: 828 us; the launch traced here: 817 us
  Pallas kernels  308 us (37%)
  waiting for transfers between devices  235 us (28%)
  starting transfers between devices  114 us (14%)
  local copies, waits for them, and re-layouts  64.6 us (8%)
  other arithmetic  45.8 us (6%)
  matrix products  19.5 us (2%)
  between operations  16.7 us (2%)
  blocking collectives  12.6 us (2%)
    pallas_call x11, Pallas kernels, token_call(): pl.pallas_call(functools.partial(token_kernel, body, counts, [how for _,...  163 us
    ppermute x40, waiting for transfers between devices, flip_chip(): return lax.ppermute(array, 'dp', [(i, i ^ 2 << bit) for i in range(n_dp)])  112 us
    pallas_call x7, Pallas kernels, weight_grad_call(): pl.pallas_call(functools.partial(weight_grad_kernel, plan, size, sides),...  56.1 us
    ppermute x40, starting transfers between devices, flip_chip(): return lax.ppermute(array, 'dp', [(i, i ^ 2 << bit) for i in range(n_dp)])  31.2 us
    pallas_call x1, Pallas kernels, attention_back_call(): pl.pallas_call(attention_back_kernel, grid=(heads,), in_specs=[block] * 4...  31.2 us
    ppermute x8, waiting for transfers between devices, to_chip(): found.append(lax.ppermute(piece, ('dp', 'seq'), routes(turn)))  31.1 us
    ppermute x8, starting transfers between devices, to_chip(): found.append(lax.ppermute(piece, ('dp', 'seq'), routes(turn)))  30.4 us
    pallas_call x1, Pallas kernels, attention_call(): pl.pallas_call(attention_kernel, grid=(heads,), in_specs=[block] * 3 + [p...  29.7 us
  transfers between devices with their start and end apart: 86, of which 33 were waited for; matrix products, arithmetic and copies ran while one was open for 14% of the time, Pallas kernels for 30%

profile of v2, /device:TPU:1, one launch (start us, length us, event | category | flops | bytes accessed | tf_op | source)
XLA Modules:
  0.0 816.9 jit_solution(14059848845064737334)
XLA Ops:
  88.5 13.4 %qkv.1 = (bf16[1152,1024]{1,0:T(8,128)(2,1)}, bf16[8,1024,72]{2,1,0:T(8,128)(2,1)}, bf16[8,1024,72]{2,1,0:T(8,128)(2,1)}, bf16[8,1024,72]{2,1,0:T(8,128)(2,1)}, f32[8,128]{1,0:T(8,128)}) custom-call(s32[1]{0:T(128)} %bitcast.me_ref, bf16[1024,1152]{1,0:T(8,128)(2,1)} %copy-done.62, f32[1,1152]{1,0:T(1,128)} %get-tuple-element.550.refs_1_, ...), custom_call_target="tpu_custom_call" | custom-call | flops 14949999616 | bytes 46800000 | tf_op jit(solution)/shard_map/qkv/pallas_call | solution.py:218
  102.0 29.7 %attention.1 = (bf16[8,1024,72]{2,1,0:T(8,128)(2,1)}, f32[8,1,1024]{2,1,0:T(1,128)}, f32[8,128]{1,0:T(8,128)}) custom-call(bf16[8,1024,72]{2,1,0:T(8,128)(2,1)} %get-tuple-element.263.query, bf16[8,1024,72]{2,1,0:T(8,128)(2,1)} %get-tuple-element.264.key, bf16[8,1024,72]{2,1,0:T(8,128)(2,1)} %get-tuple-element.265.value), custom_call_target="tpu_custom_call" | custom-call | flops 34500001792 | bytes 108000000 | tf_op jit(solution)/shard_map/attention/pallas_call | solution.py:278
  131.7 16.8 %collective-permute-done.18.refs_3_.refs_10_.refs_14_.refs_11_.refs_16_.refs_18_ = bf16[1296,1152]{1,0:T(8,128)(2,1)S(1)} collective-permute-done((bf16[1296,1152]{1,0:T(8,128)(2,1)}, bf16[1296,1152]{1,0:T(8,128)(2,1)S(1)}, u32[]{:S(2)}, u32[]{:S(2)}) %collective-permute-start.18) | collective-permute-done | bytes 2986016 | tf_op jit(solution)/shard_map/ppermute | solution.py:809
  224.8 18.5 %collective-permute-done.28.refs_18_.refs_8_.refs_12_.refs_5_.refs_7_.refs_9_ = bf16[3968,256]{1,0:T(8,128)(2,1)S(1)} collective-permute-done((bf16[3968,256]{1,0:T(8,128)(2,1)}, bf16[3968,256]{1,0:T(8,128)(2,1)S(1)}, u32[]{:S(2)}, u32[]{:S(2)}) %collective-permute-start.28) | collective-permute-done | bytes 2031648 | tf_op jit(solution)/shard_map/ppermute | solution.py:809
  244.6 27.0 %feed.1 = (f32[1024,1152]{1,0:T(8,128)}, bf16[1152,1024]{1,0:T(8,128)(2,1)}, f32[1024,2304]{1,0:T(8,128)}, bf16[2304,1024]{1,0:T(8,128)(2,1)}, f32[1024,1152]{1,...) custom-call(s32[1]{0:T(128)} %bitcast.me_ref, bf16[1024,1152]{1,0:T(8,128)(2,1)} %copy-done.62, ...), custom_call_target="tpu_custom_call" | custom-call | flops 31050000384 | bytes 97200000 | tf_op jit(solution)/shard_map/feed/pallas_call | solution.py:218
  277.9 20.7 %collective-permute-done.30.refs_9_.refs_6_.refs_8_.refs_10_ = bf16[1920,256]{1,0:T(8,128)(2,1)} collective-permute-done((bf16[1920,256]{1,0:T(8,128)(2,1)S(1)}, bf16[1920,256]{1,0:T(8,128)(2,1)}, u32[]{:S(2)}, u32[]{:S(2)}) %collective-permute-start.30) | collective-permute-done | bytes 983072 | tf_op jit(solution)/shard_map/ppermute | solution.py:809
  299.6 17.1 %tap.1 = (bf16[1024,1152]{1,0:T(8,128)(2,1)}, bf16[1152,1024]{1,0:T(8,128)(2,1)}, f32[1024,1024]{1,0:T(8,128)}, bf16[1024,1024]{1,0:T(8,128)(2,1)}, f32[1024,102...) custom-call(s32[1]{0:T(128)} %bitcast.me_ref, f32[1024,1152]{1,0:T(8,128)} %get-tuple-element.282.refs_0_, ...), custom_call_target="tpu_custom_call" | custom-call | flops 18400000000 | bytes 57600000 | tf_op jit(solution)/shard_map/tap/pallas_call | solution.py:218
  339.7 9.8 %cosine.1 = (bf16[1024,768]{1,0:T(8,128)(2,1)}, bf16[1024,1024]{1,0:T(8,128)(2,1)}, f32[1,128]{1,0:T(1,128)}, f32[1,768]{1,0:T(1,128)}, f32[1,1024]{1,0:T(1,128)}, /*index=5*/f32[8,128]{1,0:T(8,128)}) custom-call(s32[1]{0:T(128)} %bitcast.me_ref, f32[1024,768]{1,0:T(8,128)} %get-tuple-element.288.refs_0_, bf16[1024,768]{1,0:T(8,128)(2,1)} %copy-done.79, ...), custom_call_target="tpu_custom_call" | custom-call | flops 10350000128 | bytes 32400000 | tf_op jit(solution)/shard_map/cosine/pallas_call | solution.py:218
  381.8 16.7 %tap_back.1 = (bf16[1024,1024]{1,0:T(8,128)(2,1)}, f32[1024,1152]{1,0:T(8,128)}, bf16[1024,1152]{1,0:T(8,128)(2,1)}, f32[1,1024]{1,0:T(1,128)}, f32[8,128]{1,0:T(8,128)}) custom-call(s32[1]{0:T(128)} %bitcast.me_ref, bf16[1024,1024]{1,0:T(8,128)(2,1)} %get-tuple-element.295.refs_0_, bf16[1024,1024]{1,0:T(8,128)(2,1)} %collective-permute-done.38.refs_1_, ...), custom_call_target="tpu_custom_call" | custom-call | flops 18400000000 | bytes 57600000 | tf_op jit(solution)/shard_map/tap_back/pallas_call | solution.py:218
  410.8 28.4 %feed_back.1 = (f32[1024,1152]{1,0:T(8,128)}, bf16[1024,1152]{1,0:T(8,128)(2,1)}, bf16[1024,2304]{1,0:T(8,128)(2,1)}, f32[1024,1152]{1,0:T(8,128)}, bf16[1024,11...) custom-call(s32[1]{0:T(128)} %bitcast.me_ref, ...), custom_call_target="tpu_custom_call" | custom-call | flops 32199999488 | bytes 100800000 | tf_op jit(solution)/shard_map/feed_back/pallas_call | solution.py:218
  445.3 11.1 %down_grad.1 = (bf16[576,1152]{1,0:T(8,128)(2,1)}, bf16[576,1152]{1,0:T(8,128)(2,1)}, bf16[576,1152]{1,0:T(8,128)(2,1)}, bf16[576,1152]{1,0:T(8,128)(2,1)}, f32[8,128]{1,0:T(8,128)}) custom-call(s32[1]{0:T(128)} %bitcast.me_ref, bf16[2304,1024]{1,0:T(8,128)(2,1)} %get-tuple-element.319.left, bf16[1024,1152]{1,0:T(8,128)(2,1)} %get-tuple-element.320.refs_0_, ...), custom_call_target="tpu_custom_call" | custom-call | flops 13799999488 | bytes 43200000 | tf_op jit(solution)/shard_map/down_grad/pallas_call | solution.py:570
  464.2 9.8 %up_grad.1 = (bf16[288,2304]{1,0:T(8,128)(2,1)}, bf16[288,2304]{1,0:T(8,128)(2,1)}, bf16[288,2304]{1,0:T(8,128)(2,1)}, bf16[288,2304]{1,0:T(8,128)(2,1)}, f32[8,128]{1,0:T(8,128)}) custom-call(s32[1]{0:T(128)} %bitcast.me_ref, bf16[1152,1024]{1,0:T(8,128)(2,1)} %get-tuple-element.317.left, bf16[1024,2304]{1,0:T(8,128)(2,1)} %get-tuple-element.318.refs_0_, ...), custom_call_target="tpu_custom_call" | custom-call | flops 13799999488 | bytes 43200000 | tf_op jit(solution)/shard_map/up_grad/pallas_call | solution.py:570
  475.8 14.8 %mix_back.1 = (f32[1024,1152]{1,0:T(8,128)}, bf16[1024,1152]{1,0:T(8,128)(2,1)}, bf16[8,1024,72]{2,1,0:T(8,128)(2,1)}, f32[1,1152]{1,0:T(1,128)}, f32[1,1152]{1,...) custom-call(s32[1]{0:T(128)} %bitcast.me_ref, f32[1024,1152]{1,0:T(8,128)} %get-tuple-element.282.refs_0_, ...), custom_call_target="tpu_custom_call" | custom-call | flops 16099999744 | bytes 50400000 | tf_op jit(solution)/shard_map/mix_back/pallas_call | solution.py:218
  490.6 24.6 %collective-permute-done.49.refs_40_.refs_42_ = bf16[576,1152]{1,0:T(8,128)(2,1)S(1)} collective-permute-done((bf16[576,1152]{1,0:T(8,128)(2,1)}, bf16[576,1152]{1,0:T(8,128)(2,1)S(1)}, u32[]{:S(2)}, u32[]{:S(2)}) %collective-permute-start.49) | collective-permute-done | bytes 1327136 | tf_op jit(solution)/shard_map/ppermute | solution.py:809
  535.0 31.2 %attention_back.1 = (bf16[8,1024,72]{2,1,0:T(8,128)(2,1)}, bf16[8,1024,72]{2,1,0:T(8,128)(2,1)}, bf16[8,1024,72]{2,1,0:T(8,128)(2,1)}, f32[8,128]{1,0:T(8,128)}) custom-call(bf16[8,1024,72]{2,1,0:T(8,128)(2,1)} %get-tuple-element.263.query, bf16[8,1024,72]{2,1,0:T(8,128)(2,1)} %get-tuple-element.264.key, bf16[8,1024,72]{2,1,0:T(8,128)(2,1)} %get-tuple-element.265.value, ...), custom_call_target="tpu_custom_call" | custom-call | flops 35649998848 | bytes 111600000 | tf_op jit(solution)/shard_map/attention_back/pallas_call | solution.py:331
  582.6 12.8 %qkv_back.1 = (bf16[1024,1728]{1,0:T(8,128)(2,1)}, f32[1024,1152]{1,0:T(8,128)}, bf16[1024,1152]{1,0:T(8,128)(2,1)}, f32[1,1728]{1,0:T(1,128)}, f32[8,128]{1,0:T(8,128)}) custom-call(s32[1]{0:T(128)} %bitcast.me_ref, bf16[8,1024,72]{2,1,0:T(8,128)(2,1)} %get-tuple-element.345.refs_0_, bf16[8,1024,72]{2,1,0:T(8,128)(2,1)} %get-tuple-element.346.refs_1_, ...), custom_call_target="tpu_custom_call" | custom-call | flops 13799999488 | bytes 43200000 | tf_op jit(solution)/shard_map/qkv_back/pallas_call | solution.py:218
  602.2 9.7 %qkv_grad.1 = (bf16[288,1728]{1,0:T(8,128)(2,1)}, bf16[288,1728]{1,0:T(8,128)(2,1)}, bf16[288,1728]{1,0:T(8,128)(2,1)}, bf16[288,1728]{1,0:T(8,128)(2,1)}, f32[8,128]{1,0:T(8,128)}) custom-call(s32[1]{0:T(128)} %bitcast.me_ref, bf16[1152,1024]{1,0:T(8,128)(2,1)} %get-tuple-element.359.left, bf16[1024,1728]{1,0:T(8,128)(2,1)} %get-tuple-element.360.refs_0_), custom_call_target="tpu_custom_call" | custom-call | flops 11500000256 | bytes 36000000 | tf_op jit(solution)/shard_map/qkv_grad/pallas_call | solution.py:570
  622.6 15.8 %all-reduce.15.cloned.1.call-done.refs_6_.refs_52_ = bf16[576,1152]{1,0:T(8,128)(2,1)} async-done(((bf16[576,1152]{1,0:T(8,128)(2,1)}), bf16[576,1152]{1,0:T(8,128)(2,1)}) %all-reduce.15.cloned.1.call-update) | async-done | bytes 1327120 | tf_op jit(solution)/shard_map/psum | solution.py:1382
  657.3 10.4 %collective-permute-done.73 = f32[2,6912]{1,0:T(2,128)S(1)} collective-permute-done((f32[2,6912]{1,0:T(2,128)S(1)}, f32[2,6912]{1,0:T(2,128)S(1)}, u32[]{:S(2)}, u32[]{:S(2)}) %collective-permute-start.73) | collective-permute-done | bytes 55328 | tf_op jit(solution)/shard_map/ppermute | solution.py:809
  667.7 10.6 %collective-permute-done.56.refs_53_ = bf16[128,1152]{1,0:T(8,128)(2,1)S(1)} collective-permute-done((bf16[128,1152]{1,0:T(8,128)(2,1)S(1)}, bf16[128,1152]{1,0:T(8,128)(2,1)S(1)}, u32[]{:S(2)}, u32[]{:S(2)}) %collective-permute-start.56) | collective-permute-done | bytes 294944 | tf_op jit(solution)/shard_map/ppermute | solution.py:940
  692.4 14.2 %collective-permute-start.66 = (f32[1,9280]{1,0:T(1,128)S(1)}, f32[1,9280]{1,0:T(1,128)S(1)}, u32[]{:S(2)}, u32[]{:S(2)}) collective-permute-start(f32[1,9280]{1,0:T(1,128)S(1)} %add.345), channel_id=1, source_target_pairs={{0,1},{1,0},{2,3},{3,2},{4,5},{5,4},{6,7},{7,6},{8,9},{9,8},{10,11... | collective-permute-start | bytes 111368 | tf_op jit(solution)/shard_map/ppermute | solution.py:812
  734.2 15.5 %collective-permute-done.75 = f32[8,6912]{1,0:T(8,128)S(1)} collective-permute-done((f32[8,6912]{1,0:T(8,128)S(1)}, f32[8,6912]{1,0:T(8,128)S(1)}, u32[]{:S(2)}, u32[]{:S(2)}) %collective-permute-start.75) | collective-permute-done | bytes 221216 | tf_op jit(solution)/shard_map/ppermute | solution.py:812
  754.1 12.6 %all-gather = f32[8,144,16]{1,2,0:T(8,128)S(1)} all-gather(f32[1,144,16]{1,2,0:T(8,128)S(1)} %fusion.22), channel_id=1, replica_groups=mesh['dp'=8,'seq'=4] {'dp'}, dimensions={0}, use_global_device_ids=true | all-gather | bytes 82944 | tf_op jit(solution)/shard_map/all_gather | solution.py:1425
  780.2 17.3 %all-reduce.19.cloned.1.call-done = (bf16[144,1152]{1,0:T(8,128)(2,1)}, bf16[288,1728]{1,0:T(8,128)(2,1)}) async-done(((bf16[144,1152]{1,0:T(8,128)(2,1)}, bf16[288,1728]{1,0:T(8,128)(2,1)}), (bf16[144,1152]{1,0:T(8,128)(2,1)}, bf16[288,1728]{1,0:T(8,128)(2,1)})) %all-reduce.19.cloned.1.call-update) | async-done | bytes 1327120 | tf_op jit(solution)/shard_map/psum | solution.py:1401
  (529 shorter events, 392.0 us)
Async XLA Ops:
  7.2 438.1 %all-reduce.9.cloned.1.call-start = ((), (), s32[]{:S(2)}) async-start(), calls=%async_computation | async-start | bytes 786432 | tf_op jit(solution)/shard_map/psum | solution.py:1307
  84.7 63.8 %collective-permute-start.18 = (bf16[1296,1152]{1,0:T(8,128)(2,1)}, bf16[1296,1152]{1,0:T(8,128)(2,1)S(1)}, u32[]{:S(2)}, u32[]{:S(2)}) collective-permute-start(bf16[1296,1152]{1,0:T(8,128)(2,1)} %pack_near.1.refs_1_.refs_8_.refs_12_.refs_9_), channel_id=1, source_target_pairs={{0,16},{4,20},{8,24},{12,28},{16,0},{20,4},{24,8},{28,12},{1,17},{... | collective-permute-start | bytes 8957960 | tf_op jit(solution)/shard_map/ppermute | solution.py:809
  85.9 63.4 %collective-permute-start.17 = (bf16[1296,1152]{1,0:T(8,128)(2,1)}, bf16[1296,1152]{1,0:T(8,128)(2,1)S(1)}, u32[]{:S(2)}, u32[]{:S(2)}) collective-permute-start(bf16[1296,1152]{1,0:T(8,128)(2,1)} %pack_near.1.refs_1_.refs_8_.refs_12_.refs_9_), channel_id=1, source_target_pairs={{0,8},{4,12},{8,0},{12,4},{16,24},{20,28},{24,16},{28,20},{1,9},{5... | collective-permute-start | bytes 8957960 | tf_op jit(solution)/shard_map/ppermute | solution.py:809
  148.6 37.2 %collective-permute-start.19 = (bf16[720,1152]{1,0:T(8,128)(2,1)S(1)}, bf16[720,1152]{1,0:T(8,128)(2,1)}, u32[]{:S(2)}, u32[]{:S(2)}) collective-permute-start(bf16[720,1152]{1,0:T(8,128)(2,1)S(1)} %slice.291), channel_id=1, source_target_pairs={{0,8},{4,12},{8,0},{12,4},{16,24},{20,28},{24,16},{28,20},{1,9},{5... | collective-permute-start | bytes 4976648 | tf_op jit(solution)/shard_map/ppermute | solution.py:809
  194.0 49.3 %collective-permute-start.24 = (bf16[1024,1152]{1,0:T(8,128)(2,1)}, bf16[1024,1152]{1,0:T(8,128)(2,1)}, u32[]{:S(2)}, u32[]{:S(2)}) collective-permute-start(bf16[1024,1152]{1,0:T(8,128)(2,1)} %get-tuple-element.278), channel_id=1, source_target_pairs={{0,4},{4,0},{8,12},{12,8},{16,20},{20,16},{24,28},{28,24},{1,5},{5... | collective-permute-start | bytes 7077896 | tf_op jit(solution)/shard_map/ppermute | solution.py:806
  197.1 46.1 %collective-permute-start.28 = (bf16[3968,256]{1,0:T(8,128)(2,1)}, bf16[3968,256]{1,0:T(8,128)(2,1)S(1)}, u32[]{:S(2)}, u32[]{:S(2)}) collective-permute-start(bf16[3968,256]{1,0:T(8,128)(2,1)} %pack_far.1.refs_6_.refs_10_.refs_3_.refs_5_.refs_7_), channel_id=1, source_target_pairs={{0,16},{4,20},{8,24},{12,28},{16,0},{20,4},{24,8},{28,12},{1,17},{... | collective-permute-start | bytes 6094856 | tf_op jit(solution)/shard_map/ppermute | solution.py:809
  197.4 45.8 %collective-permute-start.27 = (bf16[3968,256]{1,0:T(8,128)(2,1)}, bf16[3968,256]{1,0:T(8,128)(2,1)}, u32[]{:S(2)}, u32[]{:S(2)}) collective-permute-start(bf16[3968,256]{1,0:T(8,128)(2,1)} %pack_far.1.refs_6_.refs_10_.refs_3_.refs_5_.refs_7_), channel_id=1, source_target_pairs={{0,8},{4,12},{8,0},{12,4},{16,24},{20,28},{24,16},{28,20},{1,9},{5... | collective-permute-start | bytes 6094856 | tf_op jit(solution)/shard_map/ppermute | solution.py:809
  409.0 47.5 %collective-permute-start.45 = (bf16[512,2048]{1,0:T(8,128)(2,1)}, bf16[512,2048]{1,0:T(8,128)(2,1)S(1)}, u32[]{:S(2)}, u32[]{:S(2)}) collective-permute-start(bf16[512,2048]{1,0:T(8,128)(2,1)} %get-tuple-element.327), channel_id=1, source_target_pairs={{0,8},{4,12},{8,0},{12,4},{16,24},{20,28},{24,16},{28,20},{1,9},{5... | collective-permute-start | bytes 6291464 | tf_op jit(solution)/shard_map/ppermute | solution.py:809
  410.3 112.9 %all-reduce.11.cloned.1.call-start = ((), (), s32[]{:S(2)}) async-start(), calls=%async_computation.1 | async-start | bytes 1179648 | tf_op jit(solution)/shard_map/psum | solution.py:1319
  462.4 56.5 %collective-permute-start.51 = (bf16[256,2048]{1,0:T(8,128)(2,1)}, bf16[256,2048]{1,0:T(8,128)(2,1)}, u32[]{:S(2)}, u32[]{:S(2)}) collective-permute-start(bf16[256,2048]{1,0:T(8,128)(2,1)} %add_convert_fusion.1), channel_id=1, source_target_pairs={{0,16},{4,20},{8,24},{12,28},{16,0},{20,4},{24,8},{28,12},{1,17},{... | collective-permute-start | bytes 3145736 | tf_op jit(solution)/shard_map/ppermute | solution.py:809
  463.6 51.5 %collective-permute-start.47 = (bf16[576,1152]{1,0:T(8,128)(2,1)}, bf16[576,1152]{1,0:T(8,128)(2,1)S(1)}, u32[]{:S(2)}, u32[]{:S(2)}) collective-permute-start(bf16[576,1152]{1,0:T(8,128)(2,1)} %get-tuple-element.339), channel_id=1, source_target_pairs={{0,8},{4,12},{8,0},{12,4},{16,24},{20,28},{24,16},{28,20},{1,9},{5... | collective-permute-start | bytes 3981320 | tf_op jit(solution)/shard_map/ppermute | solution.py:809
  463.9 51.2 %collective-permute-start.49 = (bf16[576,1152]{1,0:T(8,128)(2,1)}, bf16[576,1152]{1,0:T(8,128)(2,1)S(1)}, u32[]{:S(2)}, u32[]{:S(2)}) collective-permute-start(bf16[576,1152]{1,0:T(8,128)(2,1)} %get-tuple-element.343), channel_id=1, source_target_pairs={{0,16},{4,20},{8,24},{12,28},{16,0},{20,4},{24,8},{28,12},{1,17},{... | collective-permute-start | bytes 3981320 | tf_op jit(solution)/shard_map/ppermute | solution.py:809
  475.5 100.1 %all-reduce.13.cloned.1.call-start = ((), (), s32[]{:S(2)}) async-start(), calls=%async_computation.2 | async-start | bytes 2097152 | tf_op jit(solution)/shard_map/psum | solution.py:1355
  523.2 115.1 %all-reduce.15.cloned.1.call-start = ((), (), s32[]{:S(2)}) async-start(), calls=%async_computation.3 | async-start | bytes 2654208 | tf_op jit(solution)/shard_map/psum | solution.py:1382
  528.5 66.9 %collective-permute-start.55 = (bf16[288,1152]{1,0:T(8,128)(2,1)}, bf16[288,1152]{1,0:T(8,128)(2,1)}, u32[]{:S(2)}, u32[]{:S(2)}) collective-permute-start(bf16[288,1152]{1,0:T(8,128)(2,1)} %get-tuple-element.365), channel_id=1, source_target_pairs={{0,8},{4,12},{8,0},{12,4},{16,24},{20,28},{24,16},{28,20},{1,9},{5... | collective-permute-start | bytes 1990664 | tf_op jit(solution)/shard_map/ppermute | solution.py:809
  529.7 47.1 %collective-permute-start.52 = (bf16[288,2304]{1,0:T(8,128)(2,1)}, bf16[288,2304]{1,0:T(8,128)(2,1)}, u32[]{:S(2)}, u32[]{:S(2)}) collective-permute-start(bf16[288,2304]{1,0:T(8,128)(2,1)} %get-tuple-element.351), channel_id=1, source_target_pairs={{0,8},{4,12},{8,0},{12,4},{16,24},{20,28},{24,16},{28,20},{1,9},{5... | collective-permute-start | bytes 3981320 | tf_op jit(solution)/shard_map/ppermute | solution.py:809
  529.9 50.1 %collective-permute-start.53 = (bf16[288,2304]{1,0:T(8,128)(2,1)}, bf16[288,2304]{1,0:T(8,128)(2,1)}, u32[]{:S(2)}, u32[]{:S(2)}) collective-permute-start(bf16[288,2304]{1,0:T(8,128)(2,1)} %get-tuple-element.355), channel_id=1, source_target_pairs={{0,16},{4,20},{8,24},{12,28},{16,0},{20,4},{24,8},{28,12},{1,17},{... | collective-permute-start | bytes 3981320 | tf_op jit(solution)/shard_map/ppermute | solution.py:809
  575.7 150.6 %all-reduce.17.cloned.1.call-start = ((), (), s32[]{:S(2)}) async-start(), calls=%async_computation.4 | async-start | bytes 2654208 | tf_op jit(solution)/shard_map/psum | solution.py:1383
  578.9 40.9 %collective-permute-start.68 = (bf16[144,2304]{1,0:T(8,128)(2,1)}, bf16[144,2304]{1,0:T(8,128)(2,1)}, u32[]{:S(2)}, u32[]{:S(2)}) collective-permute-start(bf16[144,2304]{1,0:T(8,128)(2,1)} %add_convert_fusion.5), channel_id=1, source_target_pairs={{0,16},{4,20},{8,24},{12,28},{16,0},{20,4},{24,8},{28,12},{1,17},{... | collective-permute-start | bytes 1990664 | tf_op jit(solution)/shard_map/ppermute | solution.py:809
  599.2 39.3 %collective-permute-start.54 = (bf16[512,1152]{1,0:T(8,128)(2,1)}, bf16[512,1152]{1,0:T(8,128)(2,1)}, u32[]{:S(2)}, u32[]{:S(2)}) collective-permute-start(bf16[512,1152]{1,0:T(8,128)(2,1)} %slice.329), channel_id=1, source_target_pairs={{0,4},{4,0},{8,12},{12,8},{16,20},{20,16},{24,28},{28,24},{1,5},{5... | collective-permute-start | bytes 3538952 | tf_op jit(solution)/shard_map/ppermute | solution.py:806
  612.0 36.3 %collective-permute-start.60 = (bf16[288,1728]{1,0:T(8,128)(2,1)}, bf16[288,1728]{1,0:T(8,128)(2,1)S(1)}, u32[]{:S(2)}, u32[]{:S(2)}) collective-permute-start(bf16[288,1728]{1,0:T(8,128)(2,1)} %get-tuple-element.381), channel_id=1, source_target_pairs={{0,8},{4,12},{8,0},{12,4},{16,24},{20,28},{24,16},{28,20},{1,9},{5... | collective-permute-start | bytes 2985992 | tf_op jit(solution)/shard_map/ppermute | solution.py:809
  638.4 159.1 %all-reduce.19.cloned.1.call-start = ((), (), s32[]{:S(2)}) async-start(), calls=%async_computation.5 | async-start | bytes 2727936 | tf_op jit(solution)/shard_map/psum | solution.py:1401
  688.1 38.1 %collective-permute-start.79 = (bf16[144,1024]{1,0:T(8,128)(2,1)S(1)}, bf16[144,1024]{1,0:T(8,128)(2,1)S(1)}, u32[]{:S(2)}, u32[]{:S(2)}) collective-permute-start(bf16[144,1024]{1,0:T(8,128)(2,1)S(1)} %get-tuple-element.513), channel_id=1, source_target_pairs={{0,4},{4,0},{8,12},{12,8},{16,20},{20,16},{24,28},{28,24},{1,5},{5... | collective-permute-start | bytes 884744 | tf_op jit(solution)/shard_map/ppermute | solution.py:806
  733.2 67.3 %collective-permute-start.78 = (bf16[144,2304]{1,0:T(8,128)(2,1)S(1)}, bf16[144,2304]{1,0:T(8,128)(2,1)S(1)}, u32[]{:S(2)}, u32[]{:S(2)}) collective-permute-start(bf16[144,2304]{1,0:T(8,128)(2,1)S(1)} %get-tuple-element.499), channel_id=1, source_target_pairs={{0,4},{4,0},{8,12},{12,8},{16,20},{20,16},{24,28},{28,24},{1,5},{5... | collective-permute-start | bytes 1990664 | tf_op jit(solution)/shard_map/ppermute | solution.py:806
  (148 other events, 2008.5 us)
Sparse Core Ops, SparseCore 0:
  410.4 34.8 all-reduce.8
  475.7 39.8 all-reduce.10
  523.3 52.3 all-reduce.12
  578.5 59.8 all-reduce.14
  641.2 79.1 all-reduce.16
  734.4 63.0 all-reduce.18

commit v3 on v2

--- a/solution.py
+++ b/solution.py
@@ -1254,7 +1254,7 @@
     dsecond_came = flip_core(dsecond)
     third_plan = [(ranks(1 % bits), 0, tap_third.shape[0])]
     third_wg = weight_grad_call("third_grad", me, second_t, [dlatent], third_plan, 384)
-    second_plan = [(ranks(0), 0, tap_second.shape[0])]
+    second_plan = halves(tap_second.shape[0])
     second_wg = weight_grad_call(
         "second_grad", me, first_t, [dsecond, dsecond_came], second_plan, 512, after=third_wg[:1]
     )

time: 828 us -> 838 us (1.012)
    ppermute x40 -> x42, waiting for transfers between devices: 112 us -> 115 us  [flip_chip(): return lax.ppermute(array, 'dp', [(i, i ^ 2 << bit) for i in range(n_dp)])]
    ppermute x40 -> x42, starting transfers between devices: 31.2 us -> 35 us  [flip_chip(): return lax.ppermute(array, 'dp', [(i, i ^ 2 << bit) for i in range(n_dp)])]
    unnamed x188 -> x194, local copies, waits for them, and re-layouts: 19.8 us -> 20.9 us
  transfers between devices with their start and end apart: 86 -> 88, of which waited for: 33 -> 32; matrix products, arithmetic and copies ran while one was open for 14% -> 13% of each run, Pallas kernels for 30% -> 29%
where the time goes in v3:
time: 838 us; the launch traced here: 827 us
  Pallas kernels  308 us (37%)
  waiting for transfers between devices  243 us (29%)
  starting transfers between devices  116 us (14%)
  local copies, waits for them, and re-layouts  65.7 us (8%)
  other arithmetic  45.2 us (5%)
  matrix products  19.5 us (2%)
  between operations  16.8 us (2%)
  blocking collectives  13 us (2%)
    pallas_call x11, Pallas kernels, token_call(): pl.pallas_call(functools.partial(token_kernel, body, counts, [how for _,...  162 us
    ppermute x42, waiting for transfers between devices, flip_chip(): return lax.ppermute(array, 'dp', [(i, i ^ 2 << bit) for i in range(n_dp)])  115 us
    pallas_call x7, Pallas kernels, weight_grad_call(): pl.pallas_call(functools.partial(weight_grad_kernel, plan, size, sides),...  56.2 us
    ppermute x42, starting transfers between devices, flip_chip(): return lax.ppermute(array, 'dp', [(i, i ^ 2 << bit) for i in range(n_dp)])  35 us
    pallas_call x1, Pallas kernels, attention_back_call(): pl.pallas_call(attention_back_kernel, grid=(heads,), in_specs=[block] * 4...  31.1 us
    ppermute x8, waiting for transfers between devices, to_chip(): found.append(lax.ppermute(piece, ('dp', 'seq'), routes(turn)))  31.1 us
    ppermute x8, starting transfers between devices, to_chip(): found.append(lax.ppermute(piece, ('dp', 'seq'), routes(turn)))  30.4 us
    pallas_call x1, Pallas kernels, attention_call(): pl.pallas_call(attention_kernel, grid=(heads,), in_specs=[block] * 3 + [p...  29.7 us
  transfers between devices with their start and end apart: 88, of which 32 were waited for; matrix products, arithmetic and copies ran while one was open for 13% of the time, Pallas kernels for 29%

profile of v3, /device:TPU:1, one launch (start us, length us, event | category | flops | bytes accessed | tf_op | source)
XLA Modules:
  0.0 827.3 jit_solution(7905201189650441913)
XLA Ops:
  88.5 13.4 %qkv.1 = (bf16[1152,1024]{1,0:T(8,128)(2,1)}, bf16[8,1024,72]{2,1,0:T(8,128)(2,1)}, bf16[8,1024,72]{2,1,0:T(8,128)(2,1)}, bf16[8,1024,72]{2,1,0:T(8,128)(2,1)}, f32[8,128]{1,0:T(8,128)}) custom-call(s32[1]{0:T(128)} %bitcast.me_ref, bf16[1024,1152]{1,0:T(8,128)(2,1)} %copy-done.65, f32[1,1152]{1,0:T(1,128)} %get-tuple-element.562.refs_1_, ...), custom_call_target="tpu_custom_call" | custom-call | flops 14949999616 | bytes 46800000 | tf_op jit(solution)/shard_map/qkv/pallas_call | solution.py:218
  102.0 29.7 %attention.1 = (bf16[8,1024,72]{2,1,0:T(8,128)(2,1)}, f32[8,1,1024]{2,1,0:T(1,128)}, f32[8,128]{1,0:T(8,128)}) custom-call(bf16[8,1024,72]{2,1,0:T(8,128)(2,1)} %get-tuple-element.269.query, bf16[8,1024,72]{2,1,0:T(8,128)(2,1)} %get-tuple-element.270.key, bf16[8,1024,72]{2,1,0:T(8,128)(2,1)} %get-tuple-element.271.value), custom_call_target="tpu_custom_call" | custom-call | flops 34500001792 | bytes 108000000 | tf_op jit(solution)/shard_map/attention/pallas_call | solution.py:278
  131.6 16.8 %collective-permute-done.18.refs_3_.refs_10_.refs_14_.refs_11_.refs_16_.refs_18_ = bf16[1296,1152]{1,0:T(8,128)(2,1)S(1)} collective-permute-done((bf16[1296,1152]{1,0:T(8,128)(2,1)}, bf16[1296,1152]{1,0:T(8,128)(2,1)S(1)}, u32[]{:S(2)}, u32[]{:S(2)}) %collective-permute-start.18) | collective-permute-done | bytes 2986016 | tf_op jit(solution)/shard_map/ppermute | solution.py:809
  224.8 18.5 %collective-permute-done.28.refs_18_.refs_8_.refs_12_.refs_5_.refs_7_.refs_9_ = bf16[3968,256]{1,0:T(8,128)(2,1)S(1)} collective-permute-done((bf16[3968,256]{1,0:T(8,128)(2,1)}, bf16[3968,256]{1,0:T(8,128)(2,1)S(1)}, u32[]{:S(2)}, u32[]{:S(2)}) %collective-permute-start.28) | collective-permute-done | bytes 2031648 | tf_op jit(solution)/shard_map/ppermute | solution.py:809
  244.5 26.9 %feed.1 = (f32[1024,1152]{1,0:T(8,128)}, bf16[1152,1024]{1,0:T(8,128)(2,1)}, f32[1024,2304]{1,0:T(8,128)}, bf16[2304,1024]{1,0:T(8,128)(2,1)}, f32[1024,1152]{1,...) custom-call(s32[1]{0:T(128)} %bitcast.me_ref, bf16[1024,1152]{1,0:T(8,128)(2,1)} %copy-done.65, ...), custom_call_target="tpu_custom_call" | custom-call | flops 31050000384 | bytes 97200000 | tf_op jit(solution)/shard_map/feed/pallas_call | solution.py:218
  277.9 20.7 %collective-permute-done.30.refs_9_.refs_6_.refs_8_.refs_10_ = bf16[1920,256]{1,0:T(8,128)(2,1)} collective-permute-done((bf16[1920,256]{1,0:T(8,128)(2,1)S(1)}, bf16[1920,256]{1,0:T(8,128)(2,1)}, u32[]{:S(2)}, u32[]{:S(2)}) %collective-permute-start.30) | collective-permute-done | bytes 983072 | tf_op jit(solution)/shard_map/ppermute | solution.py:809
  299.5 17.0 %tap.1 = (bf16[1024,1152]{1,0:T(8,128)(2,1)}, bf16[1152,1024]{1,0:T(8,128)(2,1)}, f32[1024,1024]{1,0:T(8,128)}, bf16[1024,1024]{1,0:T(8,128)(2,1)}, f32[1024,102...) custom-call(s32[1]{0:T(128)} %bitcast.me_ref, f32[1024,1152]{1,0:T(8,128)} %get-tuple-element.288.refs_0_, ...), custom_call_target="tpu_custom_call" | custom-call | flops 18400000000 | bytes 57600000 | tf_op jit(solution)/shard_map/tap/pallas_call | solution.py:218
  381.8 16.7 %tap_back.1 = (bf16[1024,1024]{1,0:T(8,128)(2,1)}, f32[1024,1152]{1,0:T(8,128)}, bf16[1024,1152]{1,0:T(8,128)(2,1)}, f32[1,1024]{1,0:T(1,128)}, f32[8,128]{1,0:T(8,128)}) custom-call(s32[1]{0:T(128)} %bitcast.me_ref, bf16[1024,1024]{1,0:T(8,128)(2,1)} %get-tuple-element.301.refs_0_, bf16[1024,1024]{1,0:T(8,128)(2,1)} %collective-permute-done.38.refs_1_, ...), custom_call_target="tpu_custom_call" | custom-call | flops 18400000000 | bytes 57600000 | tf_op jit(solution)/shard_map/tap_back/pallas_call | solution.py:218
  411.0 28.4 %feed_back.1 = (f32[1024,1152]{1,0:T(8,128)}, bf16[1024,1152]{1,0:T(8,128)(2,1)}, bf16[1024,2304]{1,0:T(8,128)(2,1)}, f32[1024,1152]{1,0:T(8,128)}, bf16[1024,11...) custom-call(s32[1]{0:T(128)} %bitcast.me_ref, ...), custom_call_target="tpu_custom_call" | custom-call | flops 32199999488 | bytes 100800000 | tf_op jit(solution)/shard_map/feed_back/pallas_call | solution.py:218
  439.4 10.2 %collective-permute-done.43.refs_1_ = bf16[576,1024]{1,0:T(8,128)(2,1)S(1)} collective-permute-done((bf16[576,1024]{1,0:T(8,128)(2,1)}, bf16[576,1024]{1,0:T(8,128)(2,1)S(1)}, u32[]{:S(2)}, u32[]{:S(2)}) %collective-permute-start.43) | collective-permute-done | bytes 1179680 | tf_op jit(solution)/shard_map/ppermute | solution.py:809
  450.7 11.1 %down_grad.1 = (bf16[576,1152]{1,0:T(8,128)(2,1)}, bf16[576,1152]{1,0:T(8,128)(2,1)}, bf16[576,1152]{1,0:T(8,128)(2,1)}, bf16[576,1152]{1,0:T(8,128)(2,1)}, f32[8,128]{1,0:T(8,128)}) custom-call(s32[1]{0:T(128)} %bitcast.me_ref, bf16[2304,1024]{1,0:T(8,128)(2,1)} %get-tuple-element.325.left, bf16[1024,1152]{1,0:T(8,128)(2,1)} %get-tuple-element.326.refs_0_, ...), custom_call_target="tpu_custom_call" | custom-call | flops 13799999488 | bytes 43200000 | tf_op jit(solution)/shard_map/down_grad/pallas_call | solution.py:570
  479.7 11.3 %collective-permute-done.47 = bf16[288,1024]{1,0:T(8,128)(2,1)S(1)} collective-permute-done((bf16[288,1024]{1,0:T(8,128)(2,1)S(1)}, bf16[288,1024]{1,0:T(8,128)(2,1)S(1)}, u32[]{:S(2)}, u32[]{:S(2)}) %collective-permute-start.47) | collective-permute-done | bytes 589856 | tf_op jit(solution)/shard_map/ppermute | solution.py:809
  493.6 14.6 %mix_back.1 = (f32[1024,1152]{1,0:T(8,128)}, bf16[1024,1152]{1,0:T(8,128)(2,1)}, bf16[8,1024,72]{2,1,0:T(8,128)(2,1)}, f32[1,1152]{1,0:T(1,128)}, f32[1,1152]{1,...) custom-call(s32[1]{0:T(128)} %bitcast.me_ref, f32[1024,1152]{1,0:T(8,128)} %get-tuple-element.288.refs_0_, ...), custom_call_target="tpu_custom_call" | custom-call | flops 16099999744 | bytes 50400000 | tf_op jit(solution)/shard_map/mix_back/pallas_call | solution.py:218
  508.2 12.0 %collective-permute-done.50.refs_42_.refs_44_ = bf16[576,1152]{1,0:T(8,128)(2,1)S(1)} collective-permute-done((bf16[576,1152]{1,0:T(8,128)(2,1)}, bf16[576,1152]{1,0:T(8,128)(2,1)S(1)}, u32[]{:S(2)}, u32[]{:S(2)}) %collective-permute-start.50) | collective-permute-done | bytes 1327136 | tf_op jit(solution)/shard_map/ppermute | solution.py:809
  540.2 31.1 %attention_back.1 = (bf16[8,1024,72]{2,1,0:T(8,128)(2,1)}, bf16[8,1024,72]{2,1,0:T(8,128)(2,1)}, bf16[8,1024,72]{2,1,0:T(8,128)(2,1)}, f32[8,128]{1,0:T(8,128)}) custom-call(bf16[8,1024,72]{2,1,0:T(8,128)(2,1)} %get-tuple-element.269.query, bf16[8,1024,72]{2,1,0:T(8,128)(2,1)} %get-tuple-element.270.key, bf16[8,1024,72]{2,1,0:T(8,128)(2,1)} %get-tuple-element.271.value, ...), custom_call_target="tpu_custom_call" | custom-call | flops 35649998848 | bytes 111600000 | tf_op jit(solution)/shard_map/attention_back/pallas_call | solution.py:331
  575.4 10.7 %all-reduce.13.cloned.1.call-done.refs_8_.refs_53_ = bf16[256,2048]{1,0:T(8,128)(2,1)} async-done(((bf16[256,2048]{1,0:T(8,128)(2,1)}), bf16[256,2048]{1,0:T(8,128)(2,1)}) %all-reduce.13.cloned.1.call-update) | async-done | bytes 1048592 | tf_op jit(solution)/shard_map/psum | solution.py:1355
  593.0 12.8 %qkv_back.1 = (bf16[1024,1728]{1,0:T(8,128)(2,1)}, f32[1024,1152]{1,0:T(8,128)}, bf16[1024,1152]{1,0:T(8,128)(2,1)}, f32[1,1728]{1,0:T(1,128)}, f32[8,128]{1,0:T(8,128)}) custom-call(s32[1]{0:T(128)} %bitcast.me_ref, bf16[8,1024,72]{2,1,0:T(8,128)(2,1)} %get-tuple-element.353.refs_0_, bf16[8,1024,72]{2,1,0:T(8,128)(2,1)} %get-tuple-element.354.refs_1_, ...), custom_call_target="tpu_custom_call" | custom-call | flops 13799999488 | bytes 43200000 | tf_op jit(solution)/shard_map/qkv_back/pallas_call | solution.py:218
  630.2 18.6 %all-reduce.15.cloned.1.call-done.refs_6_.refs_54_ = bf16[576,1152]{1,0:T(8,128)(2,1)} async-done(((bf16[576,1152]{1,0:T(8,128)(2,1)}), bf16[576,1152]{1,0:T(8,128)(2,1)}) %all-reduce.15.cloned.1.call-update) | async-done | bytes 1327120 | tf_op jit(solution)/shard_map/psum | solution.py:1382
  667.7 10.4 %collective-permute-done.75 = f32[2,6912]{1,0:T(2,128)S(1)} collective-permute-done((f32[2,6912]{1,0:T(2,128)S(1)}, f32[2,6912]{1,0:T(2,128)S(1)}, u32[]{:S(2)}, u32[]{:S(2)}) %collective-permute-start.75) | collective-permute-done | bytes 55328 | tf_op jit(solution)/shard_map/ppermute | solution.py:809
  678.1 10.5 %collective-permute-done.58.refs_55_ = bf16[128,1152]{1,0:T(8,128)(2,1)S(1)} collective-permute-done((bf16[128,1152]{1,0:T(8,128)(2,1)S(1)}, bf16[128,1152]{1,0:T(8,128)(2,1)S(1)}, u32[]{:S(2)}, u32[]{:S(2)}) %collective-permute-start.58) | collective-permute-done | bytes 294944 | tf_op jit(solution)/shard_map/ppermute | solution.py:940
  702.9 14.2 %collective-permute-start.68 = (f32[1,9280]{1,0:T(1,128)S(1)}, f32[1,9280]{1,0:T(1,128)S(1)}, u32[]{:S(2)}, u32[]{:S(2)}) collective-permute-start(f32[1,9280]{1,0:T(1,128)S(1)} %add.357), channel_id=1, source_target_pairs={{0,1},{1,0},{2,3},{3,2},{4,5},{5,4},{6,7},{7,6},{8,9},{9,8},{10,11... | collective-permute-start | bytes 111368 | tf_op jit(solution)/shard_map/ppermute | solution.py:812
  744.6 15.3 %collective-permute-done.77 = f32[8,6912]{1,0:T(8,128)S(1)} collective-permute-done((f32[8,6912]{1,0:T(8,128)S(1)}, f32[8,6912]{1,0:T(8,128)S(1)}, u32[]{:S(2)}, u32[]{:S(2)}) %collective-permute-start.77) | collective-permute-done | bytes 221216 | tf_op jit(solution)/shard_map/ppermute | solution.py:812
  764.2 13.0 %all-gather = f32[8,144,16]{1,2,0:T(8,128)S(1)} all-gather(f32[1,144,16]{1,2,0:T(8,128)S(1)} %fusion.22), channel_id=1, replica_groups=mesh['dp'=8,'seq'=4] {'dp'}, dimensions={0}, use_global_device_ids=true | all-gather | bytes 82944 | tf_op jit(solution)/shard_map/all_gather | solution.py:1425
  790.7 17.2 %all-reduce.19.cloned.1.call-done = (bf16[144,1152]{1,0:T(8,128)(2,1)}, bf16[288,1728]{1,0:T(8,128)(2,1)}) async-done(((bf16[144,1152]{1,0:T(8,128)(2,1)}, bf16[288,1728]{1,0:T(8,128)(2,1)}), (bf16[144,1152]{1,0:T(8,128)(2,1)}, bf16[288,1728]{1,0:T(8,128)(2,1)})) %all-reduce.19.cloned.1.call-update) | async-done | bytes 1327120 | tf_op jit(solution)/shard_map/psum | solution.py:1401
  (542 shorter events, 409.4 us)
Async XLA Ops:
  7.2 442.4 %all-reduce.9.cloned.1.call-start = ((), (), s32[]{:S(2)}) async-start(), calls=%async_computation | async-start | bytes 786432 | tf_op jit(solution)/shard_map/psum | solution.py:1307
  84.7 63.8 %collective-permute-start.18 = (bf16[1296,1152]{1,0:T(8,128)(2,1)}, bf16[1296,1152]{1,0:T(8,128)(2,1)S(1)}, u32[]{:S(2)}, u32[]{:S(2)}) collective-permute-start(bf16[1296,1152]{1,0:T(8,128)(2,1)} %pack_near.1.refs_1_.refs_8_.refs_12_.refs_9_), channel_id=1, source_target_pairs={{0,16},{4,20},{8,24},{12,28},{16,0},{20,4},{24,8},{28,12},{1,17},{... | collective-permute-start | bytes 8957960 | tf_op jit(solution)/shard_map/ppermute | solution.py:809
  85.9 63.4 %collective-permute-start.17 = (bf16[1296,1152]{1,0:T(8,128)(2,1)}, bf16[1296,1152]{1,0:T(8,128)(2,1)S(1)}, u32[]{:S(2)}, u32[]{:S(2)}) collective-permute-start(bf16[1296,1152]{1,0:T(8,128)(2,1)} %pack_near.1.refs_1_.refs_8_.refs_12_.refs_9_), channel_id=1, source_target_pairs={{0,8},{4,12},{8,0},{12,4},{16,24},{20,28},{24,16},{28,20},{1,9},{5... | collective-permute-start | bytes 8957960 | tf_op jit(solution)/shard_map/ppermute | solution.py:809
  194.0 49.3 %collective-permute-start.24 = (bf16[1024,1152]{1,0:T(8,128)(2,1)}, bf16[1024,1152]{1,0:T(8,128)(2,1)}, u32[]{:S(2)}, u32[]{:S(2)}) collective-permute-start(bf16[1024,1152]{1,0:T(8,128)(2,1)} %get-tuple-element.284), channel_id=1, source_target_pairs={{0,4},{4,0},{8,12},{12,8},{16,20},{20,16},{24,28},{28,24},{1,5},{5... | collective-permute-start | bytes 7077896 | tf_op jit(solution)/shard_map/ppermute | solution.py:806
  197.1 46.1 %collective-permute-start.28 = (bf16[3968,256]{1,0:T(8,128)(2,1)}, bf16[3968,256]{1,0:T(8,128)(2,1)S(1)}, u32[]{:S(2)}, u32[]{:S(2)}) collective-permute-start(bf16[3968,256]{1,0:T(8,128)(2,1)} %pack_far.1.refs_6_.refs_10_.refs_3_.refs_5_.refs_7_), channel_id=1, source_target_pairs={{0,16},{4,20},{8,24},{12,28},{16,0},{20,4},{24,8},{28,12},{1,17},{... | collective-permute-start | bytes 6094856 | tf_op jit(solution)/shard_map/ppermute | solution.py:809
  197.4 45.8 %collective-permute-start.27 = (bf16[3968,256]{1,0:T(8,128)(2,1)}, bf16[3968,256]{1,0:T(8,128)(2,1)}, u32[]{:S(2)}, u32[]{:S(2)}) collective-permute-start(bf16[3968,256]{1,0:T(8,128)(2,1)} %pack_far.1.refs_6_.refs_10_.refs_3_.refs_5_.refs_7_), channel_id=1, source_target_pairs={{0,8},{4,12},{8,0},{12,4},{16,24},{20,28},{24,16},{28,20},{1,9},{5... | collective-permute-start | bytes 6094856 | tf_op jit(solution)/shard_map/ppermute | solution.py:809
  400.0 64.9 %collective-permute-start.45 = (bf16[256,2048]{1,0:T(8,128)(2,1)}, bf16[256,2048]{1,0:T(8,128)(2,1)S(1)}, u32[]{:S(2)}, u32[]{:S(2)}) collective-permute-start(bf16[256,2048]{1,0:T(8,128)(2,1)} %get-tuple-element.333), channel_id=1, source_target_pairs={{0,8},{4,12},{8,0},{12,4},{16,24},{20,28},{24,16},{28,20},{1,9},{5... | collective-permute-start | bytes 3145736 | tf_op jit(solution)/shard_map/ppermute | solution.py:809
  400.4 61.4 %collective-permute-start.46 = (bf16[256,2048]{1,0:T(8,128)(2,1)}, bf16[256,2048]{1,0:T(8,128)(2,1)}, u32[]{:S(2)}, u32[]{:S(2)}) collective-permute-start(bf16[256,2048]{1,0:T(8,128)(2,1)} %get-tuple-element.336), channel_id=1, source_target_pairs={{0,16},{4,20},{8,24},{12,28},{16,0},{20,4},{24,8},{28,12},{1,17},{... | collective-permute-start | bytes 3145736 | tf_op jit(solution)/shard_map/ppermute | solution.py:809
  409.4 40.2 %collective-permute-start.43 = (bf16[576,1024]{1,0:T(8,128)(2,1)}, bf16[576,1024]{1,0:T(8,128)(2,1)S(1)}, u32[]{:S(2)}, u32[]{:S(2)}) collective-permute-start(bf16[576,1024]{1,0:T(8,128)(2,1)} %get-tuple-element.327), channel_id=1, source_target_pairs={{0,16},{4,20},{8,24},{12,28},{16,0},{20,4},{24,8},{28,12},{1,17},{... | collective-permute-start | bytes 3538952 | tf_op jit(solution)/shard_map/ppermute | solution.py:809
  410.5 120.9 %all-reduce.11.cloned.1.call-start = ((), (), s32[]{:S(2)}) async-start(), calls=%async_computation.1 | async-start | bytes 1179648 | tf_op jit(solution)/shard_map/psum | solution.py:1319
  464.9 43.3 %collective-permute-start.53 = (bf16[128,2048]{1,0:T(8,128)(2,1)S(1)}, bf16[128,2048]{1,0:T(8,128)(2,1)}, u32[]{:S(2)}, u32[]{:S(2)}) collective-permute-start(bf16[128,2048]{1,0:T(8,128)(2,1)S(1)} %add_convert_fusion.11), channel_id=1, source_target_pairs={{0,8},{4,12},{8,0},{12,4},{16,24},{20,28},{24,16},{28,20},{1,9},{5... | collective-permute-start | bytes 1572872 | tf_op jit(solution)/shard_map/ppermute | solution.py:809
  467.0 41.3 %collective-permute-start.52 = (bf16[128,2048]{1,0:T(8,128)(2,1)}, bf16[128,2048]{1,0:T(8,128)(2,1)}, u32[]{:S(2)}, u32[]{:S(2)}) collective-permute-start(bf16[128,2048]{1,0:T(8,128)(2,1)} %add_convert_fusion.13), channel_id=1, source_target_pairs={{0,16},{4,20},{8,24},{12,28},{16,0},{20,4},{24,8},{28,12},{1,17},{... | collective-permute-start | bytes 1572872 | tf_op jit(solution)/shard_map/ppermute | solution.py:809
  468.9 53.4 %collective-permute-start.48 = (bf16[576,1152]{1,0:T(8,128)(2,1)}, bf16[576,1152]{1,0:T(8,128)(2,1)S(1)}, u32[]{:S(2)}, u32[]{:S(2)}) collective-permute-start(bf16[576,1152]{1,0:T(8,128)(2,1)} %get-tuple-element.347), channel_id=1, source_target_pairs={{0,8},{4,12},{8,0},{12,4},{16,24},{20,28},{24,16},{28,20},{1,9},{5... | collective-permute-start | bytes 3981320 | tf_op jit(solution)/shard_map/ppermute | solution.py:809
  493.3 92.8 %all-reduce.13.cloned.1.call-start = ((), (), s32[]{:S(2)}) async-start(), calls=%async_computation.2 | async-start | bytes 2097152 | tf_op jit(solution)/shard_map/psum | solution.py:1355
  531.4 117.3 %all-reduce.15.cloned.1.call-start = ((), (), s32[]{:S(2)}) async-start(), calls=%async_computation.3 | async-start | bytes 2654208 | tf_op jit(solution)/shard_map/psum | solution.py:1382
  536.7 69.1 %collective-permute-start.57 = (bf16[288,1152]{1,0:T(8,128)(2,1)}, bf16[288,1152]{1,0:T(8,128)(2,1)}, u32[]{:S(2)}, u32[]{:S(2)}) collective-permute-start(bf16[288,1152]{1,0:T(8,128)(2,1)} %get-tuple-element.375), channel_id=1, source_target_pairs={{0,8},{4,12},{8,0},{12,4},{16,24},{20,28},{24,16},{28,20},{1,9},{5... | collective-permute-start | bytes 1990664 | tf_op jit(solution)/shard_map/ppermute | solution.py:809
  537.9 48.5 %collective-permute-start.54 = (bf16[288,2304]{1,0:T(8,128)(2,1)}, bf16[288,2304]{1,0:T(8,128)(2,1)}, u32[]{:S(2)}, u32[]{:S(2)}) collective-permute-start(bf16[288,2304]{1,0:T(8,128)(2,1)} %get-tuple-element.361), channel_id=1, source_target_pairs={{0,8},{4,12},{8,0},{12,4},{16,24},{20,28},{24,16},{28,20},{1,9},{5... | collective-permute-start | bytes 3981320 | tf_op jit(solution)/shard_map/ppermute | solution.py:809
  538.2 51.5 %collective-permute-start.55 = (bf16[288,2304]{1,0:T(8,128)(2,1)}, bf16[288,2304]{1,0:T(8,128)(2,1)}, u32[]{:S(2)}, u32[]{:S(2)}) collective-permute-start(bf16[288,2304]{1,0:T(8,128)(2,1)} %get-tuple-element.365), channel_id=1, source_target_pairs={{0,16},{4,20},{8,24},{12,28},{16,0},{20,4},{24,8},{28,12},{1,17},{... | collective-permute-start | bytes 3981320 | tf_op jit(solution)/shard_map/ppermute | solution.py:809
  586.1 150.5 %all-reduce.17.cloned.1.call-start = ((), (), s32[]{:S(2)}) async-start(), calls=%async_computation.4 | async-start | bytes 2654208 | tf_op jit(solution)/shard_map/psum | solution.py:1383
  588.5 39.0 %collective-permute-start.70 = (bf16[144,2304]{1,0:T(8,128)(2,1)}, bf16[144,2304]{1,0:T(8,128)(2,1)}, u32[]{:S(2)}, u32[]{:S(2)}) collective-permute-start(bf16[144,2304]{1,0:T(8,128)(2,1)} %add_convert_fusion.3), channel_id=1, source_target_pairs={{0,16},{4,20},{8,24},{12,28},{16,0},{20,4},{24,8},{28,12},{1,17},{... | collective-permute-start | bytes 1990664 | tf_op jit(solution)/shard_map/ppermute | solution.py:809
  609.6 39.3 %collective-permute-start.56 = (bf16[512,1152]{1,0:T(8,128)(2,1)}, bf16[512,1152]{1,0:T(8,128)(2,1)}, u32[]{:S(2)}, u32[]{:S(2)}) collective-permute-start(bf16[512,1152]{1,0:T(8,128)(2,1)} %slice.345), channel_id=1, source_target_pairs={{0,4},{4,0},{8,12},{12,8},{16,20},{20,16},{24,28},{28,24},{1,5},{5... | collective-permute-start | bytes 3538952 | tf_op jit(solution)/shard_map/ppermute | solution.py:806
  620.5 38.1 %collective-permute-start.62 = (bf16[288,1728]{1,0:T(8,128)(2,1)}, bf16[288,1728]{1,0:T(8,128)(2,1)S(1)}, u32[]{:S(2)}, u32[]{:S(2)}) collective-permute-start(bf16[288,1728]{1,0:T(8,128)(2,1)} %get-tuple-element.391), channel_id=1, source_target_pairs={{0,8},{4,12},{8,0},{12,4},{16,24},{20,28},{24,16},{28,20},{1,9},{5... | collective-permute-start | bytes 2985992 | tf_op jit(solution)/shard_map/ppermute | solution.py:809
  648.8 159.1 %all-reduce.19.cloned.1.call-start = ((), (), s32[]{:S(2)}) async-start(), calls=%async_computation.5 | async-start | bytes 2727936 | tf_op jit(solution)/shard_map/psum | solution.py:1401
  743.5 67.3 %collective-permute-start.80 = (bf16[144,2304]{1,0:T(8,128)(2,1)S(1)}, bf16[144,2304]{1,0:T(8,128)(2,1)S(1)}, u32[]{:S(2)}, u32[]{:S(2)}) collective-permute-start(bf16[144,2304]{1,0:T(8,128)(2,1)S(1)} %get-tuple-element.511), channel_id=1, source_target_pairs={{0,4},{4,0},{8,12},{12,8},{16,20},{20,16},{24,28},{28,24},{1,5},{5... | collective-permute-start | bytes 1990664 | tf_op jit(solution)/shard_map/ppermute | solution.py:806
  (153 other events, 2090.9 us)
Sparse Core Ops, SparseCore 0:
  410.7 34.8 all-reduce.8
  493.4 37.9 all-reduce.10
  533.9 52.1 all-reduce.12
  588.9 59.8 all-reduce.14
  651.6 79.1 all-reduce.16
  744.7 63.0 all-reduce.18
